TPU v7x, 32 devices: a whole 2x2x4 slice. The times are simulated.
32 devices in a mesh: dp: 8 (over y, x, core), tensor: 4 (over z).
Axes of the slice: x: 2, y: 2, z: 4, core: 2. Of those that a mesh axis runs over, the one named last changes fastest.
Arguments:
- tokens: bfloat16 [16384, 1024], P(('dp', 'tensor')), may hold values from -6 to 6
- lengths: int32 [8, 16], P('dp'), may hold values from 1 to 512, 2048 in all within a row
- doc_pairs: int32 [8, 8], P('dp'), may hold values from 0 to 7, each once within a row
- qkv_weight: bfloat16 [1024, 3, 1024], P(None, None, 'tensor'), may hold values from -0.1875 to 0.1875
- qkv_bias: bfloat16 [3, 1024], P(None, 'tensor'), may hold values from -1.1953125 to 1.1953125
- attn_weight: bfloat16 [1024, 1024], P('tensor'), may hold values from -1.5 to 1.5
- attn_bias: bfloat16 [1024], replicated, may hold values from -1.1953125 to 1.1953125
- ffn_in_weight: bfloat16 [1024, 4096], P(None, 'tensor'), may hold values from -0.1875 to 0.1875
- ffn_in_bias: bfloat16 [4096], P('tensor'), may hold values from -1.1953125 to 1.1953125
- ffn_out_weight: bfloat16 [4096, 1024], P('tensor'), may hold values from -0.09375 to 0.09375
- ffn_out_bias: bfloat16 [1024], replicated, may hold values from -1.1953125 to 1.1953125
- norm_gains: bfloat16 [2, 1024], replicated, may hold values from 0.5 to 1.5
- norm_shifts: bfloat16 [2, 1024], replicated, may hold values from -1.1953125 to 1.1953125
- proj_weight: bfloat16 [1024, 128], replicated, may hold values from -0.1875 to 0.1875
- log_temp: float32 [1], replicated, may hold values from -3.5 to -2.3
Outputs:
- contrast_loss: float32 [1], replicated
- activations: bfloat16 [16384, 1024], P(('dp', 'tensor'))
- tokens_grad: float32 [16384, 1024], P(('dp', 'tensor'))
- qkv_weight_grad: float32 [1024, 3, 1024], P('dp', None, 'tensor')
- qkv_bias_grad: float32 [3, 1024], P(None, 'tensor')
- attn_weight_grad: float32 [1024, 1024], P('tensor', 'dp')
- attn_bias_grad: float32 [1024], replicated
- ffn_in_weight_grad: float32 [1024, 4096], P('dp', 'tensor')
- ffn_in_bias_grad: float32 [4096], P('tensor')
- ffn_out_weight_grad: float32 [4096, 1024], P('tensor', 'dp')
- ffn_out_bias_grad: float32 [1024], replicated
- norm_gains_grad: float32 [2, 1024], replicated
- norm_shifts_grad: float32 [2, 1024], replicated
- proj_weight_grad: float32 [1024, 128], replicated
- log_temp_grad: float32 [1], replicated
Inputs may be any that keep to these rules, and one draw needn't show every extreme that they name: The 16 lengths of a row sum to 2048; the longest of each row is exactly 512. Each row holds every number of 0 to 7 once; query segment q of a row is paired with segment 8 + doc_pairs[q] of the same row.
All inputs are finite; a program needn't handle non-finite values.
Results may differ from a plain program's by a relative error of at most 0.022.
Values may be sent and summed in bfloat16 or wider, within the bound.
A program may use at most 320 MiB of HBM per device.

v0:
```python
from functools import partial
import math

import jax
import jax.numpy as jnp
from jax import lax
from jax.sharding import PartitionSpec as P

HDIM = 64
EMB = 128
SEQ = 2048
SEGS = 16
BLOCK = 512
NQ = 8


highest = lax.Precision.HIGHEST
eps_norm = 1e-05
eps_unit = 1e-06
sharpness = 10.0
masked_score = -1000000000.0


def dense_product(left, right):
    return jnp.dot(left, right, preferred_element_type=jnp.float32)


def matmul(left, right):
    return jnp.dot(left, right, precision=highest, preferred_element_type=jnp.float32)


def layer_norm(values, gain, shift):
    mean_value = jnp.mean(values, axis=-1, keepdims=True)
    centered = values - mean_value
    variance = jnp.mean(centered * centered, axis=-1, keepdims=True)
    return centered * lax.rsqrt(variance + eps_norm) * gain + shift


def norm_back(values, gain, shift, grad):
    unused, pullback = jax.vjp(layer_norm, values, gain, shift)
    return pullback(grad)


def segment_layout(row_lengths):
    seg_ends = jnp.cumsum(row_lengths, dtype=jnp.int32)
    seg_starts = seg_ends - row_lengths
    positions = jnp.arange(SEQ, dtype=jnp.int32)
    seg_ids = jnp.sum(
        (positions[:, None] >= seg_ends[None, :]).astype(jnp.int32), axis=1, dtype=jnp.int32
    )
    member = seg_ids[:, None] == jnp.arange(SEGS, dtype=jnp.int32)[None, :]
    offsets = positions - jnp.sum(
        jnp.where(member, seg_starts[None, :], 0), axis=1, dtype=jnp.int32
    )
    return (seg_ids, member, offsets)


def rotary_tables(offsets):
    half_dim = HDIM // 2
    inv_freq = jnp.exp(jnp.arange(half_dim, dtype=jnp.float32) * (-2.0 * math.log(10000.0) / HDIM))
    angles = offsets.astype(jnp.float32)[:, None] * inv_freq[None, :]
    return (jnp.cos(angles), jnp.sin(angles))


def rotate(values, cosine, sine_table):
    half_dim = values.shape[-1] // 2
    front_half = values[..., :half_dim]
    back_half = values[..., half_dim:]
    cos_wide = cosine[:, None, :]
    sin_wide = sine_table[:, None, :]
    return jnp.concatenate(
        [
            front_half * cos_wide - back_half * sin_wide,
            back_half * cos_wide + front_half * sin_wide,
        ],
        axis=-1,
    )


def unit_rows(prefix_emb):
    return prefix_emb * lax.rsqrt(
        jnp.sum(prefix_emb * prefix_emb, axis=1, keepdims=True) + eps_unit
    )


def contrast_tail(similar, temp_log, doc_mask, query_mask, counts, positive):
    smooth_max = jnp.log(matmul(jnp.exp(sharpness * (similar - 1.0)), doc_mask)) / sharpness + 1.0
    seg_scores = matmul(query_mask.T, smooth_max) / counts[:NQ, None]
    logits = seg_scores * jnp.exp(-temp_log[0])
    return jnp.sum(jnp.log(jnp.sum(jnp.exp(logits), axis=1)) - jnp.sum(logits * positive, axis=1))


def contrast_row(row_emb, member, row_pairs, temp_log, loss_scale):
    onehot = member.astype(jnp.float32)
    counts = jnp.sum(onehot, axis=0)
    query_mask = onehot[:, :NQ]
    doc_mask = onehot[:, NQ:]
    positive = (row_pairs[:, None] == jnp.arange(NQ, dtype=jnp.int32)[None, :]).astype(jnp.float32)
    tail = partial(
        contrast_tail, doc_mask=doc_mask, query_mask=query_mask, counts=counts, positive=positive
    )
    running = jnp.zeros((), jnp.float32)
    temp_grad = jnp.zeros_like(temp_log)
    row_grad = jnp.zeros(row_emb.shape, jnp.float32)
    for prefix in (EMB, EMB * 3 // 4, EMB // 2):
        unit_vecs, unit_pull = jax.vjp(unit_rows, row_emb[:, :prefix])
        unit_low = unit_vecs.astype(jnp.bfloat16)
        similar = jnp.einsum("ie,je->ij", unit_low, unit_low, preferred_element_type=jnp.float32)
        value, tail_pull = jax.vjp(tail, similar, temp_log)
        sim_grad, temp_part = tail_pull(jnp.asarray(loss_scale, jnp.float32))
        sim_low = sim_grad.astype(jnp.bfloat16)
        unit_grad = dense_product(sim_low, unit_low) + jnp.einsum(
            "ij,ie->je", sim_low, unit_low, preferred_element_type=jnp.float32
        )
        prefix_grad = unit_pull(unit_grad)[0]
        row_grad = row_grad + jnp.pad(prefix_grad, ((0, 0), (0, EMB - prefix)))
        running = running + value * loss_scale
        temp_grad = temp_grad + temp_part
    return (running, row_grad, temp_grad)


def score_product(left, right):
    return jnp.einsum("qhc,khc->hqk", left, right, preferred_element_type=jnp.float32)


def value_product(left, right):
    return jnp.einsum("hqk,khc->qhc", left, right, preferred_element_type=jnp.float32)


def key_product(left, right):
    return jnp.einsum("hqk,qhc->khc", left, right, preferred_element_type=jnp.float32)


def block_live(seg_ids, query_start, key_start):
    return (seg_ids[query_start] <= seg_ids[key_start + BLOCK - 1]) & (
        seg_ids[key_start] <= seg_ids[query_start + BLOCK - 1]
    )


def block_scores(query_block, key_heads, seg_ids, query_start, row_start, live_flags):
    block_parts = []
    for key_index, live in enumerate(live_flags):
        key_start = row_start + key_index * BLOCK
        block_parts.append(score_product(query_block, key_heads[key_start : key_start + BLOCK]))
    raw_scores = jnp.concatenate(block_parts, axis=2) * HDIM ** (-0.5)
    same_doc = (
        seg_ids[query_start : query_start + BLOCK, None]
        == seg_ids[None, row_start : row_start + SEQ]
    )
    return jnp.where(same_doc[None], raw_scores, masked_score)


def attend(query_heads, key_heads, value_heads, seg_ids, head_count):
    per_row = SEQ // BLOCK
    mixed_parts = []
    log_totals = []
    for query_index in range(per_row):
        query_start = query_index * BLOCK
        query_block = query_heads[query_start : query_start + BLOCK]
        live_flags = [
            block_live(seg_ids, query_start, key_index * BLOCK) for key_index in range(per_row)
        ]
        raw_scores = block_scores(query_block, key_heads, seg_ids, query_start, 0, live_flags)
        row_max = jnp.max(raw_scores, axis=2, keepdims=True)
        shifted_exp = jnp.exp(raw_scores - row_max)
        row_total = jnp.sum(shifted_exp, axis=2, keepdims=True)
        probs_low = (shifted_exp / row_total).astype(jnp.bfloat16)
        log_totals.append(row_max + jnp.log(row_total))
        block_out = jnp.zeros((BLOCK, head_count, HDIM), jnp.float32)
        for key_index, live in enumerate(live_flags):
            key_start = key_index * BLOCK
            block_out = block_out + value_product(
                probs_low[:, :, key_index * BLOCK : (key_index + 1) * BLOCK],
                value_heads[key_start : key_start + BLOCK],
            )
        mixed_parts.append(block_out)
    return (jnp.concatenate(mixed_parts, axis=0), log_totals)


def attend_back(
    query_heads, key_heads, value_heads, mixed_grad, log_totals, seg_ids, row_count, head_count
):
    per_row = SEQ // BLOCK
    score_scale = HDIM ** (-0.5)
    empty = jnp.zeros((BLOCK, head_count, HDIM), jnp.float32)
    query_grads = []
    key_grads = [empty] * (row_count * per_row)
    value_grads = [empty] * (row_count * per_row)
    block_number = 0
    for query_index in range(per_row):
        query_start = query_index * BLOCK
        query_block = query_heads[query_start : query_start + BLOCK]
        grad_block = mixed_grad[query_start : query_start + BLOCK]
        live_flags = [
            block_live(seg_ids, query_start, key_index * BLOCK) for key_index in range(per_row)
        ]
        raw_scores = block_scores(query_block, key_heads, seg_ids, query_start, 0, live_flags)
        attn_probs = jnp.exp(raw_scores - log_totals[block_number])
        grad_parts = []
        for key_index, live in enumerate(live_flags):
            key_start = key_index * BLOCK
            grad_parts.append(score_product(grad_block, value_heads[key_start : key_start + BLOCK]))
        prob_grads = jnp.concatenate(grad_parts, axis=2)
        delta_sum = jnp.sum(attn_probs * prob_grads, axis=2, keepdims=True)
        score_low = (attn_probs * (prob_grads - delta_sum)).astype(jnp.bfloat16)
        probs_low = attn_probs.astype(jnp.bfloat16)
        block_grad = empty
        for key_index, live in enumerate(live_flags):
            key_start = key_index * BLOCK
            score_piece = score_low[:, :, key_index * BLOCK : (key_index + 1) * BLOCK]
            prob_piece = probs_low[:, :, key_index * BLOCK : (key_index + 1) * BLOCK]
            block_grad = block_grad + value_product(
                score_piece, key_heads[key_start : key_start + BLOCK]
            )
            key_grads[key_index] = key_grads[key_index] + key_product(score_piece, query_block)
            value_grads[key_index] = value_grads[key_index] + key_product(prob_piece, grad_block)
        query_grads.append(block_grad * score_scale)
        block_number = block_number + 1
    return (
        jnp.concatenate(query_grads, axis=0),
        jnp.concatenate(key_grads, axis=0) * score_scale,
        jnp.concatenate(value_grads, axis=0),
    )


def per_device(
    tokens,
    lengths,
    doc_pairs,
    qkv_weight,
    qkv_bias,
    attn_weight,
    attn_bias,
    ffn_in_weight,
    ffn_in_bias,
    ffn_out_weight,
    ffn_out_bias,
    norm_gains,
    norm_shifts,
    proj_weight,
    log_temp,
):
    row_count = lengths.shape[0]
    local_rows = tokens.shape[0]
    head_count = qkv_weight.shape[2] // HDIM
    tensor_count = lax.axis_size("tensor")
    layouts = [segment_layout(lengths[0])]
    seg_ids = layouts[0][0] + 0
    offsets = jnp.concatenate([layout[2] for layout in layouts])
    cosine, sine_table = rotary_tables(offsets)
    gains = norm_gains.astype(jnp.float32)
    shifts = norm_shifts.astype(jnp.float32)
    gathered = lax.all_gather(tokens, "tensor", axis=0, tiled=True)
    group_tokens = gathered.shape[0]
    projected = (
        jnp.einsum("td,dkc->tkc", gathered, qkv_weight, preferred_element_type=jnp.float32)
        + qkv_bias.astype(jnp.float32)[None]
    )
    split_heads = projected.reshape(group_tokens, 3, head_count, HDIM)
    query_heads = rotate(split_heads[:, 0], cosine, sine_table).astype(jnp.bfloat16)
    key_heads = rotate(split_heads[:, 1], cosine, sine_table).astype(jnp.bfloat16)
    value_heads = split_heads[:, 2].astype(jnp.bfloat16)
    mixed_values, log_totals = attend(query_heads, key_heads, value_heads, seg_ids, head_count)
    mixed_heads = mixed_values.reshape(group_tokens, head_count * HDIM).astype(jnp.bfloat16)
    attn_out = lax.psum_scatter(
        dense_product(mixed_heads, attn_weight).astype(jnp.bfloat16),
        "tensor",
        scatter_dimension=0,
        tiled=True,
    ).astype(jnp.float32) + attn_bias.astype(jnp.float32)
    resid_one = tokens.astype(jnp.float32) + attn_out
    normed = layer_norm(resid_one, gains[0], shifts[0])
    normed_all = lax.all_gather(normed.astype(jnp.bfloat16), "tensor", axis=0, tiled=True)
    ffn_pre = dense_product(normed_all, ffn_in_weight) + ffn_in_bias.astype(jnp.float32)
    hidden = jax.nn.gelu(ffn_pre, approximate=False).astype(jnp.bfloat16)
    ffn_out = lax.psum_scatter(
        dense_product(hidden, ffn_out_weight).astype(jnp.bfloat16),
        "tensor",
        scatter_dimension=0,
        tiled=True,
    ).astype(jnp.float32) + ffn_out_bias.astype(jnp.float32)
    resid_two = normed + ffn_out
    output = layer_norm(resid_two, gains[1], shifts[1])
    output_low = output.astype(jnp.bfloat16)
    embedded = dense_product(output_low, proj_weight).astype(jnp.bfloat16)
    embedded_all = lax.all_gather(embedded, "tensor", axis=0, tiled=True)
    loss_scale = 1.0 / (NQ * row_count * lax.axis_size("dp"))
    emb_float = embedded_all.astype(jnp.float32)
    row_loss, row_grad, row_temp = contrast_row(
        emb_float, layouts[0][1], doc_pairs[0], log_temp, loss_scale
    )
    own_start = lax.axis_index("tensor") * local_rows
    emb_grad = lax.dynamic_slice_in_dim(row_grad, own_start, local_rows, 0).astype(jnp.bfloat16)
    proj_grad = jnp.einsum("td,te->de", output_low, emb_grad, preferred_element_type=jnp.float32)
    output_grad = jnp.einsum("te,de->td", emb_grad, proj_weight, preferred_element_type=jnp.float32)
    resid_two_grad, gain_two_grad, shift_two_grad = norm_back(
        resid_two, gains[1], shifts[1], output_grad
    )
    ffn_grad = resid_two_grad.astype(jnp.bfloat16)
    out_bias_grad = jnp.sum(ffn_grad.astype(jnp.float32), axis=0)
    ffn_grad_all = lax.all_gather(ffn_grad, "tensor", axis=0, tiled=True)
    out_weight_grad = jnp.einsum(
        "tf,td->fd", hidden, ffn_grad_all, preferred_element_type=jnp.float32
    )
    hidden_grad = jnp.einsum(
        "td,fd->tf", ffn_grad_all, ffn_out_weight, preferred_element_type=jnp.float32
    )
    unused, gelu_pull = jax.vjp(partial(jax.nn.gelu, approximate=False), ffn_pre)
    pre_grad = gelu_pull(hidden_grad)[0].astype(jnp.bfloat16)
    in_bias_grad = jnp.sum(pre_grad.astype(jnp.float32), axis=0)
    in_weight_grad = jnp.einsum(
        "td,tf->df", normed_all, pre_grad, preferred_element_type=jnp.float32
    )
    normed_grad = (
        lax.psum_scatter(
            jnp.einsum(
                "tf,df->td", pre_grad, ffn_in_weight, preferred_element_type=jnp.float32
            ).astype(jnp.bfloat16),
            "tensor",
            scatter_dimension=0,
            tiled=True,
        ).astype(jnp.float32)
        + resid_two_grad
    )
    resid_one_grad, gain_one_grad, shift_one_grad = norm_back(
        resid_one, gains[0], shifts[0], normed_grad
    )
    attn_grad = resid_one_grad.astype(jnp.bfloat16)
    attn_bias_grad = jnp.sum(attn_grad.astype(jnp.float32), axis=0)
    attn_grad_all = lax.all_gather(attn_grad, "tensor", axis=0, tiled=True)
    attn_weight_grad = jnp.einsum(
        "tc,td->cd", mixed_heads, attn_grad_all, preferred_element_type=jnp.float32
    )
    mixed_grad = jnp.einsum(
        "td,cd->tc", attn_grad_all, attn_weight, preferred_element_type=jnp.float32
    ).astype(jnp.bfloat16)
    mixed_grad = mixed_grad.reshape(group_tokens, head_count, HDIM)
    query_grad, key_grad, value_grad = attend_back(
        query_heads, key_heads, value_heads, mixed_grad, log_totals, seg_ids, row_count, head_count
    )
    qkv_grad = jnp.stack(
        [
            rotate(query_grad, cosine, -sine_table),
            rotate(key_grad, cosine, -sine_table),
            value_grad,
        ],
        axis=1,
    )
    qkv_grad = qkv_grad.reshape(group_tokens, 3, head_count * HDIM).astype(jnp.bfloat16)
    qkv_bias_grad = jnp.sum(qkv_grad.astype(jnp.float32), axis=0)
    qkv_weight_grad = jnp.einsum(
        "td,tkc->dkc", gathered, qkv_grad, preferred_element_type=jnp.float32
    )
    tokens_grad = (
        lax.psum_scatter(
            jnp.einsum(
                "tkc,dkc->td", qkv_grad, qkv_weight, preferred_element_type=jnp.float32
            ).astype(jnp.bfloat16),
            "tensor",
            scatter_dimension=0,
            tiled=True,
        ).astype(jnp.float32)
        + resid_one_grad
    )
    qkv_weight_red, attn_weight_red, in_weight_red, out_weight_red = (
        lax.psum_scatter(qkv_weight_grad, "dp", scatter_dimension=0, tiled=True),
        lax.psum_scatter(attn_weight_grad, "dp", scatter_dimension=1, tiled=True),
        lax.psum_scatter(in_weight_grad, "dp", scatter_dimension=0, tiled=True),
        lax.psum_scatter(out_weight_grad, "dp", scatter_dimension=1, tiled=True),
    )
    qkv_bias_red, in_bias_red = lax.psum((qkv_bias_grad, in_bias_grad), "dp")
    tensor_share = 1.0 / tensor_count
    summed = lax.psum(
        (
            attn_bias_grad,
            out_bias_grad,
            jnp.stack([gain_one_grad, gain_two_grad]),
            jnp.stack([shift_one_grad, shift_two_grad]),
            proj_grad,
            (row_loss * tensor_share).reshape(1),
            row_temp * tensor_share,
        ),
        ("dp", "tensor"),
    )
    return (
        summed[5],
        output_low,
        tokens_grad,
        qkv_weight_red,
        qkv_bias_red,
        attn_weight_red,
        summed[0],
        in_weight_red,
        in_bias_red,
        out_weight_red,
        summed[1],
        summed[2],
        summed[3],
        summed[4],
        summed[6],
    )


def solution(mesh):
    in_specs = (
        P(("dp", "tensor"), None),
        P("dp", None),
        P("dp", None),
        P(None, None, "tensor"),
        P(None, "tensor"),
        P("tensor", None),
        P(),
        P(None, "tensor"),
        P("tensor"),
        P("tensor", None),
        P(),
        P(),
        P(),
        P(),
        P(),
    )
    out_specs = (
        P(),
        P(("dp", "tensor"), None),
        P(("dp", "tensor"), None),
        P("dp", None, "tensor"),
        P(None, "tensor"),
        P("tensor", "dp"),
        P(),
        P("dp", "tensor"),
        P("tensor"),
        P("tensor", "dp"),
        P(),
        P(),
        P(),
        P(),
        P(),
    )
    return jax.shard_map(
        per_device, mesh=mesh, in_specs=in_specs, out_specs=out_specs, check_vma=False
    )
```

profile of v0, /device:TPU:24, one launch (start us, length us, event | category | flops | bytes accessed | tf_op | source)
XLA Modules:
  0.0 1691.7 jit_solution(1009194318456675686)
XLA Ops:
  16.0 72.7 %all-gather.5.cloned.1.call-done = bf16[2048,1024]{1,0:T(8,128)(2,1)} async-done(((bf16[512,1024]{1,0:T(8,128)(2,1)}), bf16[2048,1024]{1,0:T(8,128)(2,1)}) %all-gather.5.cloned.1.call-update) | async-done | bytes 4194320 | tf_op jit(solution)/shard_map/all_gather | solution.py:253
  88.6 6.1 fusion.51
  132.5 5.3 fusion.527
  137.8 6.3 fusion.14
  144.2 14.5 fusion.25
  168.0 5.3 fusion.525
  173.3 6.1 fusion.15
  179.4 14.5 fusion.28
  208.9 9.0 fusion.22
  226.2 6.6 fusion.531
  236.5 9.0 fusion.19
  265.8 77.3 %reduce-scatter.9.cloned.1.call-done = bf16[512,1024]{1,0:T(8,128)(2,1)} async-done(((bf16[2048,1024]{1,0:T(8,128)(2,1)}), bf16[512,1024]{1,0:T(8,128)(2,1)}) %reduce-scatter.9.cloned.1.call-update) | async-done | bytes 1048592 | tf_op jit(solution)/shard_map/reduce_scatter | solution.py:265
  349.5 79.4 %all-gather.7.cloned.1.call-done = bf16[2048,1024]{1,0:T(8,128)(2,1)} async-done(((bf16[512,1024]{1,0:T(8,128)(2,1)}), bf16[2048,1024]{1,0:T(8,128)(2,1)}) %all-gather.7.cloned.1.call-update) | async-done | bytes 4194320 | tf_op jit(solution)/shard_map/all_gather | solution.py:273
  428.9 25.5 %multiply_convert_fusion.7 = (bf16[2048,1024]{1,0:T(8,128)(2,1)S(1)}, f32[2048,1024]{1,0:T(8,128)}, f32[2048,1024]{1,0:T(8,128)}) fusion(f32[1024]{0:T(1024)S(1)} %convert_element_type.183, bf16[2048,1024]{1,0:T(8,128)(2,1)} %all-gather.7.cloned.1.call-done, bf16[1024,1024]{1,0:T(8,128)(2,1)S(1)} %copy-done), kind=kOutput, calls=%fused_computation.72 | convolution fusion | flops 4433379328 | bytes 27267072 | tf_op jit(solution)/shard_map/dot_general | solution.py:25
  456.5 6.1 convolution_convert_fusion.2
  464.1 76.0 %reduce-scatter.11.cloned.1.call-done = bf16[512,1024]{1,0:T(8,128)(2,1)} async-done(((bf16[2048,1024]{1,0:T(8,128)(2,1)}), bf16[512,1024]{1,0:T(8,128)(2,1)}) %reduce-scatter.11.cloned.1.call-update) | async-done | bytes 1048592 | tf_op jit(solution)/shard_map/reduce_scatter | solution.py:276
  544.3 16.2 all_gather.17
  567.8 8.2 fusion.557
  575.9 14.1 fusion.18
  593.8 26.2 %multiply_convert_fusion.4 = bf16[2048,2048]{1,0:T(8,128)(2,1)} fusion(f32[2048,2048]{1,0:T(8,128)} %fusion.557, f32[2048,8]{0,1:T(8,128)} %fusion.54, pred[2048,16]{0,1:T(8,128)(4,1)S(1)} %iota_compare_fusion), kind=kOutput, calls=%fused_computation.31 | convolution fusion | flops 423624704 | bytes 25247744 | tf_op jit(solution)/shard_map/transpose(jvp())/dot_general | solution.py:29
  620.0 6.0 fusion.559
  630.2 8.2 fusion.556
  638.4 13.8 fusion.17
  656.0 15.4 multiply_convert_fusion.5
  671.4 6.0 fusion.558
  681.6 10.7 fusion.16
  696.1 13.1 multiply_convert_fusion.6
  709.2 6.0 fusion.521
  725.6 79.0 %all-gather.9.cloned.1.call-done = bf16[2048,1024]{1,0:T(8,128)(2,1)} async-done(((bf16[512,1024]{1,0:T(8,128)(2,1)}), bf16[2048,1024]{1,0:T(8,128)(2,1)}) %all-gather.9.cloned.1.call-update) | async-done | bytes 4194320 | tf_op jit(solution)/shard_map/all_gather | solution.py:301
  804.6 14.1 convert_reduce_fusion
  820.8 6.3 convolution_convert_fusion.1
  827.2 77.4 %reduce-scatter.13.cloned.1.call-done = bf16[512,1024]{1,0:T(8,128)(2,1)} async-done(((bf16[2048,1024]{1,0:T(8,128)(2,1)}), bf16[512,1024]{1,0:T(8,128)(2,1)}) %reduce-scatter.13.cloned.1.call-update) | async-done | bytes 1048592 | tf_op jit(solution)/shard_map/reduce_scatter | solution.py:315
  915.1 79.1 %all-gather.11.cloned.1.call-done = bf16[2048,1024]{1,0:T(8,128)(2,1)} async-done(((bf16[512,1024]{1,0:T(8,128)(2,1)}), bf16[2048,1024]{1,0:T(8,128)(2,1)}) %all-gather.11.cloned.1.call-update) | async-done | bytes 4194320 | tf_op jit(solution)/shard_map/all_gather | solution.py:330
  1038.6 25.7 %multiply_convert_fusion = bf16[4,512,2048]{1,2,0:T(8,128)(2,1)} fusion(f32[4,512,512]{1,2,0:T(8,128)} %fusion.450, f32[4,512,512]{1,2,0:T(8,128)} %fusion.446, f32[4,512,512]{1,2,0:T(8,128)} %fusion.442, f32[4,512,512]{1,2,0:T(8,128)} %fusion.438, f32[4,512]{1,0:T(4,128)S(1)} %copy-done.135, f32[4,512,512]{1,2,0:T(8,128)S(1)} %copy-done.16, ...), kind=kOutput, calls=%fused_computation.16 | output fusion | flops 92278784 | bytes 42999808 | tf_op jit(solution)/shard_map/sub | solution.py:205
  1094.6 25.2 %multiply_convert_fusion.3 = bf16[4,512,2048]{1,2,0:T(8,128)(2,1)} fusion(f32[4,512,512]{1,2,0:T(8,128)} %fusion.453, f32[4,512,512]{1,2,0:T(8,128)} %fusion.449, f32[4,512,512]{1,2,0:T(8,128)} %fusion.445, f32[4,512,512]{1,2,0:T(8,128)} %fusion.441, f32[4,512]{1,0:T(4,128)S(1)} %copy-done.133, f32[4,512,512]{1,2,0:T(8,128)S(1)} %copy-done.11, ...), kind=kOutput, calls=%fused_computation.28 | output fusion | flops 92278784 | bytes 42999808 | tf_op jit(solution)/shard_map/sub | solution.py:205
  1143.4 25.5 %multiply_convert_fusion.1 = bf16[4,512,2048]{1,2,0:T(8,128)(2,1)} fusion(f32[4,512,512]{1,2,0:T(8,128)} %fusion.451, f32[4,512,512]{1,2,0:T(8,128)} %fusion.447, f32[4,512,512]{1,2,0:T(8,128)} %fusion.443, f32[4,512,512]{1,2,0:T(8,128)} %fusion.439, f32[4,512]{1,0:T(4,128)S(1)} %copy-done.131, f32[4,512,512]{1,2,0:T(8,128)S(1)} %copy-done.8, ...), kind=kOutput, calls=%fused_computation.20 | output fusion | flops 92278784 | bytes 42999808 | tf_op jit(solution)/shard_map/sub | solution.py:205
  1199.1 25.3 %multiply_convert_fusion.2 = bf16[4,512,2048]{1,2,0:T(8,128)(2,1)} fusion(f32[4,512,512]{1,2,0:T(8,128)} %fusion.452, f32[4,512,512]{1,2,0:T(8,128)} %fusion.448, f32[4,512,512]{1,2,0:T(8,128)} %fusion.444, f32[4,512,512]{1,2,0:T(8,128)} %fusion.440, f32[4,512]{1,0:T(4,128)S(1)} %copy-done.129, f32[4,512,512]{1,2,0:T(8,128)S(1)} %copy-done.3, ...), kind=kOutput, calls=%fused_computation.24 | output fusion | flops 92278784 | bytes 42999808 | tf_op jit(solution)/shard_map/sub | solution.py:205
  1262.8 7.7 fusion.121
  1270.6 7.4 bitcast_convert_fusion
  1279.7 10.6 fusion.561
  1290.4 10.1 fusion.562
  1311.3 46.1 %all-reduce.2 = (f32[1]{0:T(128)}, f32[1024]{0:T(1024)}, f32[1024]{0:T(1024)}, f32[2,1024]{1,0:T(2,128)}, f32[2,1024]{1,0:T(2,128)}, /*index=5*/f32[1]{0:T(128)}) all-reduce(f32[1]{0:T(128)} %bitcast.21, f32[1024]{0:T(1024)S(1)} %copy-done.145, f32[1024]{0:T(1024)S(1)} %copy-done.144, ...), channel_id=1, replica_groups=mesh['dp'=8,'tensor'=4] {'dp','tensor'}, use_global_device_ids=true, to_apply=%region_30.31 | all-reduce | flops 6146 | bytes 49168 | tf_op jit(solution)/shard_map/psum | solution.py:373
  1359.8 13.9 all-reduce.3
  1375.6 22.0 %reduce-scatter.15.cloned.1.call-done = bf16[512,1024]{1,0:T(8,128)(2,1)} async-done(((bf16[2048,1024]{1,0:T(8,128)(2,1)}), bf16[512,1024]{1,0:T(8,128)(2,1)}) %reduce-scatter.15.cloned.1.call-update) | async-done | bytes 1048592 | tf_op jit(solution)/shard_map/reduce_scatter | solution.py:355
  1401.1 131.1 %all-reduce.6.cloned.1.call-done = f32[1024,128]{1,0:T(8,128)} async-done(((f32[1024,128]{1,0:T(8,128)}), f32[1024,128]{1,0:T(8,128)}) %all-reduce.6.cloned.1.call-update) | async-done | bytes 524304 | tf_op jit(solution)/shard_map/psum | solution.py:373
  1532.2 55.4 %reduce-scatter.21.cloned.1.call-done = f32[128,1024]{1,0:T(8,128)} async-done(((f32[1024,1024]{1,0:T(8,128)}), f32[128,1024]{1,0:T(8,128)}) %reduce-scatter.21.cloned.1.call-update) | async-done | bytes 524304 | tf_op jit(solution)/shard_map/reduce_scatter | solution.py:368
  1587.5 55.5 %reduce-scatter.23.cloned.1.call-done = f32[1024,128]{1,0:T(8,128)} async-done(((f32[1024,1024]{1,0:T(8,128)}), f32[1024,128]{1,0:T(8,128)}) %reduce-scatter.23.cloned.1.call-update) | async-done | bytes 524304 | tf_op jit(solution)/shard_map/reduce_scatter | solution.py:369
  1643.1 39.8 %reduce-scatter.19.cloned.1.call-done = f32[256,128]{1,0:T(8,128)} async-done(((f32[256,1024]{1,0:T(8,128)}), f32[256,128]{1,0:T(8,128)}) %reduce-scatter.19.cloned.1.call-update) | async-done | bytes 131088 | tf_op jit(solution)/shard_map/reduce_scatter | solution.py:367
  (609 shorter events, 349.6 us)
Async XLA Ops:
  7.2 421.7 %copy-start = (bf16[1024,1024]{1,0:T(8,128)(2,1)S(1)}, bf16[1024,1024]{1,0:T(8,128)(2,1)}, u32[]{:S(2)}) copy-start(bf16[1024,1024]{1,0:T(8,128)(2,1)} %param.22) | copy-start | bytes 6291460
  7.2 81.4 %all-gather.5.cloned.1.call-start = ((), (), s32[]{:S(2)}) async-start(), calls=%async_computation.8 | async-start | bytes 5242880 | tf_op jit(solution)/shard_map/all_gather | solution.py:253
  7.9 335.2 %reduce-scatter.9.cloned.1.call-start = ((), (), s32[]{:S(2)}) async-start(), calls=%async_computation.9 | async-start | bytes 5242880 | tf_op jit(solution)/shard_map/reduce_scatter | solution.py:265
  12.3 84.9 %copy-start.66 = (f32[2048,32]{0,1:T(8,128)}, f32[2048,32]{0,1:T(8,128)S(1)}, u32[]{:S(2)}) copy-start(f32[2048,32]{0,1:T(8,128)S(1)} %get-tuple-element.134) | copy-start | bytes 786436
  16.0 192.9 %copy-start.49 = (pred[512,2048]{0,1:T(8,128)(4,1)}, pred[512,2048]{0,1:T(8,128)(4,1)S(1)}, u32[]{:S(2)}) copy-start(pred[512,2048]{0,1:T(8,128)(4,1)S(1)} %get-tuple-element.136) | copy-start | bytes 3145732
  97.9 27.0 %copy-start.38 = (bf16[512,4,64]{0,2,1:T(8,128)(2,1)}, bf16[512,4,64]{0,2,1:T(8,128)(2,1)S(1)}, u32[]{:S(2)}) copy-start(bf16[512,4,64]{0,2,1:T(8,128)(2,1)S(1)} %get-tuple-element.126) | copy-start | bytes 786436
  97.9 27.7 %copy-start.36 = (bf16[512,4,64]{0,2,1:T(8,128)(2,1)}, bf16[512,4,64]{0,2,1:T(8,128)(2,1)S(1)}, u32[]{:S(2)}) copy-start(bf16[512,4,64]{0,2,1:T(8,128)(2,1)S(1)} %get-tuple-element.127) | copy-start | bytes 786436
  97.9 28.5 %copy-start.34 = (bf16[512,4,64]{0,2,1:T(8,128)(2,1)}, bf16[512,4,64]{0,2,1:T(8,128)(2,1)S(1)}, u32[]{:S(2)}) copy-start(bf16[512,4,64]{0,2,1:T(8,128)(2,1)S(1)} %get-tuple-element.125) | copy-start | bytes 786436
  97.9 31.8 %copy-start.30 = (bf16[512,4,64]{0,2,1:T(8,128)(2,1)}, bf16[512,4,64]{0,2,1:T(8,128)(2,1)S(1)}, u32[]{:S(2)}) copy-start(bf16[512,4,64]{0,2,1:T(8,128)(2,1)S(1)} %get-tuple-element.124) | copy-start | bytes 786436
  98.1 24.1 %copy-start.44 = (bf16[512,4,64]{0,2,1:T(8,128)(2,1)}, bf16[512,4,64]{0,2,1:T(8,128)(2,1)S(1)}, u32[]{:S(2)}) copy-start(bf16[512,4,64]{0,2,1:T(8,128)(2,1)S(1)} %get-tuple-element.122) | copy-start | bytes 786436
  98.1 31.6 %copy-start.42 = (bf16[512,4,64]{0,2,1:T(8,128)(2,1)}, bf16[512,4,64]{0,2,1:T(8,128)(2,1)S(1)}, u32[]{:S(2)}) copy-start(bf16[512,4,64]{0,2,1:T(8,128)(2,1)S(1)} %get-tuple-element.123) | copy-start | bytes 786436
  104.3 104.6 %copy-start.2 = (f32[4,512,512]{1,2,0:T(8,128)}, f32[4,512,512]{1,2,0:T(8,128)S(1)}, u32[]{:S(2)}) copy-start(f32[4,512,512]{1,2,0:T(8,128)S(1)} %fusion.547) | copy-start | bytes 12582916
  105.1 103.8 %copy-start.4 = (f32[4,512,512]{1,2,0:T(8,128)}, f32[4,512,512]{1,2,0:T(8,128)S(1)}, u32[]{:S(2)}) copy-start(f32[4,512,512]{1,2,0:T(8,128)S(1)} %fusion.546) | copy-start | bytes 12582916
  109.1 99.8 %copy-start.5 = (f32[4,512,512]{1,2,0:T(8,128)}, f32[4,512,512]{1,2,0:T(8,128)S(1)}, u32[]{:S(2)}) copy-start(f32[4,512,512]{1,2,0:T(8,128)S(1)} %fusion.545) | copy-start | bytes 12582916
  113.3 95.6 %copy-start.6 = (f32[4,512,512]{1,2,0:T(8,128)}, f32[4,512,512]{1,2,0:T(8,128)S(1)}, u32[]{:S(2)}) copy-start(f32[4,512,512]{1,2,0:T(8,128)S(1)} %fusion.544) | copy-start | bytes 12582916
  261.2 81.9 %copy-start.18 = (bf16[512,1024]{1,0:T(8,128)(2,1)S(1)}, bf16[512,1024]{1,0:T(8,128)(2,1)}, u32[]{:S(2)}) copy-start(bf16[512,1024]{1,0:T(8,128)(2,1)} %param.15) | copy-start | bytes 3145732
  265.7 83.8 %copy-start.163 = (bf16[1024]{0:T(1024)(128)(2,1)S(1)}, bf16[1024]{0:T(1024)(128)(2,1)}, u32[]{:S(2)}) copy-start(bf16[1024]{0:T(1024)(128)(2,1)} %param.23) | copy-start | bytes 6148
  265.7 163.2 %all-gather.7.cloned.1.call-start = ((), (), s32[]{:S(2)}) async-start(), calls=%async_computation.10 | async-start | bytes 5242880 | tf_op jit(solution)/shard_map/all_gather | solution.py:273
  265.8 277.5 %copy-start.120 = (f32[1,1024]{1,0:T(1,128)}, f32[1,1024]{1,0:T(1,128)S(1)}, u32[]{:S(2)}) copy-start(f32[1,1024]{1,0:T(1,128)S(1)} %get-tuple-element.143) | copy-start | bytes 12292
  346.6 107.8 %copy-start.140 = (f32[512]{0:T(512)}, f32[512]{0:T(512)S(1)}, u32[]{:S(2)}) copy-start(f32[512]{0:T(512)S(1)} %multiply_reduce_fusion.9) | copy-start | bytes 6148
  346.6 193.5 %copy-start.124 = (f32[512]{0:T(512)}, f32[512]{0:T(512)S(1)}, u32[]{:S(2)}) copy-start(f32[512]{0:T(512)S(1)} %fusion.484) | copy-start | bytes 6148
  349.4 190.7 %reduce-scatter.11.cloned.1.call-start = ((), (), s32[]{:S(2)}) async-start(), calls=%async_computation.11 | async-start | bytes 5242880 | tf_op jit(solution)/shard_map/reduce_scatter | solution.py:276
  349.5 104.9 %copy-start.153 = (f32[1024]{0:T(1024)}, f32[1024]{0:T(1024)S(1)}, u32[]{:S(2)}) copy-start(f32[1024]{0:T(1024)S(1)} %convert_element_type.183) | copy-start | bytes 12292
  428.9 27.6 %copy-start.176 = (bf16[1024,1024]{1,0:T(8,128)(2,1)S(1)}, bf16[1024,1024]{1,0:T(8,128)(2,1)}, u32[]{:S(2)}) copy-start(bf16[1024,1024]{1,0:T(8,128)(2,1)} %param.24) | copy-start | bytes 6291460
  462.6 81.3 %copy-start.102 = (bf16[1024,128]{1,0:T(8,128)(2,1)S(1)}, bf16[1024,128]{1,0:T(8,128)(2,1)}, u32[]{:S(2)}) copy-start(bf16[1024,128]{1,0:T(8,128)(2,1)} %param.28) | copy-start | bytes 786436
  462.6 342.0 %all-gather.9.cloned.1.call-start = ((), (), s32[]{:S(2)}) async-start(), calls=%async_computation.12 | async-start | bytes 5242880 | tf_op jit(solution)/shard_map/all_gather | solution.py:301
  720.0 84.6 %copy-start.154 = (f32[1024]{0:T(1024)S(1)}, f32[1024]{0:T(1024)}, u32[]{:S(2)}) copy-start(f32[1024]{0:T(1024)} %copy-done.153) | copy-start | bytes 12292
  725.6 179.0 %reduce-scatter.13.cloned.1.call-start = ((), (), s32[]{:S(2)}) async-start(), calls=%async_computation.13 | async-start | bytes 5242880 | tf_op jit(solution)/shard_map/reduce_scatter | solution.py:315
  820.7 83.8 %copy-start.19 = (bf16[512,1024]{1,0:T(8,128)(2,1)S(1)}, bf16[512,1024]{1,0:T(8,128)(2,1)}, u32[]{:S(2)}) copy-start(bf16[512,1024]{1,0:T(8,128)(2,1)} %param.15) | copy-start | bytes 3145732
  820.8 83.8 %copy-start.125 = (f32[512]{0:T(512)S(1)}, f32[512]{0:T(512)}, u32[]{:S(2)}) copy-start(f32[512]{0:T(512)} %copy-done.124) | copy-start | bytes 6148
  827.1 81.5 %copy-start.141 = (f32[512]{0:T(512)S(1)}, f32[512]{0:T(512)}, u32[]{:S(2)}) copy-start(f32[512]{0:T(512)} %copy-done.140) | copy-start | bytes 6148
  827.1 81.5 %copy-start.23 = (bf16[512,1024]{1,0:T(8,128)(2,1)S(1)}, bf16[512,1024]{1,0:T(8,128)(2,1)}, u32[]{:S(2)}) copy-start(bf16[512,1024]{1,0:T(8,128)(2,1)} %reduce-scatter.9.cloned.1.call-done) | copy-start | bytes 3145732
  827.1 167.1 %copy-start.107 = (bf16[256,1024]{1,0:T(8,128)(2,1)S(1)}, bf16[256,1024]{1,0:T(8,128)(2,1)}, u32[]{:S(2)}) copy-start(bf16[256,1024]{1,0:T(8,128)(2,1)} %param.20) | copy-start | bytes 1572868
  827.1 167.1 %all-gather.11.cloned.1.call-start = ((), (), s32[]{:S(2)}) async-start(), calls=%async_computation.14 | async-start | bytes 5242880 | tf_op jit(solution)/shard_map/all_gather | solution.py:330
  911.7 82.6 %copy-start.138 = (f32[512]{0:T(512)}, f32[512]{0:T(512)S(1)}, u32[]{:S(2)}) copy-start(f32[512]{0:T(512)S(1)} %negate_multiply_fusion.1) | copy-start | bytes 6148
  914.8 458.8 %reduce-scatter.17.cloned.1.call-start = ((), (), s32[]{:S(2)}) async-start(), calls=%async_computation.16 | async-start | bytes 3538944 | tf_op jit(solution)/shard_map/reduce_scatter | solution.py:366
  998.0 92.8 %copy-start.32 = (bf16[512,256]{0,1:T(8,128)(2,1)}, bf16[512,256]{0,1:T(8,128)(2,1)S(1)}, u32[]{:S(2)}) copy-start(bf16[512,256]{0,1:T(8,128)(2,1)S(1)} %get-tuple-element.116) | copy-start | bytes 786436
  1038.6 25.7 %copy-start.45 = (bf16[512,4,64]{0,2,1:T(8,128)(2,1)S(1)}, bf16[512,4,64]{0,2,1:T(8,128)(2,1)}, u32[]{:S(2)}) copy-start(bf16[512,4,64]{0,2,1:T(8,128)(2,1)} %copy-done.44) | copy-start | bytes 786436
  1143.4 25.5 %copy-start.43 = (bf16[512,4,64]{0,2,1:T(8,128)(2,1)S(1)}, bf16[512,4,64]{0,2,1:T(8,128)(2,1)}, u32[]{:S(2)}) copy-start(bf16[512,4,64]{0,2,1:T(8,128)(2,1)} %copy-done.42) | copy-start | bytes 786436
  1199.1 34.3 %copy-start.41 = (bf16[512,4,64]{0,2,1:T(8,128)(2,1)S(1)}, bf16[512,4,64]{0,2,1:T(8,128)(2,1)}, u32[]{:S(2)}) copy-start(bf16[512,4,64]{0,2,1:T(8,128)(2,1)} %copy-done.40) | copy-start | bytes 786436
  1270.6 127.0 %reduce-scatter.15.cloned.1.call-start = ((), (), s32[]{:S(2)}) async-start(), calls=%async_computation.15 | async-start | bytes 5242880 | tf_op jit(solution)/shard_map/reduce_scatter | solution.py:355
  1278.1 254.1 %all-reduce.6.cloned.1.call-start = ((), (), s32[]{:S(2)}) async-start(), calls=%async_computation.20 | async-start | bytes 1048576 | tf_op jit(solution)/shard_map/psum | solution.py:373
  1279.4 308.1 %reduce-scatter.21.cloned.1.call-start = ((), (), s32[]{:S(2)}) async-start(), calls=%async_computation.18 | async-start | bytes 4718592 | tf_op jit(solution)/shard_map/reduce_scatter | solution.py:368
  1290.4 352.7 %reduce-scatter.23.cloned.1.call-start = ((), (), s32[]{:S(2)}) async-start(), calls=%async_computation.19 | async-start | bytes 4718592 | tf_op jit(solution)/shard_map/reduce_scatter | solution.py:369
  1300.7 59.1 %copy-start.155 = (f32[1024]{0:T(1024)S(1)}, f32[1024]{0:T(1024)}, u32[]{:S(2)}) copy-start(f32[1024]{0:T(1024)} %get-tuple-element.84) | copy-start | bytes 12292
  1300.7 96.9 %copy-start.139 = (f32[512]{0:T(512)S(1)}, f32[512]{0:T(512)}, u32[]{:S(2)}) copy-start(f32[512]{0:T(512)} %copy-done.138) | copy-start | bytes 6148
  1300.7 384.1 %copy-start.1 = (bf16[1024,1024]{1,0:T(8,128)(2,1)S(1)}, bf16[1024,1024]{1,0:T(8,128)(2,1)}, u32[]{:S(2)}) copy-start(bf16[1024,1024]{1,0:T(8,128)(2,1)} %param.22) | copy-start | bytes 6291460
  1300.7 382.2 %reduce-scatter.19.cloned.1.call-start = ((), (), s32[]{:S(2)}) async-start(), calls=%async_computation.17 | async-start | bytes 1179648 | tf_op jit(solution)/shard_map/reduce_scatter | solution.py:367
  (154 other events, 1127.3 us)
Sparse Core Ops, SparseCore 0:
  9.6 78.9 all-gather.4
  265.8 77.2 reduce-scatter.8
  349.5 79.2 all-gather.6
  462.7 77.3 reduce-scatter.10
  725.7 78.8 all-gather.8
  827.2 77.2 reduce-scatter.12
  914.9 79.2 all-gather.10
  1270.7 47.4 reduce-scatter.16
  1320.5 77.0 reduce-scatter.14
  1404.1 128.0 all-reduce.5
  1536.1 51.3 reduce-scatter.20
  1591.7 51.3 reduce-scatter.22
  1646.8 36.0 reduce-scatter.18
where the time goes:
time: 1700 us; the launch traced here: 1690 us
  waiting for transfers between devices  846 us (50%)
  matrix products  490 us (29%)
  other arithmetic  236 us (14%)
  blocking collectives  76.2 us (4%)
  local copies, waits for them, and re-layouts  21.9 us (1%)
  between operations  21.6 us (1%)
    psum x1, waiting for transfers between devices, per_device(): lax.psum((attn_bias_grad, out_bias_grad, jnp.stack([gain_one_grad, gain_t...  131 us
    sub x4, other arithmetic, attend_back(): score_low = (attn_probs * (prob_grads - delta_sum)).astype(jnp.bfloat16)  102 us
    dot_general x12, matrix products, matmul(): jnp.dot(left, right, precision=highest, preferred_element_type=jnp.float32)  101 us
    dot_general x32, matrix products, score_product(): jnp.einsum('qhc,khc->hqk', left, right, preferred_element_type=jnp.float32)  94.4 us
    all_gather x1, waiting for transfers between devices, per_device(): lax.all_gather(normed.astype(jnp.bfloat16), 'tensor', axis=0, tiled=True)  79.4 us
    all_gather x1, waiting for transfers between devices, per_device(): attn_grad_all = lax.all_gather(attn_grad, 'tensor', axis=0, tiled=True)  79.1 us
    all_gather x1, waiting for transfers between devices, per_device(): ffn_grad_all = lax.all_gather(ffn_grad, 'tensor', axis=0, tiled=True)  79 us
    dot_general x32, matrix products, value_product(): jnp.einsum('hqk,khc->qhc', left, right, preferred_element_type=jnp.float32)  77.9 us
  transfers between devices with their start and end apart: 13, of which 12 were waited for; matrix products, arithmetic and copies ran while one was open for 3% of the time, Pallas kernels for 0%

commit v1 on v0

v1 whole, which is shorter than its diff:
```python
from functools import partial
import math

import jax
import jax.numpy as jnp
from jax import lax
from jax.experimental import pallas as pl
from jax.experimental.pallas import tpu as pltpu
from jax.sharding import PartitionSpec as P

HDIM = 64
EMB = 128
SEQ = 2048
SEGS = 16
NQ = 8
MESH = pl.DeviceIdType.MESH
ANY = pl.ANY
F32 = jnp.float32
BF = jnp.bfloat16
eps_norm = 1e-05
eps_unit = 1e-06
VMEM_BIG = 60 * 1024 * 1024


def dot(left, right, left_dim=1, right_dim=0, precision=None):
    return lax.dot_general(
        left,
        right,
        (((left_dim,), (right_dim,)), ((), ())),
        preferred_element_type=F32,
        precision=precision,
    )


def hbm_specs(count):
    return [pl.BlockSpec(memory_space=ANY)] * count


def vmem_specs(count):
    return [pl.BlockSpec(memory_space=pltpu.VMEM)] * count


def rotate_lanes(values, cosine, sine):
    out = []
    front = lax.rem(lax.broadcasted_iota(jnp.int32, (1, 128), 1), 64) < 32
    for start in range(0, values.shape[1], 128):
        part = values[:, start : start + 128]
        partner = jnp.where(front, pltpu.roll(part, 96, 1), pltpu.roll(part, 32, 1))
        out.append(part * cosine + partner * sine)
    return out[0] if len(out) == 1 else jnp.concatenate(out, axis=1)


PROJ_COLS = 256


def project_kernel(window_ref, weight_ref, bias_ref, cos_ref, sin_ref, query_ref, key_ref, value_ref):
    step = pl.program_id(0)
    per_kind = pl.num_programs(0) // 3
    local = query_ref.shape[0]
    bias = bias_ref[0].astype(F32)

    @pl.when(step < per_kind)
    def _():
        rows = pl.ds(local, local)
        made = dot(window_ref[rows, :], weight_ref[0]) + bias
        query_ref[...] = rotate_lanes(made, cos_ref[rows, :], sin_ref[rows, :]).astype(BF)

    @pl.when((step >= per_kind) & (step < 2 * per_kind))
    def _():
        for part in range(3):
            rows = pl.ds(part * local, local)
            made = dot(window_ref[rows, :], weight_ref[0]) + bias
            key_ref[rows, :] = rotate_lanes(made, cos_ref[rows, :], sin_ref[rows, :]).astype(BF)

    @pl.when(step >= 2 * per_kind)
    def _():
        for part in range(3):
            rows = pl.ds(part * local, local)
            value_ref[rows, :] = (dot(window_ref[rows, :], weight_ref[0]) + bias).astype(BF)


def project(window, weight, bias, cosine, sine):
    width = weight.shape[2]
    per = width // PROJ_COLS
    long = window.shape[0]
    local = long // 3
    flops = 2 * width * width * (local + 2 * long)
    return pl.pallas_call(
        project_kernel,
        grid=(3 * per,),
        in_specs=[
            pl.BlockSpec((long, width), lambda n: (0, 0)),
            pl.BlockSpec((1, width, PROJ_COLS), lambda n: (n // per, 0, lax.rem(n, per))),
            pl.BlockSpec((1, 1, PROJ_COLS), lambda n: (n // per, 0, lax.rem(n, per))),
            pl.BlockSpec((long, 128), lambda n: (0, 0)),
            pl.BlockSpec((long, 128), lambda n: (0, 0)),
        ],
        out_specs=[
            pl.BlockSpec((local, PROJ_COLS), lambda n: (0, jnp.minimum(n, per - 1))),
            pl.BlockSpec((long, PROJ_COLS), lambda n: (0, jnp.clip(n - per, 0, per - 1))),
            pl.BlockSpec((long, PROJ_COLS), lambda n: (0, jnp.clip(n - 2 * per, 0, per - 1))),
        ],
        out_shape=[
            jax.ShapeDtypeStruct((local, width), BF),
            jax.ShapeDtypeStruct((long, width), BF),
            jax.ShapeDtypeStruct((long, width), BF),
        ],
        compiler_params=pltpu.CompilerParams(vmem_limit_bytes=40 * 2**20),
        cost_estimate=pl.CostEstimate(flops=flops, bytes_accessed=14 * 2**20, transcendentals=0),
    )(window, weight, bias, cosine, sine)


BQ = 128
BK = 256
SCALE = HDIM**-0.5


def split_pair(values):
    first = lax.broadcasted_iota(jnp.int32, (1, 128), 1) < 64
    zero = jnp.zeros_like(values)
    return jnp.where(first, values, zero), jnp.where(first, zero, values)


def attend_kernel(bounds_ref, query_ref, key_ref, value_ref, segq_ref, segk_ref, mixed_ref, lse_ref):
    first = lax.broadcasted_iota(jnp.int32, (1, 128), 1) < 64
    for block in range(query_ref.shape[0] // BQ):
        rows = pl.ds(block * BQ, BQ)
        queries = split_pair(query_ref[rows, :] * jnp.asarray(SCALE, BF))
        seg_q = segq_ref[rows, 0:1]

        def body(index, carry):
            keys_at = pl.ds(pl.multiple_of(index * BK, BK), BK)
            keys = key_ref[keys_at, :]
            values = value_ref[keys_at, :]
            live = seg_q == segk_ref[0:1, keys_at]
            made = []
            for head in range(2):
                top, total, acc = carry[head]
                scores = jnp.where(live, dot(queries[head], keys, 1, 1), -1e9)
                new_top = jnp.maximum(top, jnp.max(scores, axis=1, keepdims=True))
                probs = jnp.exp(scores - new_top)
                fade = jnp.exp(top - new_top)
                total = total * fade + jnp.sum(probs, axis=1, keepdims=True)
                acc = acc * fade + dot(probs.astype(BF), values)
                made.append((new_top, total, acc))
            return tuple(made)

        start = tuple(
            (jnp.full((BQ, 1), -2e9, F32), jnp.zeros((BQ, 1), F32), jnp.zeros((BQ, 128), F32)) for _ in range(2)
        )
        done = lax.fori_loop(bounds_ref[block, 0], bounds_ref[block, 1], body, start)
        parts = [acc / total for top, total, acc in done]
        logs = [top + jnp.log(total) for top, total, acc in done]
        mixed_ref[rows, :] = jnp.where(first, parts[0], parts[1]).astype(BF)
        lse_ref[0, rows, :] = jnp.where(first, logs[0], logs[1])


def attend(bounds, queries, keys, values, seg_q, seg_k):
    local, width = queries.shape
    long = keys.shape[0]
    groups = width // 128
    return pl.pallas_call(
        attend_kernel,
        grid_spec=pltpu.PrefetchScalarGridSpec(
            num_scalar_prefetch=1,
            grid=(groups,),
            in_specs=[
                pl.BlockSpec((local, 128), lambda g, b: (0, g)),
                pl.BlockSpec((long, 128), lambda g, b: (0, g)),
                pl.BlockSpec((long, 128), lambda g, b: (0, g)),
                pl.BlockSpec((local, 128), lambda g, b: (0, 0)),
                pl.BlockSpec((8, long), lambda g, b: (0, 0)),
            ],
            out_specs=[
                pl.BlockSpec((local, 128), lambda g, b: (0, g)),
                pl.BlockSpec((1, local, 128), lambda g, b: (g, 0, 0)),
            ],
        ),
        out_shape=[
            jax.ShapeDtypeStruct((local, width), BF),
            jax.ShapeDtypeStruct((groups, local, 128), F32),
        ],
        compiler_params=pltpu.CompilerParams(vmem_limit_bytes=40 * 2**20),
        cost_estimate=pl.CostEstimate(flops=2 * 2**30, bytes_accessed=8 * 2**20, transcendentals=4 * 2**20),
    )(bounds, queries, keys, values, seg_q, seg_k)


def attend_back_kernel(
    bounds_ref, query_ref, key_ref, value_ref, mixed_ref, grad_ref, lse_ref, segq_ref, segk_ref, cos_ref, sin_ref,
    dq_ref, dk_ref, dv_ref, dk_acc, dv_acc,
):
    first = lax.broadcasted_iota(jnp.int32, (1, 128), 1) < 64
    local = query_ref.shape[0]
    dk_acc[...] = jnp.zeros_like(dk_acc)
    dv_acc[...] = jnp.zeros_like(dv_acc)
    for block in range(local // BQ):
        rows = pl.ds(block * BQ, BQ)
        queries = split_pair(query_ref[rows, :] * jnp.asarray(SCALE, BF))
        grads = split_pair(grad_ref[rows, :])
        product = mixed_ref[rows, :].astype(F32) * grad_ref[rows, :].astype(F32)
        deltas = [jnp.sum(part, axis=1, keepdims=True) for part in split_pair(product)]
        logs = (lse_ref[0, rows, 0:1], lse_ref[0, rows, 64:65])
        seg_q = segq_ref[rows, 0:1]

        def body(index, carry):
            keys_at = pl.ds(pl.multiple_of(index * BK, BK), BK)
            keys = key_ref[keys_at, :]
            values = value_ref[keys_at, :]
            live = seg_q == segk_ref[0:1, keys_at]
            made, dk, dv = [], 0.0, 0.0
            for head in range(2):
                scores = jnp.where(live, dot(queries[head], keys, 1, 1), -1e9)
                probs = jnp.exp(scores - logs[head])
                score_low = (probs * (dot(grads[head], values, 1, 1) - deltas[head])).astype(BF)
                made.append(carry[head] + dot(score_low, keys))
                dk = dk + dot(score_low, queries[head], 0, 0)
                dv = dv + dot(probs.astype(BF), grads[head], 0, 0)
            dk_acc[keys_at, :] += dk
            dv_acc[keys_at, :] += dv
            return tuple(made)

        start = (jnp.zeros((BQ, 128), F32),) * 2
        done = lax.fori_loop(bounds_ref[block, 0], bounds_ref[block, 1], body, start)
        at = pl.ds(local + block * BQ, BQ)
        grad = jnp.where(first, done[0], done[1]) * SCALE
        dq_ref[rows, :] = rotate_lanes(grad, cos_ref[at, :], -sin_ref[at, :]).astype(BF)
    dk_ref[...] = rotate_lanes(dk_acc[...], cos_ref[...], -sin_ref[...]).astype(BF)
    dv_ref[...] = dv_acc[...].astype(BF)


def attend_back(bounds, queries, keys, values, mixed, grad, lse, seg_q, seg_k, cosine, sine):
    local, width = queries.shape
    long = keys.shape[0]
    groups = width // 128
    short_spec = pl.BlockSpec((local, 128), lambda g, b: (0, g))
    long_spec = pl.BlockSpec((long, 128), lambda g, b: (0, g))
    return pl.pallas_call(
        attend_back_kernel,
        grid_spec=pltpu.PrefetchScalarGridSpec(
            num_scalar_prefetch=1,
            grid=(groups,),
            in_specs=[
                short_spec,
                long_spec,
                long_spec,
                short_spec,
                short_spec,
                pl.BlockSpec((1, local, 128), lambda g, b: (g, 0, 0)),
                pl.BlockSpec((local, 128), lambda g, b: (0, 0)),
                pl.BlockSpec((8, long), lambda g, b: (0, 0)),
                pl.BlockSpec((long, 128), lambda g, b: (0, 0)),
                pl.BlockSpec((long, 128), lambda g, b: (0, 0)),
            ],
            out_specs=[short_spec, long_spec, long_spec],
            scratch_shapes=[pltpu.VMEM((long, 128), F32)] * 2,
        ),
        out_shape=[
            jax.ShapeDtypeStruct((local, width), BF),
            jax.ShapeDtypeStruct((long, width), BF),
            jax.ShapeDtypeStruct((long, width), BF),
        ],
        compiler_params=pltpu.CompilerParams(vmem_limit_bytes=40 * 2**20),
        cost_estimate=pl.CostEstimate(flops=5 * 2**30, bytes_accessed=16 * 2**20, transcendentals=4 * 2**20),
    )(bounds, queries, keys, values, mixed, grad, lse, seg_q, seg_k, cosine, sine)


CB = 256
HIGH = lax.Precision.HIGHEST


def halves(values):
    high = values.astype(BF)
    return high, (values - high.astype(F32)).astype(BF)


def contrast_kernel(
    info_ref, emb_ref, segc_ref, counts_ref, positive_ref, temp_ref, grad_ref, loss_ref, tgrad_ref,
    unit, docs, marks, ratio, ones_, out,
):
    own0, query_blocks, doc0 = info_ref[0], info_ref[1], info_ref[2]
    blocks = emb_ref.shape[0] // CB
    own_blocks = grad_ref.shape[0] // CB
    lane = lax.broadcasted_iota(jnp.int32, (1, 128), 1)
    loss_scale = temp_ref[0, 1]
    temp_inv = jnp.exp(-temp_ref[0:1, 0:1])
    segs = segc_ref[...]
    docs[...] = jnp.where((segs - NQ == lane) | ((segs == lane) & (lane >= NQ)), 1.0, 0.0).astype(BF)
    marks[...] = jnp.where((segs == lane) & (lane < NQ), 1.0, 0.0)
    out[...] = jnp.zeros_like(out)
    loss = jnp.zeros((1, 1), F32)
    tgrad = jnp.zeros((1, 1), F32)

    def at(index):
        return pl.ds(pl.multiple_of(index * CB, CB), CB)

    def similar(rows, columns):
        return jnp.exp(10.0 * (dot(unit[at(rows), :], unit[at(columns), :], 1, 1) - 1.0))

    for prefix in (EMB, EMB * 3 // 4, EMB // 2):
        emb = jnp.where(lane < prefix, emb_ref[...].astype(F32), 0.0)
        scale_full = lax.rsqrt(jnp.sum(emb * emb, axis=1, keepdims=True) + eps_unit)
        unit[...] = (emb * scale_full).astype(BF)

        def total_rows(index, seg_sum):
            def total_cols(column, total):
                high, low = halves(similar(index, column))
                mask = docs[at(column), :]
                return total + dot(high, mask) + dot(low, mask)

            total = lax.fori_loop(doc0, blocks, total_cols, jnp.zeros((CB, 128), F32))
            total = jnp.where(lane < NQ, total, 1.0)
            ratio[at(index), :] = 1.0 / total
            smooth = jnp.log(total) / 10.0 + 1.0
            return seg_sum + dot(marks[at(index), :], smooth, 0, 0, HIGH)

        seg_sum = lax.fori_loop(0, query_blocks, total_rows, jnp.zeros((128, 128), F32))
        valid = (lax.broadcasted_iota(jnp.int32, (NQ, 128), 1)) < NQ
        inv_counts = 1.0 / counts_ref[0:NQ, :]
        logits = jnp.where(valid, seg_sum[0:NQ, :] * inv_counts * temp_inv, 0.0)
        top = jnp.max(jnp.where(valid, logits, -1e30), axis=1, keepdims=True)
        powers = jnp.where(valid, jnp.exp(logits - top), 0.0)
        power_sum = jnp.sum(powers, axis=1, keepdims=True)
        positive = positive_ref[...]
        term = jnp.log(power_sum) + top - jnp.sum(logits * positive, axis=1, keepdims=True)
        loss = loss + jnp.sum(term, axis=0, keepdims=True) * loss_scale
        dlogits = (powers / power_sum - positive) * loss_scale
        tgrad = tgrad - jnp.sum(jnp.sum(dlogits * logits, axis=1, keepdims=True), axis=0, keepdims=True)
        ones_[...] = jnp.zeros_like(ones_)
        ones_[0:NQ, :] = dlogits * temp_inv * inv_counts

        def weigh(index, unused):
            weight = dot(marks[at(index), :], ones_[...], 1, 0, HIGH) * ratio[at(index), :]
            weight = jnp.where(lane < NQ, weight, 0.0)
            high = weight.astype(BF).astype(F32)
            ratio[at(index), :] = high + pltpu.roll(weight - high, NQ, 1)
            return unused

        lax.fori_loop(0, query_blocks, weigh, 0)

        def sim_grad(rows, columns):
            spread = dot(ratio[at(rows), :].astype(BF), docs[at(columns), :], 1, 1)
            return (similar(rows, columns) * spread).astype(BF)

        for own in range(own_blocks):
            mine = own0 + own

            def as_query(column, total):
                return total + dot(sim_grad(mine, column), unit[at(column), :])

            def as_doc(row, total):
                return total + dot(sim_grad(row, mine), unit[at(row), :], 0, 0)

            grad = jnp.zeros((CB, 128), F32)
            grad = lax.fori_loop(doc0, jnp.where(mine < query_blocks, blocks, doc0), as_query, grad)
            grad = lax.fori_loop(0, jnp.where(mine >= doc0, query_blocks, 0), as_doc, grad)
            part = jnp.where(lane < prefix, emb_ref[at(mine), :].astype(F32), 0.0)
            scale = lax.rsqrt(jnp.sum(part * part, axis=1, keepdims=True) + eps_unit)
            full = part * scale
            back = scale * (grad - full * jnp.sum(full * grad, axis=1, keepdims=True))
            out[pl.ds(own * CB, CB), :] += jnp.where(lane < prefix, back, 0.0)
    grad_ref[...] = out[...].astype(BF)
    loss_ref[...] = jnp.broadcast_to(loss, loss_ref.shape)
    tgrad_ref[...] = jnp.broadcast_to(tgrad, tgrad_ref.shape)


def contrast(info, emb_all, seg_col, counts, positive, temp_row, local):
    rows = emb_all.shape[0]
    return pl.pallas_call(
        contrast_kernel,
        in_specs=[pl.BlockSpec(memory_space=pltpu.SMEM)] + vmem_specs(5),
        out_specs=vmem_specs(3),
        out_shape=[
            jax.ShapeDtypeStruct((local, 128), BF),
            jax.ShapeDtypeStruct((8, 128), F32),
            jax.ShapeDtypeStruct((8, 128), F32),
        ],
        scratch_shapes=[
            pltpu.VMEM((rows, 128), BF),
            pltpu.VMEM((rows, 128), BF),
            pltpu.VMEM((rows, 128), F32),
            pltpu.VMEM((rows, 128), F32),
            pltpu.VMEM((128, 128), F32),
            pltpu.VMEM((local, 128), F32),
        ],
        compiler_params=pltpu.CompilerParams(vmem_limit_bytes=40 * 2**20),
        cost_estimate=pl.CostEstimate(flops=2**30, bytes_accessed=2**22, transcendentals=2**22),
    )(info, emb_all, seg_col, counts, positive, temp_row)


CW = 512
SLOTS_G, SLOTS_S, SLOTS_R, SLOTS_T, SLOTS_K = 3, 3, 4, 4, 6
SMALL_ROWS = 112


def neighbours():
    dp = lax.axis_index("dp")
    low = lax.rem(dp, 8)
    core = lax.rem(low, 2)
    x = lax.rem(low // 2, 2)
    y = low // 4
    return dp, low, core, x, y, dp + 1 - 2 * core, dp + 2 - 4 * x, dp + 4 - 8 * y


def entry_barrier(z, dp, plane, z_count):
    barrier = pltpu.get_barrier_semaphore()
    for other in plane:
        pl.semaphore_signal(barrier, inc=1, device_id={"dp": other, "tensor": z}, device_id_type=MESH)
    for step in range(1, z_count):
        peer = lax.rem(z + step, z_count)
        pl.semaphore_signal(barrier, inc=1, device_id={"dp": dp, "tensor": peer}, device_id_type=MESH)
    pl.semaphore_wait(barrier, len(plane) + z_count - 1)


def remote(src, dst, send_sem, recv_sem, dp, z):
    return pltpu.make_async_remote_copy(
        src_ref=src,
        dst_ref=dst,
        send_sem=send_sem,
        recv_sem=recv_sem,
        device_id={"dp": dp, "tensor": z},
        device_id_type=MESH,
    )


def scatter_kernel(
    window, attn_grad, normed, ffn_grad, dq, dk, dv, mixed, pre_grad, hidden, dxw, small_ref, proj_ref,
    out_qkv, out_attn, out_in, out_out, small_out, proj_out, from_left, from_right,
    xw, xa, xn, xf, gs, gkv, sbuf, rbuf, ta, tb, xra, xrb, s2a, s2b, yra, yrb, keep, zs, zrl, zrr,
    sacc, srec, zsm, pacc, prec, zpw,
    x_sem, g_sem, s_sem, r_sem, t_sem, xr_sem, s2_sem, yr_sem, zs_sem, zr_sem, sm_sem, smz_sem, h_sem, credit,
):
    dp, low, core, x, y, to_core, to_x, to_y = neighbours()
    z = lax.axis_index("tensor")
    nz = 4
    chunks = [("out", i) for i in range(8)] + [("in", i) for i in range(8)] + [("qa", i) for i in range(8)]
    count = len(chunks)
    local = attn_grad.shape[0]
    has_l = z > 0
    has_r = z < nz - 1

    x_loads = [
        pltpu.make_async_copy(src, dst, x_sem.at[index])
        for index, (src, dst) in enumerate(((ffn_grad, xf), (normed, xn), (window, xw), (attn_grad, xa)))
    ]
    for load in x_loads:
        load.start()

    def g_loads(index):
        kind, part = chunks[index]
        slot = index % SLOTS_G
        if kind != "qa":
            source = hidden if kind == "out" else pre_grad
            return [pltpu.make_async_copy(source.at[:, pl.ds(part * CW, CW)], gs.at[slot], g_sem.at[slot, 0])]
        columns = pl.ds((part // 2) * 256, 256)
        one, many = (dq, dk) if part % 2 == 0 else (mixed, dv)
        return [
            pltpu.make_async_copy(one.at[:, columns], gs.at[slot, :, pl.ds(0, 256)], g_sem.at[slot, 0]),
            pltpu.make_async_copy(many.at[:, columns], gkv.at[slot], g_sem.at[slot, 1]),
        ]

    for index in range(2):
        for load in g_loads(index):
            load.start()

    entry_barrier(z, dp, (to_core, to_x, to_y), nz)

    halo_l = remote(dxw.at[pl.ds(0, local)], from_right, h_sem.at[0], h_sem.at[1], dp, z - 1)
    halo_r = remote(dxw.at[pl.ds(2 * local, local)], from_left, h_sem.at[2], h_sem.at[3], dp, z + 1)

    peers = (to_core, to_x, to_y)

    def small_moves(stage):
        return [
            remote(sacc.at[stage], srec.at[stage], sm_sem.at[stage, 0], sm_sem.at[stage, 1], peers[stage], z),
            remote(pacc.at[stage], prec.at[stage], sm_sem.at[stage, 2], sm_sem.at[stage, 3], peers[stage], z),
        ]

    def small_z_moves(step):
        peer = lax.rem(z + step, nz)
        return [
            remote(sacc.at[3], zsm.at[step - 1], smz_sem.at[step - 1, 0], smz_sem.at[step - 1, 1], dp, peer),
            remote(pacc.at[3], zpw.at[step - 1], smz_sem.at[step - 1, 2], smz_sem.at[step - 1, 3], dp, peer),
        ]

    def small_stage(stage):
        if stage == 0:
            sacc[0] = small_ref[...]
            pacc[0] = proj_ref[...].astype(BF)
        if 1 <= stage <= 3:
            for move in small_moves(stage - 1):
                move.wait_recv()
            sacc[stage] = sacc[stage - 1] + srec[stage - 1]
            pacc[stage] = (pacc[stage - 1].astype(F32) + prec[stage - 1].astype(F32)).astype(BF)
        if stage <= 2:
            for move in small_moves(stage):
                move.start()
        if stage == 3:
            for step in range(1, nz):
                for move in small_z_moves(step):
                    move.start()
        if stage == 4:
            for step in range(1, nz):
                for move in small_z_moves(step):
                    move.wait_recv()
            for target, mine, others, low_rows in ((small_out, sacc, zsm, 0), (proj_out, pacc, zpw, 0)):
                total = None
                for owner in range(nz):
                    value = jnp.where(z == owner, mine[3].astype(F32), 0.0)
                    for step in range(1, nz):
                        value = jnp.where(lax.rem(z - step + nz, nz) == owner, others[step - 1].astype(F32), value)
                    total = value if total is None else total + value
                target[...] = total

    def block_columns(j, core_bit):
        xj = lax.rem(j, 2)
        yj = j // 2
        block = core_bit + 2 * (x + xj - 2 * x * xj) + 4 * (y + yj - 2 * y * yj)
        return pl.ds(pl.multiple_of(block * 128, 128), 128)

    def product(index, j, core_bit):
        kind, part = chunks[index]
        slot = index % SLOTS_G
        at = block_columns(j, core_bit)
        if kind == "out":
            return dot(xf[:, at], gs[slot], 0, 0)
        if kind == "in":
            return dot(xn[:, at], gs[slot], 0, 0)
        one = xw[pl.ds(local, local), at] if part % 2 == 0 else xa[:, at]
        return jnp.concatenate(
            [dot(one, gs[slot, :, 0:256], 0, 0), dot(xw[:, at], gkv[slot], 0, 0)], axis=1
        )

    def core_move(index):
        return remote(
            sbuf.at[index % SLOTS_S], rbuf.at[index % SLOTS_R], s_sem.at[index % SLOTS_S], r_sem.at[index % SLOTS_R],
            to_core, z,
        )

    half = CW // 2

    def ta_move(index):
        slot = index % SLOTS_T
        return remote(ta.at[slot, pl.ds(2, 2)], xra.at[index], t_sem.at[slot, 0], xr_sem.at[index, 0], to_x, z)

    def tb_move(index):
        slot = index % SLOTS_T
        return remote(tb.at[slot, pl.ds(2, 2)], xrb.at[index], t_sem.at[slot, 1], xr_sem.at[index, 1], to_y, z)

    def s2a_move(index):
        return remote(s2a.at[index], yra.at[index], s2_sem.at[index, 0], yr_sem.at[index, 0], to_y, z)

    def s2b_move(index):
        return remote(s2b.at[index], yrb.at[index], s2_sem.at[index, 1], yr_sem.at[index, 1], to_x, z)

    def right_move(index):
        return remote(zs.at[index], zrl.at[index], zs_sem.at[index], zr_sem.at[index, 0], dp, z + 1)

    def left_move(index):
        return remote(zs.at[index], zrr.at[index], zs_sem.at[index], zr_sem.at[index, 1], dp, z - 1)

    def stage_one(index):
        kind, part = chunks[index]
        if index == 0:
            x_loads[0].wait()
        if kind == "in" and part == 0:
            x_loads[1].wait()
        if kind == "qa" and part == 0:
            x_loads[2].wait()
            x_loads[3].wait()
        for load in g_loads(index):
            load.wait()
        if index >= SLOTS_S:
            core_move(index - SLOTS_S).wait_send()

        def body(j, unused):
            sbuf[index % SLOTS_S, j] = product(index, j, 1 - core).astype(BF)
            return unused

        lax.fori_loop(0, 4, body, 0)
        if index >= SLOTS_R:
            pl.semaphore_wait(credit, 1)
        core_move(index).start()

    def stage_two(index):
        core_move(index).wait_recv()
        slot = index % SLOTS_T
        if index >= SLOTS_T:
            ta_move(index - SLOTS_T).wait_send()
            tb_move(index - SLOTS_T).wait_send()

        def body(j, unused):
            total = product(index, j, core) + rbuf[index % SLOTS_R, j].astype(F32)
            ta[slot, j // 2 + 2 * lax.rem(j, 2)] = total[:, :half].astype(BF)
            tb[slot, j] = total[:, half:].astype(BF)
            return unused

        lax.fori_loop(0, 4, body, 0)
        if index + SLOTS_R < count:
            pl.semaphore_signal(credit, inc=1, device_id={"dp": to_core, "tensor": z}, device_id_type=MESH)
        ta_move(index).start()
        tb_move(index).start()

    def stage_three(index):
        slot = index % SLOTS_T
        kslot = index % SLOTS_K
        ta_move(index).wait_recv()
        s2a[index] = (ta[slot, 1].astype(F32) + xra[index, 1].astype(F32)).astype(BF)
        s2a_move(index).start()
        keep[kslot, :, :half] = ta[slot, 0].astype(F32) + xra[index, 0].astype(F32)
        tb_move(index).wait_recv()
        s2b[index] = (tb[slot, 1].astype(F32) + xrb[index, 1].astype(F32)).astype(BF)
        s2b_move(index).start()
        keep[kslot, :, half:] = tb[slot, 0].astype(F32) + xrb[index, 0].astype(F32)

    def stage_four(index):
        kslot = index % SLOTS_K
        goal = chunks[index][1] // 2
        s2a_move(index).wait_recv()
        keep[kslot, :, :half] += yra[index].astype(F32)
        s2b_move(index).wait_recv()
        keep[kslot, :, half:] += yrb[index].astype(F32)
        if goal > 0:

            @pl.when(z == 0)
            def _():
                zs[index] = keep[kslot].astype(BF)
                right_move(index).start()

        if goal < nz - 1:

            @pl.when(z == nz - 1)
            def _():
                zs[index] = keep[kslot].astype(BF)
                left_move(index).start()

    def stage_five(index, hop):
        kslot = index % SLOTS_K
        kind, part = chunks[index]
        goal = part // 2
        if hop <= goal:

            @pl.when(z == hop)
            def _():
                right_move(index).wait_recv()
                keep[kslot] += zrl[index].astype(F32)
                if hop < goal:
                    zs[index] = keep[kslot].astype(BF)
                    right_move(index).start()

        if hop <= nz - 1 - goal:

            @pl.when(z == nz - 1 - hop)
            def _():
                left_move(index).wait_recv()
                keep[kslot] += zrr[index].astype(F32)
                if nz - 1 - hop > goal:
                    zs[index] = keep[kslot].astype(BF)
                    left_move(index).start()

        if hop == nz - 1:

            @pl.when(z == goal)
            def _():
                if kind == "qa":
                    if part % 2 == 0:
                        out_qkv[:, 0:512] = keep[kslot]
                    else:
                        out_attn[...] = keep[kslot, :, 0:256]
                        out_qkv[:, 512:768] = keep[kslot, :, 256:512]
                else:
                    target = out_in if kind == "in" else out_out
                    target[:, pl.ds((part % 2) * CW, CW)] = keep[kslot]

    lag_three, lag_four = 3, 4
    for step in range(count + lag_four + nz):
        if step < count:
            stage_one(step)
        if step == 0:
            small_stage(0)
            pl.when(has_l)(lambda: halo_l.start())
            pl.when(has_r)(lambda: halo_r.start())
        if 0 <= step - 1 < count:
            stage_two(step - 1)
        if step + 2 < count:
            for load in g_loads(step + 2):
                load.start()
        if step in (2, 4, 6, 8):
            small_stage(step // 2)
        if 0 <= step - lag_three < count:
            stage_three(step - lag_three)
        if 0 <= step - lag_four < count:
            stage_four(step - lag_four)
        for hop in range(1, nz):
            index = step - lag_four - hop
            if 0 <= index < count:
                stage_five(index, hop)

    for index in range(count):
        goal = chunks[index][1] // 2
        if index >= count - SLOTS_S:
            core_move(index).wait_send()
        if index >= count - SLOTS_T:
            ta_move(index).wait_send()
            tb_move(index).wait_send()
        s2a_move(index).wait_send()
        s2b_move(index).wait_send()
        pl.when(z < goal)(lambda index=index: right_move(index).wait_send())
        pl.when(z > goal)(lambda index=index: left_move(index).wait_send())
    for stage in range(3):
        for move in small_moves(stage):
            move.wait_send()
    for step in range(1, nz):
        for move in small_z_moves(step):
            move.wait_send()

    @pl.when(has_l)
    def _():
        halo_l.wait_send()
        halo_r.wait_recv()

    @pl.when(has_r)
    def _():
        halo_r.wait_send()
        halo_l.wait_recv()


def scatter(window, attn_grad, normed, ffn_grad, dq, dk, dv, mixed, pre_grad, hidden, dxw, small, proj_grad):
    local, width = attn_grad.shape
    long = window.shape[0]
    dma = pltpu.SemaphoreType.DMA
    n = 24
    half = CW // 2
    shape = jax.ShapeDtypeStruct
    return pl.pallas_call(
        scatter_kernel,
        in_specs=hbm_specs(11) + vmem_specs(2),
        out_specs=vmem_specs(6) + hbm_specs(2),
        out_shape=[
            shape((128, 768), F32),
            shape((128, 256), F32),
            shape((128, 1024), F32),
            shape((128, 1024), F32),
            shape(small.shape, F32),
            shape(proj_grad.shape, F32),
            shape((local, width), BF),
            shape((local, width), BF),
        ],
        scratch_shapes=[
            pltpu.VMEM((long, width), BF),
            pltpu.VMEM((local, width), BF),
            pltpu.VMEM((local, width), BF),
            pltpu.VMEM((local, width), BF),
            pltpu.VMEM((SLOTS_G, local, CW), BF),
            pltpu.VMEM((SLOTS_G, long, 256), BF),
            pltpu.VMEM((SLOTS_S, 4, 128, CW), BF),
            pltpu.VMEM((SLOTS_R, 4, 128, CW), BF),
            pltpu.VMEM((SLOTS_T, 4, 128, half), BF),
            pltpu.VMEM((SLOTS_T, 4, 128, half), BF),
            pltpu.VMEM((n, 2, 128, half), BF),
            pltpu.VMEM((n, 2, 128, half), BF),
            pltpu.VMEM((n, 128, half), BF),
            pltpu.VMEM((n, 128, half), BF),
            pltpu.VMEM((n, 128, half), BF),
            pltpu.VMEM((n, 128, half), BF),
            pltpu.VMEM((SLOTS_K, 128, CW), F32),
            pltpu.VMEM((n, 128, CW), BF),
            pltpu.VMEM((n, 128, CW), BF),
            pltpu.VMEM((n, 128, CW), BF),
            pltpu.VMEM((4,) + small.shape, F32),
            pltpu.VMEM((3,) + small.shape, F32),
            pltpu.VMEM((3,) + small.shape, F32),
            pltpu.VMEM((4,) + proj_grad.shape, BF),
            pltpu.VMEM((3,) + proj_grad.shape, BF),
            pltpu.VMEM((3,) + proj_grad.shape, BF),
            dma((4,)),
            dma((SLOTS_G, 2)),
            dma((SLOTS_S,)),
            dma((SLOTS_R,)),
            dma((SLOTS_T, 2)),
            dma((n, 2)),
            dma((n, 2)),
            dma((n, 2)),
            dma((n,)),
            dma((n, 2)),
            dma((3, 4)),
            dma((3, 4)),
            dma((4,)),
            pltpu.SemaphoreType.REGULAR,
        ],
        compiler_params=pltpu.CompilerParams(
            collective_id=2, has_side_effects=True, vmem_limit_bytes=VMEM_BIG
        ),
    )(window, attn_grad, normed, ffn_grad, dq, dk, dv, mixed, pre_grad, hidden, dxw, small, proj_grad)


def source_rows(kind, ref, start, rows):
    return ref.at[:, pl.ds(start, rows), :] if kind == "qkv" else ref.at[pl.ds(start, rows), :]


def gathered_rows(kind, ref, shard, start, rows):
    if kind == "qkv":
        return ref.at[:, pl.ds(start, rows), pl.ds(pl.multiple_of(shard * 256, 256), 256)]
    if kind == "in":
        return ref.at[pl.ds(start, rows), pl.ds(pl.multiple_of(shard * 1024, 1024), 1024)]
    per = ref.shape[0] // 4
    return ref.at[pl.ds(pl.multiple_of(shard * per + start, 16), rows), :]


def shard_rows(kind, ref):
    return ref.shape[1] if kind == "qkv" else ref.shape[0]


def gather_kernel(kinds, with_tokens, *refs):
    n = len(kinds)
    nz = 4
    srcs, refs = refs[:n], refs[n:]
    if with_tokens:
        (tokens, bias), refs = refs[:2], refs[2:]
    outs, refs = refs[:n], refs[n:]
    if with_tokens:
        (window, bias_all), refs = refs[:2], refs[2:]
    z_recv, z_send, p_recv, p_send, l_sem = refs[:5]
    stage, refs = refs[5 : 5 + n], refs[5 + n :]
    if with_tokens:
        h_sem, b_sem, token_stage = refs
    dp, low, core, x, y, to_core, to_x, to_y = neighbours()
    z = lax.axis_index("tensor")
    has_l = z > 0
    has_r = z < nz - 1
    low_x = low + 2 - 4 * x
    low_y = low + 4 - 8 * y
    low_xy = low_x + 4 - 8 * y

    copies_in = [pltpu.make_async_copy(srcs[m], stage[m], l_sem.at[m, 0]) for m in range(n)]
    copies_out = [
        pltpu.make_async_copy(
            stage[m], gathered_rows(kinds[m], outs[m], z, 0, shard_rows(kinds[m], srcs[m])), l_sem.at[m, 1]
        )
        for m in range(n)
    ]
    for copy in copies_in:
        copy.start()
    if with_tokens:
        token_in = pltpu.make_async_copy(tokens, token_stage, h_sem.at[7])
        token_in.start()
        bias_all[pl.ds(z, 1)] = bias[...].reshape(1, *bias.shape)
    entry_barrier(z, dp, (to_core, to_x, to_y), nz)

    def piece(m, shard, index, half=None):
        rows = shard_rows(kinds[m], srcs[m]) // 8
        start = index * rows
        if half is not None:
            rows = rows // 2
            start = start + half * rows
        return gathered_rows(kinds[m], outs[m], shard, pl.multiple_of(start, 16), rows)

    def shard_of(side, distance):
        return z - distance if side == 0 else z + distance

    def onward(side):
        return z + 1 if side == 0 else z - 1

    def can_send(side):
        return has_r if side == 0 else has_l

    def arrives(side, distance):
        return z >= distance if side == 0 else z + distance < nz

    def own_move(m, side):
        rows = shard_rows(kinds[m], srcs[m]) // 8
        src = source_rows(kinds[m], srcs[m], pl.multiple_of(low * rows, 16), rows)
        return remote(src, piece(m, z, low), z_send.at[m, side, 0], z_recv.at[m, side, 0], dp, onward(side))

    def relay_move(m, side, distance):
        at = piece(m, shard_of(side, distance), low)
        return remote(at, at, z_send.at[m, side, distance], z_recv.at[m, side, distance], dp, onward(side))

    def plane_move(m, side, distance, kind):
        shard = shard_of(side, distance)
        at = {
            0: (low, None), 1: (low, None), 4: (low, None), 2: (low_x, 0), 3: (low_y, 1),
            5: (low_x, None), 6: (low_y, None), 7: (low_xy, 0), 8: (low_xy, 1),
        }[kind]
        ref = piece(m, shard, *at)
        to = {0: to_x, 1: to_y, 2: to_y, 3: to_x}.get(kind, to_core)
        slot = side * 3 + distance - 1
        return remote(ref, ref, p_send.at[m, slot, kind], p_recv.at[m, slot, kind], to, z)

    if with_tokens:
        local = tokens.shape[0]
        to_left = remote(tokens, window.at[pl.ds(2 * local, local)], h_sem.at[0], h_sem.at[1], dp, z - 1)
        to_right = remote(tokens, window.at[pl.ds(0, local)], h_sem.at[2], h_sem.at[3], dp, z + 1)
        own_tokens = pltpu.make_async_copy(token_stage, window.at[pl.ds(local, local)], h_sem.at[4])
        fill_left = pltpu.make_async_copy(token_stage, window.at[pl.ds(0, local)], h_sem.at[5])
        fill_right = pltpu.make_async_copy(token_stage, window.at[pl.ds(2 * local, local)], h_sem.at[6])

        def bias_move(step):
            peer = lax.rem(z + step, nz)
            return remote(bias, bias_all.at[z], b_sem.at[0, step - 1], b_sem.at[1, step - 1], dp, peer)

        for step in range(1, nz):
            bias_move(step).start()

    def own_start(m):
        for side in (0, 1):
            pl.when(can_send(side))(lambda side=side: own_move(m, side).start())

    own_start(0)
    if with_tokens:
        token_in.wait()
        own_tokens.start()
        pl.when(jnp.logical_not(has_l))(lambda: fill_left.start())
        pl.when(jnp.logical_not(has_r))(lambda: fill_right.start())
    for copy_in, copy_out in zip(copies_in, copies_out):
        copy_in.wait()
        copy_out.start()

    def stage_z(m, distance, side):
        if side == 0 and distance == 2 and m + 1 < n:
            own_start(m + 1)
        if side == 0 and distance == 3 and with_tokens and m == 0:
            pl.when(has_l)(lambda: to_left.start())
            pl.when(has_r)(lambda: to_right.start())

        @pl.when(arrives(side, distance))
        def _():
            if distance == 1:
                own_move(m, side).wait_recv()
            else:
                relay_move(m, side, distance - 1).wait_recv()
            if distance < 3:
                pl.when(can_send(side))(lambda: relay_move(m, side, distance).start())
            for kind in (0, 1, 4):
                plane_move(m, side, distance, kind).start()

    def stage_xy(m, distance, side):
        @pl.when(arrives(side, distance))
        def _():
            for kind in (0, 1):
                plane_move(m, side, distance, kind).wait_recv()
                plane_move(m, side, distance, kind + 2).start()
                plane_move(m, side, distance, kind + 5).start()

    def stage_diagonal(m, distance, side):
        @pl.when(arrives(side, distance))
        def _():
            for kind in (2, 3):
                plane_move(m, side, distance, kind).wait_recv()
                plane_move(m, side, distance, kind + 5).start()

    events = [(m, distance, side) for m in range(n) for distance in (1, 2, 3) for side in (0, 1)]
    lag = 4
    for step in range(len(events) + 2 * lag):
        if step < len(events):
            stage_z(*events[step])
        if 0 <= step - lag < len(events):
            stage_xy(*events[step - lag])
        if 0 <= step - 2 * lag < len(events):
            stage_diagonal(*events[step - 2 * lag])

    for m, distance, side in events:

        @pl.when(arrives(side, distance))
        def _():
            for kind in (4, 5, 6, 7, 8):
                plane_move(m, side, distance, kind).wait_recv()
            for kind in range(9):
                plane_move(m, side, distance, kind).wait_send()
            if distance < 3:
                pl.when(can_send(side))(lambda: relay_move(m, side, distance).wait_send())

    for m in range(n):
        for side in (0, 1):
            pl.when(can_send(side))(lambda side=side: own_move(m, side).wait_send())
        copies_out[m].wait()
    if with_tokens:
        own_tokens.wait()
        for step in range(1, nz):
            bias_move(step).wait()

        @pl.when(has_l)
        def _():
            to_left.wait_send()
            to_right.wait_recv()

        @pl.when(has_r)
        def _():
            to_right.wait_send()
            to_left.wait_recv()

        pl.when(jnp.logical_not(has_l))(lambda: fill_left.wait())
        pl.when(jnp.logical_not(has_r))(lambda: fill_right.wait())


def gather(kinds, arrays, collective_id, tokens=None, bias=None):
    n = len(kinds)
    with_tokens = tokens is not None
    width = 1024
    shapes = {"qkv": (3, width, width), "attn": (width, width), "in": (width, 4 * width), "out": (4 * width, width)}
    out_shape = [jax.ShapeDtypeStruct(shapes[kind], BF) for kind in kinds]
    in_specs = hbm_specs(n)
    out_specs = hbm_specs(n)
    dma = pltpu.SemaphoreType.DMA
    scratch = [dma((n, 2, 3)), dma((n, 2, 3)), dma((n, 6, 9)), dma((n, 6, 9)), dma((n, 2))]
    scratch += [pltpu.VMEM(array.shape, BF) for array in arrays]
    args = list(arrays)
    if with_tokens:
        args += [tokens, bias]
        in_specs += hbm_specs(1) + vmem_specs(1)
        out_specs += hbm_specs(1) + vmem_specs(1)
        out_shape += [
            jax.ShapeDtypeStruct((3 * tokens.shape[0], width), BF),
            jax.ShapeDtypeStruct((4,) + bias.shape, BF),
        ]
        scratch += [dma((8,)), dma((2, 3)), pltpu.VMEM(tokens.shape, BF)]
    return pl.pallas_call(
        partial(gather_kernel, tuple(kinds), with_tokens),
        in_specs=in_specs,
        out_specs=out_specs,
        out_shape=out_shape,
        scratch_shapes=scratch,
        compiler_params=pltpu.CompilerParams(
            collective_id=collective_id, has_side_effects=True, vmem_limit_bytes=40 * 2**20
        ),
    )(*args)


def norm_forward(values, gain, shift):
    mean_value = jnp.mean(values, axis=-1, keepdims=True)
    centered = values - mean_value
    variance = jnp.mean(centered * centered, axis=-1, keepdims=True)
    scale = lax.rsqrt(variance + eps_norm)
    unit = centered * scale
    return unit * gain + shift, unit, scale


def norm_back(unit, scale, gain, grad):
    dn = grad * gain
    back = scale * (
        dn - jnp.mean(dn, axis=-1, keepdims=True) - unit * jnp.mean(dn * unit, axis=-1, keepdims=True)
    )
    return back, jnp.sum(grad * unit, axis=0), jnp.sum(grad, axis=0)


def per_device(
    tokens, lengths, doc_pairs, qkv_weight, qkv_bias, attn_weight, attn_bias, ffn_in_weight, ffn_in_bias,
    ffn_out_weight, ffn_out_bias, norm_gains, norm_shifts, proj_weight, log_temp,
):
    local, width = tokens.shape
    dp_count = lax.axis_size("dp")
    tensor_count = lax.axis_size("tensor")
    groups = dp_count // 8
    z = lax.axis_index("tensor")
    base = z * local

    row_lengths = lengths[0]
    seg_range = jnp.arange(SEGS, dtype=jnp.int32)
    seg_ends = jnp.sum(jnp.where(seg_range[:, None] >= seg_range[None, :], row_lengths[None, :], 0), axis=1)
    seg_starts = seg_ends - row_lengths
    positions = jnp.arange(SEQ, dtype=jnp.int32)
    seg_ids = jnp.sum((positions[:, None] >= seg_ends[None, :]).astype(jnp.int32), axis=1)
    near = jnp.arange(3 * local, dtype=jnp.int32) + base - local
    near_ids = jnp.sum((near[:, None] >= seg_ends[None, :]).astype(jnp.int32), axis=1)
    near_ids = jnp.where((near >= 0) & (near < SEQ), near_ids, -1)
    near_member = near_ids[:, None] == jnp.arange(SEGS, dtype=jnp.int32)[None, :]
    near_starts = jnp.sum(jnp.where(near_member, seg_starts[None, :], 0), axis=1)
    offsets = jnp.where(near_ids >= 0, near - near_starts, 0)
    half_dim = HDIM // 2
    inv_freq = jnp.exp(jnp.arange(half_dim, dtype=F32) * (-2.0 * math.log(10000.0) / HDIM))
    angles = offsets.astype(F32)[:, None] * inv_freq[None, :]
    cosine, sine = jnp.cos(angles), jnp.sin(angles)
    cosine = jnp.concatenate([cosine] * 4, axis=1)
    sine = jnp.concatenate([-sine, sine] * 2, axis=1)
    seg_q = jnp.broadcast_to(lax.slice_in_dim(near_ids, local, 2 * local)[:, None], (local, 128))
    seg_k = jnp.broadcast_to(near_ids[None, :], (8, 3 * local))
    starts_at = jnp.arange(local // BQ, dtype=jnp.int32) * BQ + base
    first_seg = jnp.sum((starts_at[:, None] >= seg_ends[None, :]).astype(jnp.int32), axis=1)
    last_seg = jnp.sum(((starts_at + BQ - 1)[:, None] >= seg_ends[None, :]).astype(jnp.int32), axis=1)
    first_key = jnp.sum(jnp.where(first_seg[:, None] == seg_range, seg_starts, 0), axis=1) - base + local
    last_key = jnp.sum(jnp.where(last_seg[:, None] == seg_range, seg_ends, 0), axis=1) - base + local
    bounds = jnp.stack([first_key // BK, (last_key + BK - 1) // BK], axis=1)
    query_end = seg_ends[NQ - 1]
    info = jnp.stack([base // CB, (query_end + CB - 1) // CB, query_end // CB])
    seg_col = jnp.broadcast_to(seg_ids[:, None], (SEQ, 128))
    counts = jnp.broadcast_to(row_lengths.astype(F32)[:, None], (SEGS, 128))
    positive = (doc_pairs[0][:, None] == jnp.arange(128, dtype=jnp.int32)[None, :]).astype(F32)
    loss_scale = 1.0 / (NQ * dp_count)
    temp_row = jnp.concatenate([log_temp, jnp.full((127,), loss_scale, F32)]).reshape(1, 128)

    gains = norm_gains.astype(F32)
    shifts = norm_shifts.astype(F32)
    bias = jnp.concatenate([qkv_bias.reshape(6, 128), ffn_in_bias.reshape(8, 128), jnp.zeros((2, 128), BF)])
    qkv_all, window, bias_all = gather(("qkv",), (jnp.transpose(qkv_weight, (1, 0, 2)),), 0, tokens, bias)
    attn_all, in_all, out_all = gather(("attn", "in", "out"), (attn_weight, ffn_in_weight, ffn_out_weight), 1)
    qkv_bias_all = jnp.transpose(bias_all[:, :6].reshape(4, 3, 256), (1, 0, 2)).reshape(3, 1, width)
    in_bias_all = bias_all[:, 6:14].reshape(4 * width).astype(F32)

    queries, keys, values = project(window, qkv_all, qkv_bias_all, cosine, sine)
    mixed, lse = attend(bounds, queries, keys, values, seg_q, seg_k)
    attn_out = dot(mixed, attn_all) + attn_bias.astype(F32)
    normed, unit_one, scale_one = norm_forward(tokens.astype(F32) + attn_out, gains[0], shifts[0])
    normed_low = normed.astype(BF)
    ffn_pre = dot(normed_low, in_all) + in_bias_all
    hidden = jax.nn.gelu(ffn_pre, approximate=False).astype(BF)
    resid_two = normed + dot(hidden, out_all) + ffn_out_bias.astype(F32)
    output, unit_two, scale_two = norm_forward(resid_two, gains[1], shifts[1])
    output_low = output.astype(BF)
    embedded = dot(output_low, proj_weight).astype(BF)
    embedded_all = lax.all_gather(embedded, "tensor", axis=0, tiled=True)
    emb_grad, row_loss, row_temp = contrast(info, embedded_all, seg_col, counts, positive, temp_row, local)

    proj_grad = dot(output_low, emb_grad, 0, 0)
    output_grad = dot(emb_grad, proj_weight, 1, 1)
    resid_two_grad, gain_two_grad, shift_two_grad = norm_back(unit_two, scale_two, gains[1], output_grad)
    ffn_grad = resid_two_grad.astype(BF)
    out_bias_grad = jnp.sum(ffn_grad.astype(F32), axis=0)
    hidden_grad = dot(ffn_grad, out_all, 1, 1)
    unused, gelu_pull = jax.vjp(partial(jax.nn.gelu, approximate=False), ffn_pre)
    pre_grad = gelu_pull(hidden_grad)[0].astype(BF)
    in_bias_grad = jnp.sum(pre_grad.astype(F32), axis=0)
    normed_grad = dot(pre_grad, in_all, 1, 1) + resid_two_grad
    resid_one_grad, gain_one_grad, shift_one_grad = norm_back(unit_one, scale_one, gains[0], normed_grad)
    attn_grad = resid_one_grad.astype(BF)
    attn_bias_grad = jnp.sum(attn_grad.astype(F32), axis=0)
    mixed_grad = dot(attn_grad, attn_all, 1, 1).astype(BF)
    dq, dk, dv = attend_back(bounds, queries, keys, values, mixed, mixed_grad, lse, seg_q, seg_k, cosine, sine)
    window_grad = dot(dk, qkv_all[1], 1, 1) + dot(dv, qkv_all[2], 1, 1)
    window_low = window_grad.astype(BF)
    own_grad = window_grad[local : 2 * local] + dot(dq, qkv_all[0], 1, 1) + resid_one_grad
    qkv_bias_grad = jnp.concatenate([jnp.sum(part.astype(F32), axis=0) for part in (dq, dk, dv)])

    share = 1.0 / tensor_count
    small = jnp.concatenate(
        [
            attn_bias_grad, out_bias_grad, gain_one_grad, gain_two_grad, shift_one_grad, shift_two_grad,
            qkv_bias_grad, in_bias_grad, row_loss[0, :1] * share, row_temp[0, :1] * share,
            jnp.zeros((SMALL_ROWS * 128 - 13 * width - 2,), F32),
        ]
    ).reshape(SMALL_ROWS, 128)

    def arrange(array):
        if groups == 1:
            return array
        rows = array.shape[0]
        return array.reshape(rows, groups, 8, -1).transpose(0, 2, 1, 3).reshape(rows, width)

    qkv_red, attn_red, in_red, out_red, small, proj_red, from_left, from_right = scatter(
        arrange(window), arrange(attn_grad), arrange(normed_low), arrange(ffn_grad),
        dq, dk, dv, mixed, pre_grad, hidden, window_low, small, proj_grad,
    )
    if groups > 1:
        ranks = [[high * 8 + low for high in range(groups)] for low in range(8)]
        qkv_red, attn_red, in_red, out_red = (
            lax.psum_scatter(part, "dp", scatter_dimension=0, axis_index_groups=ranks, tiled=True)
            for part in (qkv_red, attn_red, in_red, out_red)
        )
        small, proj_red = lax.psum((small, proj_red), "dp", axis_index_groups=ranks)
    tokens_grad = (
        own_grad
        + jnp.where(z > 0, from_left.astype(F32), 0.0)
        + jnp.where(z < tensor_count - 1, from_right.astype(F32), 0.0)
    )
    flat = small.reshape(-1)

    def cut(start, length):
        return lax.slice_in_dim(flat, start * width, (start + length) * width)

    qkv_bias_red = lax.dynamic_slice_in_dim(cut(6, 3).reshape(3, width), z * 256, 256, 1)
    in_bias_red = lax.dynamic_slice_in_dim(cut(9, 4), z * width, width, 0)
    return (
        flat[13 * width : 13 * width + 1],
        output_low,
        tokens_grad,
        qkv_red.reshape(-1, 3, 256),
        qkv_bias_red,
        attn_red.T,
        cut(0, 1),
        in_red,
        in_bias_red,
        out_red.T,
        cut(1, 1),
        cut(2, 2).reshape(2, width),
        cut(4, 2).reshape(2, width),
        proj_red,
        flat[13 * width + 1 : 13 * width + 2],
    )


def solution(mesh):
    in_specs = (
        P(("dp", "tensor"), None),
        P("dp", None),
        P("dp", None),
        P(None, None, "tensor"),
        P(None, "tensor"),
        P("tensor", None),
        P(),
        P(None, "tensor"),
        P("tensor"),
        P("tensor", None),
        P(),
        P(),
        P(),
        P(),
        P(),
    )
    out_specs = (
        P(),
        P(("dp", "tensor"), None),
        P(("dp", "tensor"), None),
        P("dp", None, "tensor"),
        P(None, "tensor"),
        P("tensor", "dp"),
        P(),
        P("dp", "tensor"),
        P("tensor"),
        P("tensor", "dp"),
        P(),
        P(),
        P(),
        P(),
        P(),
    )
    return jax.shard_map(
        per_device, mesh=mesh, in_specs=in_specs, out_specs=out_specs, check_vma=False
    )
```

time: 1700 us -> 667 us (0.39)
  waiting for transfers between devices: 846 us -> 0 us
  Pallas kernels: 0 us -> 499 us
  matrix products: 490 us -> 81 us
  other arithmetic: 236 us -> 21.5 us
  blocking collectives: 76.2 us -> 17.1 us
    pallas_call x0 -> x7, Pallas kernels: none -> 499 us  [the longest x1 188 us: scatter(): pl.pallas_call(scatter_kernel, in_specs=hbm_specs(11) + vmem_specs(2), ou...]
    dot_general x132 -> x12, matrix products: 490 us -> 81 us  [dot(): lax.dot_general(left, right, (((left_dim,), (right_dim,)), ((), ())), pre...]
    reduce_scatter x8 -> x0, waiting for transfers between devices: 403 us -> none  [the longest x1 77.4 us: per_device(): lax.psum_scatter(jnp.einsum('tf,df->td', pre_grad, ffn_in_weight, preferr...]
    all_gather x4 -> x0, waiting for transfers between devices: 310 us -> none  [the longest x1 79.4 us: per_device(): lax.all_gather(normed.astype(jnp.bfloat16), 'tensor', axis=0, tiled=True)]
    psum x1 -> x0, waiting for transfers between devices: 131 us -> none  [per_device(): lax.psum((attn_bias_grad, out_bias_grad, jnp.stack([gain_one_grad, gain_t...]
    sub x4, other arithmetic: 102 us -> 0.69 us  [the longest x1 0.67 us: per_device(): seg_starts = seg_ends - row_lengths]
    psum x2 -> x0, blocking collectives: 60 us -> none  [the longest x1 46.1 us: per_device(): lax.psum((attn_bias_grad, out_bias_grad, jnp.stack([gain_one_grad, gain_t...]
    convert_element_type x15 -> x8, other arithmetic: 52.7 us -> 4.8 us  [the longest x1 2.96 us: per_device(): output_low = output.astype(BF)]
  transfers between devices with their start and end apart: 13 -> 0, of which waited for: 12 -> 0; matrix products, arithmetic and copies ran while one was open for 3% -> 0% of each run, Pallas kernels for 0% -> 0%
where the time goes in v1:
time: 667 us; the launch traced here: 659 us
  Pallas kernels  499 us (75%)
  matrix products  81 us (12%)
  local copies, waits for them, and re-layouts  33.1 us (5%)
  other arithmetic  21.5 us (3%)
  blocking collectives  17.1 us (3%)
  between operations  7.06 us (1%)
    pallas_call x1, Pallas kernels, scatter(): pl.pallas_call(scatter_kernel, in_specs=hbm_specs(11) + vmem_specs(2), ou...  188 us
    pallas_call x2, Pallas kernels, gather(): pl.pallas_call(partial(gather_kernel, tuple(kinds), with_tokens), in_spec...  145 us
    dot_general x12, matrix products, dot(): lax.dot_general(left, right, (((left_dim,), (right_dim,)), ((), ())), pre...  81 us
    pallas_call x1, Pallas kernels, attend_back(): pl.pallas_call(attend_back_kernel, grid_spec=pltpu.PrefetchScalarGridSpec...  53.2 us
    pallas_call x1, Pallas kernels, contrast(): pl.pallas_call(contrast_kernel, in_specs=[pl.BlockSpec(memory_space=pltpu...  49.1 us
    pallas_call x1, Pallas kernels, attend(): pl.pallas_call(attend_kernel, grid_spec=pltpu.PrefetchScalarGridSpec(num_...  47.9 us
    unnamed x109, local copies, waits for them, and re-layouts  20.8 us
    all_gather x1, blocking collectives, per_device(): embedded_all = lax.all_gather(embedded, 'tensor', axis=0, tiled=True)  17.1 us

profile of v1, /device:TPU:24, one launch (start us, length us, event | category | flops | bytes accessed | tf_op | source)
XLA Modules:
  0.0 659.2 jit_solution(15693027174814209849)
XLA Ops:
  0.7 0.7 reshape.303
  1.5 0.8 maximum_maximum_fusion.refs_2_
  2.2 1.4 copy-done.9
  3.6 1.2 copy-done.10
  4.9 41.1 %shard_map.262 = (bf16[3,1024,1024]{2,1,0:T(8,128)(2,1)S(1)}, bf16[1536,1024]{1,0:T(8,128)(2,1)S(1)}, bf16[4,16,128]{2,1,0:T(8,128)(2,1)S(1)}) custom-call(bf16[3,1024,256]{2,1,0:T(8,128)(2,1)S(1)} %bitcast.79, bf16[512,1024]{1,0:T(8,128)(2,1)S(1)} %copy-done.10, bf16[16,128]{1,0:T(8,128)(2,1)S(1)} %maximum_maximum_fusion.refs_2_), custom_call_target="tpu_custom_call" | custom-call | tf_op jit(solution)/shard_map/pallas_call | solution.py:1016
  46.0 2.6 copy-done.21
  49.3 0.8 select_reduce_fusion.1
  52.6 2.8 fusion.20
  55.4 1.3 pad_maximum_fusion
  56.7 16.2 %shard_map.263 = (bf16[512,1024]{1,0:T(8,128)(2,1)S(1)}, bf16[1536,1024]{1,0:T(8,128)(2,1)S(1)}, bf16[1536,1024]{1,0:T(8,128)(2,1)S(1)}) custom-call(bf16[1536,1024]{1,0:T(8,128)(2,1)S(1)} %get-tuple-element.40.window_ref.window, bf16[3,1024,1024]{2,1,0:T(8,128)(2,1)} %copy-done.21, bf16[3,1,1024]{2,1,0:T(2,128)(2,1)S(1)} %copy.77.bias_ref, ...), custom_call_target="tpu_custom_call" | custom-call | flops 7516192768 | bytes 14680064 | tf_op jit(solution)/shard_map/pallas_call | solution.py:88
  73.0 1.6 copy-done.23
  74.8 3.5 copy-done.24
  78.3 47.9 %shard_map.264 = (bf16[512,1024]{1,0:T(8,128)(2,1)S(1)}, f32[8,512,128]{2,1,0:T(8,128)S(1)}) custom-call(s32[4,2]{1,0:T(4,128)S(1)} %pad_add_fusion.bounds_ref, bf16[512,1024]{1,0:T(8,128)(2,1)S(1)} %get-tuple-element.43.query_ref, bf16[1536,1024]{1,0:T(8,128)(2,1)S(1)} %get-tuple-element.44.key_ref, bf16[1536,1024]{1,0:T(8,128)(2,1)S(1)} %copy-done.24, ...), custom_call_target="tpu_custom_call" | custom-call | flops 2147483648 | bytes 8388608 | tf_op jit(solution)/shard_map/pallas_call | solution.py:162
  126.2 104.0 %shard_map.265 = (bf16[1024,1024]{1,0:T(8,128)(2,1)S(1)}, bf16[1024,4096]{1,0:T(8,128)(2,1)}, bf16[4096,1024]{1,0:T(8,128)(2,1)}) custom-call(bf16[256,1024]{1,0:T(8,128)(2,1)S(1)} %copy-done.18, bf16[1024,1024]{1,0:T(8,128)(2,1)S(1)} %copy-done.7, bf16[1024,1024]{1,0:T(8,128)(2,1)S(1)} %copy-done.8), custom_call_target="tpu_custom_call" | custom-call | tf_op jit(solution)/shard_map/pallas_call | solution.py:1016
  230.3 1.4 fusion.36
  232.6 2.2 copy-done.47
  234.9 24.0 %multiply_convert_fusion = (bf16[512,4096]{1,0:T(8,128)(2,1)S(1)}, f32[512,4096]{1,0:T(8,128)}, f32[512,4096]{1,0:T(8,128)}) fusion(f32[4096]{0:T(1024)S(1)} %bitcast_convert_fusion, bf16[512,1024]{1,0:T(8,128)(2,1)S(1)} %fusion.17.normed, bf16[1024,4096]{1,0:T(8,128)(2,1)S(1)} %copy-done.47), kind=kOutput, calls=%fused_computation.4 | convolution fusion | flops 4433379328 | bytes 30425088 | tf_op jit(solution)/shard_map/dot_general | solution.py:26
  258.9 6.1 fusion.37
  265.0 1.9 multiply_reduce_fusion.4
  270.9 3.0 add_convert_fusion.1
  273.9 1.7 convolution_convert_fusion.1
  275.5 17.1 %all_gather.3.emb_ref = bf16[2048,128]{1,0:T(8,128)(2,1)S(1)} all-gather(bf16[512,128]{1,0:T(8,128)(2,1)S(1)} %convolution_convert_fusion.1), channel_id=1, replica_groups=mesh['dp'=8,'tensor'=4] {'tensor'}, dimensions={0}, use_global_device_ids=true | all-gather | bytes 655360 | tf_op jit(solution)/shard_map/all_gather | solution.py:1109
  293.9 49.1 %shard_map.266 = (bf16[512,128]{1,0:T(8,128)(2,1)S(1)}, f32[8,128]{1,0:T(8,128)S(1)}, f32[8,128]{1,0:T(8,128)S(1)}) custom-call(s32[3]{0:T(128)S(1)} %pad_add_fusion.1.info_ref, bf16[2048,128]{1,0:T(8,128)(2,1)S(1)} %all_gather.3.emb_ref, s32[2048,128]{1,0:T(8,128)S(1)} %broadcast_in_dim.71.segc_ref, f32[16,128]{1,0:T(8,128)S(1)} %broadcast_in_dim.72.counts_ref, ...), custom_call_target="tpu_custom_call" | custom-call | flops 1073741824 | bytes 4194304 | tf_op jit(solution)/shard_map/pallas_call | solution.py:368
  343.0 3.1 multiply_reduce_fusion
  346.1 3.6 convert_reduce_fusion.4
  349.7 14.4 %convert_reduce_fusion = (f32[4096]{0:T(1024)}, bf16[512,4096]{1,0:T(8,128)(2,1)S(1)}) fusion(f32[512,4096]{1,0:T(8,128)} %get-tuple-element.144, f32[512,4096]{1,0:T(8,128)} %get-tuple-element.162, f32[4096]{0:T(1024)S(1)} %bitcast_convert_fusion, bf16[512,1024]{1,0:T(8,128)(2,1)S(1)} %get-tuple-element.138.ffn_grad, bf16[4096,1024]{1,0:T(8,128)(2,1)} %get-tuple-element.49), kind=kOutput, calls=%fused_computation.2 | convolution fusion | flops 4330614784 | bytes 30441472 | tf_op jit(solution)/shard_map/dot_general | solution.py:26
  364.1 11.2 %multiply_reduce_fusion.1 = (f32[1024]{0:T(1024)}, f32[512]{0:T(512)S(1)}, f32[512]{0:T(512)S(1)}, f32[1024]{0:T(1024)}, f32[512,1024]{1,0:T(8,128)S(1)}) fusion(f32[512,1024]{1,0:T(8,128)S(1)} %copy-done.30, f32[512]{0:T(512)S(1)} %add_rsqrt_fusion.1, f32[512]{0:T(512)S(1)} %broadcast_multiply_fusion.5, f32[1024]{0:T(1024)S(1)} %bitcast.89, ...), kind=kOutput, calls=%fused_computation.33 | convolution fusion | flops 4300207104 | bytes 18894848 | tf_op jit(solution)/shard_map/dot_general | solution.py:26
  375.4 2.0 convert_reduce_fusion.5
  377.4 1.3 convolution_convert_fusion.grad_ref
  379.5 0.7 copy-done.26
  380.4 53.2 %shard_map.267 = (bf16[512,1024]{1,0:T(8,128)(2,1)S(1)}, bf16[1536,1024]{1,0:T(8,128)(2,1)S(1)}, bf16[1536,1024]{1,0:T(8,128)(2,1)S(1)}) custom-call(s32[4,2]{1,0:T(4,128)S(1)} %pad_add_fusion.bounds_ref, bf16[512,1024]{1,0:T(8,128)(2,1)S(1)} %copy-done.28, bf16[1536,1024]{1,0:T(8,128)(2,1)} %copy-done.22, bf16[1536,1024]{1,0:T(8,128)(2,1)} %copy-done.23, ...), custom_call_target="tpu_custom_call" | custom-call | flops 5368709120 | bytes 16777216 | tf_op jit(solution)/shard_map/pallas_call | solution.py:237
  433.7 3.5 fusion.12
  437.3 6.2 fusion.38
  447.3 0.7 concatenate.19
  448.0 2.5 fusion.39.proj_ref
  450.5 187.7 %shard_map.268 = (f32[128,768]{1,0:T(8,128)}, f32[128,256]{1,0:T(8,128)}, f32[128,1024]{1,0:T(8,128)}, f32[128,1024]{1,0:T(8,128)}, f32[112,128]{1,0:T(8,128)}, ...) custom-call(bf16[1536,1024]{1,0:T(8,128)(2,1)} %copy-done.6, ...), custom_call_target="tpu_custom_call" | custom-call | tf_op jit(solution)/shard_map/pallas_call | solution.py:734
  638.2 1.3 fusion.32
  639.6 5.7 fusion.8
  645.2 1.2 copy.78
  646.5 0.9 copy.79
  647.4 0.7 slice.95
  648.7 0.8 copy.80
  649.5 1.3 slice_bitcast_fusion.1
  650.7 0.7 slice_bitcast_fusion
  652.1 2.0 copy.81
  654.1 0.7 fusion.33
  656.0 1.9 copy.85
  657.9 0.8 copy.86
  (159 shorter events, 11.4 us)
Async XLA Ops:
  0.6 273.2 %copy-start = (bf16[1024,128]{1,0:T(8,128)(2,1)S(1)}, bf16[1024,128]{1,0:T(8,128)(2,1)}, u32[]{:S(2)}) copy-start(bf16[1024,128]{1,0:T(8,128)(2,1)} %param.28) | copy-start | bytes 786436
  46.0 2.6 copy-start.21
  48.6 24.4 %copy-start.6 = (bf16[1536,1024]{1,0:T(8,128)(2,1)}, bf16[1536,1024]{1,0:T(8,128)(2,1)S(1)}, u32[]{:S(2)}) copy-start(bf16[1536,1024]{1,0:T(8,128)(2,1)S(1)} %get-tuple-element.40.window_ref.window) | copy-start | bytes 9437188
  56.7 16.3 %copy-start.14 = (f32[1536,128]{1,0:T(8,128)}, f32[1536,128]{1,0:T(8,128)S(1)}, u32[]{:S(2)}) copy-start(f32[1536,128]{1,0:T(8,128)S(1)} %get-tuple-element.171.cos_ref) | copy-start | bytes 2359300
  56.7 16.3 %copy-start.16 = (f32[1536,128]{1,0:T(8,128)}, f32[1536,128]{1,0:T(8,128)S(1)}, u32[]{:S(2)}) copy-start(f32[1536,128]{1,0:T(8,128)S(1)} %get-tuple-element.172.sin_ref) | copy-start | bytes 2359300
  73.0 1.6 copy-start.23
  74.6 155.6 %copy-start.22 = (bf16[1536,1024]{1,0:T(8,128)(2,1)}, bf16[1536,1024]{1,0:T(8,128)(2,1)S(1)}, u32[]{:S(2)}) copy-start(bf16[1536,1024]{1,0:T(8,128)(2,1)S(1)} %get-tuple-element.44.key_ref) | copy-start | bytes 9437188
  74.6 155.6 %copy-start.27 = (bf16[512,1024]{1,0:T(8,128)(2,1)}, bf16[512,1024]{1,0:T(8,128)(2,1)S(1)}, u32[]{:S(2)}) copy-start(bf16[512,1024]{1,0:T(8,128)(2,1)S(1)} %get-tuple-element.43.query_ref) | copy-start | bytes 3145732
  74.6 51.6 %copy-start.7 = (bf16[1024,1024]{1,0:T(8,128)(2,1)S(1)}, bf16[1024,1024]{1,0:T(8,128)(2,1)}, u32[]{:S(2)}) copy-start(bf16[1024,1024]{1,0:T(8,128)(2,1)} %refs_1_.3) | copy-start | bytes 6291460
  74.6 51.6 %copy-start.8 = (bf16[1024,1024]{1,0:T(8,128)(2,1)S(1)}, bf16[1024,1024]{1,0:T(8,128)(2,1)}, u32[]{:S(2)}) copy-start(bf16[1024,1024]{1,0:T(8,128)(2,1)} %refs_2_.1) | copy-start | bytes 6291460
  74.6 51.6 %copy-start.18 = (bf16[256,1024]{1,0:T(8,128)(2,1)S(1)}, bf16[256,1024]{1,0:T(8,128)(2,1)}, u32[]{:S(2)}) copy-start(bf16[256,1024]{1,0:T(8,128)(2,1)} %refs_0_.1) | copy-start | bytes 1572868
  74.8 3.5 copy-start.24
  78.3 152.0 %copy-start.19 = (s32[8,1536]{1,0:T(8,128)}, s32[8,1536]{1,0:T(8,128)S(1)}, u32[]{:S(2)}) copy-start(s32[8,1536]{1,0:T(8,128)S(1)} %broadcast_in_dim.70.segk_ref) | copy-start | bytes 147460
  126.2 105.5 %copy-start.12 = (bf16[512,1024]{1,0:T(8,128)(2,1)}, bf16[512,1024]{1,0:T(8,128)(2,1)S(1)}, u32[]{:S(2)}) copy-start(bf16[512,1024]{1,0:T(8,128)(2,1)S(1)} %get-tuple-element.46.mixed_ref.mixed) | copy-start | bytes 3145732
  126.2 105.5 %copy-start.25 = (f32[8,512,128]{2,1,0:T(8,128)}, f32[8,512,128]{2,1,0:T(8,128)S(1)}, u32[]{:S(2)}) copy-start(f32[8,512,128]{2,1,0:T(8,128)S(1)} %get-tuple-element.51.lse_ref) | copy-start | bytes 6291460
  126.2 104.1 %copy-start.11 = (bf16[512,1024]{1,0:T(8,128)(2,1)S(1)}, bf16[512,1024]{1,0:T(8,128)(2,1)}, u32[]{:S(2)}) copy-start(bf16[512,1024]{1,0:T(8,128)(2,1)} %refs_1_.2) | copy-start | bytes 3145732
  230.3 1.8 copy-start.40
  230.3 1.8 copy-start.45
  230.3 1.9 copy-start.41
  230.3 4.5 copy-start.47
  231.7 27.2 %copy-start.29 = (f32[512,1024]{1,0:T(8,128)}, f32[512,1024]{1,0:T(8,128)S(1)}, u32[]{:S(2)}) copy-start(f32[512,1024]{1,0:T(8,128)S(1)} %get-tuple-element.161) | copy-start | bytes 6291460
  232.2 26.7 %slice-start.2 = ((s8[8388608]{0:T(1024)(128)(4,1)}), s8[4194304]{0:T(1024)(128)(4,1)S(1)}, s32[]{:S(2)}) async-start(s8[8388608]{0:T(1024)(128)(4,1)} %bitcast.101), calls=%async_computation.2 | async-start | bytes 8388608
  232.6 26.3 %copy-start.33 = (bf16[512,1024]{1,0:T(8,128)(2,1)}, bf16[512,1024]{1,0:T(8,128)(2,1)S(1)}, u32[]{:S(2)}) copy-start(bf16[512,1024]{1,0:T(8,128)(2,1)S(1)} %fusion.17.normed) | copy-start | bytes 3145732
  234.9 24.0 %slice-start.3 = ((s8[8388608]{0:T(1024)(128)(4,1)}), s8[4194304]{0:T(1024)(128)(4,1)S(1)}, s32[]{:S(2)}) async-start(s8[8388608]{0:T(1024)(128)(4,1)} %bitcast.101), calls=%async_computation.3 | async-start | bytes 8388608
  258.9 6.1 copy-start.34
  265.0 28.2 %copy-start.46 = (s32[1,8]{1,0:T(1,128)S(1)}, s32[1,8]{1,0:T(1,128)}, u32[]{:S(2)}) copy-start(s32[1,8]{1,0:T(1,128)} %param.17) | copy-start | bytes 100
  349.7 14.4 %copy-start.31 = (bf16[512,1024]{1,0:T(8,128)(2,1)}, bf16[512,1024]{1,0:T(8,128)(2,1)S(1)}, u32[]{:S(2)}) copy-start(bf16[512,1024]{1,0:T(8,128)(2,1)S(1)} %get-tuple-element.138.ffn_grad) | copy-start | bytes 3145732
  349.7 14.4 %copy-start.30 = (f32[512,1024]{1,0:T(8,128)S(1)}, f32[512,1024]{1,0:T(8,128)}, u32[]{:S(2)}) copy-start(f32[512,1024]{1,0:T(8,128)} %copy-done.29) | copy-start | bytes 6291460
  364.1 11.2 %copy-start.35 = (bf16[512,4096]{1,0:T(8,128)(2,1)}, bf16[512,4096]{1,0:T(8,128)(2,1)S(1)}, u32[]{:S(2)}) copy-start(bf16[512,4096]{1,0:T(8,128)(2,1)S(1)} %get-tuple-element.136.pre_grad) | copy-start | bytes 12582916
  377.4 1.8 copy-start.15
  377.4 2.1 copy-start.17
  377.4 2.1 copy-start.20
  377.4 2.8 copy-start.26
  377.4 3.0 copy-start.28
  377.4 56.3 %slice-start = ((s8[6291456]{0:T(1024)(128)(4,1)}), s8[4194304]{0:T(1024)(128)(4,1)S(1)}, s32[]{:S(2)}) async-start(s8[6291456]{0:T(1024)(128)(4,1)} %bitcast.80), calls=%async_computation | async-start | bytes 8388608
  380.4 53.3 %slice-start.1 = ((s8[6291456]{0:T(1024)(128)(4,1)}), s8[2097152]{0:T(1024)(128)(4,1)S(1)}, s32[]{:S(2)}) async-start(s8[6291456]{0:T(1024)(128)(4,1)} %bitcast.80), calls=%async_computation.1 | async-start | bytes 4194304
  433.7 9.8 %copy-start.4 = (bf16[512,1024]{1,0:T(8,128)(2,1)}, bf16[512,1024]{1,0:T(8,128)(2,1)S(1)}, u32[]{:S(2)}) copy-start(bf16[512,1024]{1,0:T(8,128)(2,1)S(1)} %get-tuple-element.52.dq) | copy-start | bytes 3145732
  433.7 10.0 %copy-start.2 = (bf16[1536,1024]{1,0:T(8,128)(2,1)}, bf16[1536,1024]{1,0:T(8,128)(2,1)S(1)}, u32[]{:S(2)}) copy-start(bf16[1536,1024]{1,0:T(8,128)(2,1)S(1)} %get-tuple-element.53.dk) | copy-start | bytes 9437188
  433.7 10.6 %copy-start.3 = (bf16[1536,1024]{1,0:T(8,128)(2,1)}, bf16[1536,1024]{1,0:T(8,128)(2,1)S(1)}, u32[]{:S(2)}) copy-start(bf16[1536,1024]{1,0:T(8,128)(2,1)S(1)} %get-tuple-element.54.dv) | copy-start | bytes 9437188
  443.5 3.8 copy-start.39
  443.5 3.8 copy-start.42
  443.5 3.8 copy-start.43
  443.5 3.8 copy-start.44
  450.4 189.1 %copy-start.5 = (bf16[512,1024]{1,0:T(8,128)(2,1)S(1)}, bf16[512,1024]{1,0:T(8,128)(2,1)}, u32[]{:S(2)}) copy-start(bf16[512,1024]{1,0:T(8,128)(2,1)} %copy-done.4) | copy-start | bytes 3145732
  450.5 189.1 %copy-start.36 = (f32[512,1024]{1,0:T(8,128)S(1)}, f32[512,1024]{1,0:T(8,128)}, u32[]{:S(2)}) copy-start(f32[512,1024]{1,0:T(8,128)} %get-tuple-element.142) | copy-start | bytes 6291460
  639.5 9.2 %copy-start.38 = (f32[128,256]{1,0:T(8,128)S(1)}, f32[128,256]{1,0:T(8,128)}, u32[]{:S(2)}) copy-start(f32[128,256]{1,0:T(8,128)} %get-tuple-element.61) | copy-start | bytes 393220
  639.5 19.2 %copy-start.1 = (bf16[1024,128]{1,0:T(8,128)(2,1)S(1)}, bf16[1024,128]{1,0:T(8,128)(2,1)}, u32[]{:S(2)}) copy-start(bf16[1024,128]{1,0:T(8,128)(2,1)} %param.28) | copy-start | bytes 786436
  645.2 12.7 %copy-start.37 = (f32[1024,128]{1,0:T(8,128)S(1)}, f32[1024,128]{1,0:T(8,128)}, u32[]{:S(2)}) copy-start(f32[1024,128]{1,0:T(8,128)} %get-tuple-element.201) | copy-start | bytes 1572868
  (4 other events, 5.6 us)

commit v2 on v1

v2 whole, which is shorter than its diff:
```python
from functools import partial
import math

import jax
import jax.numpy as jnp
from jax import lax
from jax.experimental import pallas as pl
from jax.experimental.pallas import tpu as pltpu
from jax.sharding import PartitionSpec as P

HDIM = 64
EMB = 128
SEQ = 2048
SEGS = 16
NQ = 8
MESH = pl.DeviceIdType.MESH
ANY = pl.ANY
F32 = jnp.float32
BF = jnp.bfloat16
eps_norm = 1e-05
eps_unit = 1e-06
VMEM_BIG = 60 * 1024 * 1024


def dot(left, right, left_dim=1, right_dim=0, precision=None):
    return lax.dot_general(
        left,
        right,
        (((left_dim,), (right_dim,)), ((), ())),
        preferred_element_type=F32,
        precision=precision,
    )


def hbm_specs(count):
    return [pl.BlockSpec(memory_space=ANY)] * count


def vmem_specs(count):
    return [pl.BlockSpec(memory_space=pltpu.VMEM)] * count


def rotate_lanes(values, cosine, sine):
    out = []
    front = lax.rem(lax.broadcasted_iota(jnp.int32, (1, 128), 1), 64) < 32
    for start in range(0, values.shape[1], 128):
        part = values[:, start : start + 128]
        partner = jnp.where(front, pltpu.roll(part, 96, 1), pltpu.roll(part, 32, 1))
        out.append(part * cosine + partner * sine)
    return out[0] if len(out) == 1 else jnp.concatenate(out, axis=1)


FWD_ROWS = 128
BACK_ROWS = 256
BK = 256
FWD_GROUPS = 8
BACK_GROUPS = 4
SCALE = HDIM**-0.5


def split_pair(values, dim=1):
    shape = (1, 128) if dim == 1 else (128, 1)
    first = lax.broadcasted_iota(jnp.int32, shape, dim) < 64
    zero = jnp.zeros_like(values)
    return jnp.where(first, values, zero), jnp.where(first, zero, values)


def turn(values):
    return values.astype(F32).T.astype(BF)


def attend_kernel(bounds_ref, query_ref, key_ref, turned_ref, segq_ref, segk_ref, mixed_ref, lse_ref):
    first = lax.broadcasted_iota(jnp.int32, (128, 1), 0) < 64
    one = jnp.ones((), BF)
    groups = range(0, query_ref.shape[1], 128)
    for block in range(query_ref.shape[0] // FWD_ROWS):
        rows = pl.ds(block * FWD_ROWS, FWD_ROWS)
        queries = [split_pair(turn(query_ref[rows, at : at + 128] * jnp.asarray(SCALE, BF)), 0) for at in groups]
        seg_q = segq_ref[0:1, rows]

        def body(index, carry):
            keys_at = pl.ds(pl.multiple_of(index * BK, BK), BK)
            live = segk_ref[keys_at, 0:1] == seg_q
            made = []
            for group, at in enumerate(groups):
                keys = key_ref[keys_at, at : at + 128]
                values = turned_ref[at : at + 128, keys_at]
                weights = (jnp.where(first, values, one), jnp.where(first, one, values))
                for head in range(2):
                    top, acc = carry[2 * group + head]
                    scores = jnp.where(live, dot(keys, queries[group][head]), -1e9)
                    new_top = jnp.maximum(top, jnp.max(scores, axis=0, keepdims=True))
                    probs = jnp.exp(scores - new_top).astype(BF)
                    acc = acc * jnp.exp(top - new_top) + dot(weights[head], probs)
                    made.append((new_top, acc))
            return tuple(made)

        start = tuple((jnp.full((1, FWD_ROWS), -2e9, F32), jnp.zeros((128, FWD_ROWS), F32)) for _ in range(2 * len(groups)))
        done = lax.fori_loop(bounds_ref[block, 0], bounds_ref[block, 1], body, start)
        for group, at in enumerate(groups):
            (top0, acc0), (top1, acc1) = done[2 * group : 2 * group + 2]
            total0, total1 = acc0[64:65], acc1[0:1]
            mixed = jnp.concatenate([acc0[0:64] / total0, acc1[64:128] / total1], axis=0)
            mixed_ref[rows, at : at + 128] = mixed.T.astype(BF)
            lse_ref[2 * group : 2 * group + 1, rows] = top0 + jnp.log(total0)
            lse_ref[2 * group + 1 : 2 * group + 2, rows] = top1 + jnp.log(total1)


def attend(bounds, queries, keys, turned, seg_q, seg_k):
    local, width = queries.shape
    long = keys.shape[0]
    lanes = FWD_GROUPS * 128
    return pl.pallas_call(
        attend_kernel,
        grid_spec=pltpu.PrefetchScalarGridSpec(
            num_scalar_prefetch=1,
            grid=(width // lanes,),
            in_specs=[
                pl.BlockSpec((local, lanes), lambda g, b: (0, g)),
                pl.BlockSpec((long, lanes), lambda g, b: (0, g)),
                pl.BlockSpec((lanes, long), lambda g, b: (g, 0)),
                pl.BlockSpec((8, local), lambda g, b: (0, 0)),
                pl.BlockSpec((long, 128), lambda g, b: (0, 0)),
            ],
            out_specs=[
                pl.BlockSpec((local, lanes), lambda g, b: (0, g)),
                pl.BlockSpec((2 * FWD_GROUPS, local), lambda g, b: (g, 0)),
            ],
        ),
        out_shape=[
            jax.ShapeDtypeStruct((local, width), BF),
            jax.ShapeDtypeStruct((width // HDIM, local), F32),
        ],
        compiler_params=pltpu.CompilerParams(vmem_limit_bytes=40 * 2**20),
        cost_estimate=pl.CostEstimate(flops=2 * 2**30, bytes_accessed=8 * 2**20, transcendentals=4 * 2**20),
    )(bounds, queries, keys, turned, seg_q, seg_k)


def attend_back_kernel(
    bounds_ref, query_ref, key_ref, turned_ref, value_ref, mixed_ref, grad_ref, lse_ref, segq_ref, segk_ref,
    cos_ref, sin_ref, dq_ref, dk_ref, dv_ref, dk_acc, dv_acc,
):
    local = query_ref.shape[0]
    groups = range(0, query_ref.shape[1], 128)
    dk_acc[...] = jnp.zeros_like(dk_acc)
    dv_acc[...] = jnp.zeros_like(dv_acc)
    head_row = lax.broadcasted_iota(jnp.int32, (8, 128), 0)
    head_lane = lax.broadcasted_iota(jnp.int32, (8, 128), 1) // 64
    chosen = jnp.where(head_row == head_lane, 1.0, 0.0)
    for block in range(local // BACK_ROWS):
        rows = pl.ds(block * BACK_ROWS, BACK_ROWS)
        queries, grads, turned_q, turned_g, deltas, logs = [], [], [], [], [], []
        for group, at in enumerate(groups):
            lanes = slice(at, at + 128)
            queries.append(split_pair(query_ref[rows, lanes] * jnp.asarray(SCALE, BF)))
            grads.append(split_pair(grad_ref[rows, lanes]))
            turned_q.append(split_pair(turn(query_ref[rows, lanes] * jnp.asarray(SCALE, BF)), 0))
            turned_g.append(split_pair(turn(grad_ref[rows, lanes]), 0))
            product = mixed_ref[rows, lanes].astype(F32) * grad_ref[rows, lanes].astype(F32)
            delta = dot(chosen, product, 1, 1, lax.Precision.HIGHEST)
            deltas.append((delta[0:1], delta[1:2]))
            logs.append((lse_ref[2 * group : 2 * group + 1, rows], lse_ref[2 * group + 1 : 2 * group + 2, rows]))
        seg_q = segq_ref[0:1, rows]

        def body(index, carry):
            keys_at = pl.ds(pl.multiple_of(index * BK, BK), BK)
            live = segk_ref[keys_at, 0:1] == seg_q
            made = []
            for group, at in enumerate(groups):
                lanes = slice(at, at + 128)
                keys = key_ref[keys_at, lanes]
                values = value_ref[keys_at, lanes]
                turned = turned_ref[lanes, keys_at]
                dk, dv = 0.0, 0.0
                for head in range(2):
                    scores = jnp.where(live, dot(keys, turned_q[group][head]), -1e9)
                    probs = jnp.exp(scores - logs[group][head])
                    score_low = (probs * (dot(values, turned_g[group][head]) - deltas[group][head])).astype(BF)
                    made.append(carry[2 * group + head] + dot(turned, score_low))
                    dk = dk + dot(score_low, queries[group][head])
                    dv = dv + dot(probs.astype(BF), grads[group][head])
                dk_acc[keys_at, lanes] += dk
                dv_acc[keys_at, lanes] += dv
            return tuple(made)

        start = (jnp.zeros((128, BACK_ROWS), F32),) * (2 * len(groups))
        done = lax.fori_loop(bounds_ref[block, 0], bounds_ref[block, 1], body, start)
        at_window = pl.ds(local + block * BACK_ROWS, BACK_ROWS)
        for group, at in enumerate(groups):
            grad = jnp.concatenate([done[2 * group][0:64], done[2 * group + 1][64:128]], axis=0).T * SCALE
            back = rotate_lanes(grad, cos_ref[at_window, :], -sin_ref[at_window, :])
            dq_ref[rows, at : at + 128] = back.astype(BF)
    dk_ref[...] = rotate_lanes(dk_acc[...], cos_ref[...], -sin_ref[...]).astype(BF)
    dv_ref[...] = dv_acc[...].astype(BF)


def attend_back(bounds, queries, keys, turned, values, mixed, grad, lse, seg_q, seg_k, cosine, sine):
    local, width = queries.shape
    long = keys.shape[0]
    lanes = BACK_GROUPS * 128
    short_spec = pl.BlockSpec((local, lanes), lambda g, b: (0, g))
    long_spec = pl.BlockSpec((long, lanes), lambda g, b: (0, g))
    return pl.pallas_call(
        attend_back_kernel,
        grid_spec=pltpu.PrefetchScalarGridSpec(
            num_scalar_prefetch=1,
            grid=(width // lanes,),
            in_specs=[
                short_spec,
                long_spec,
                pl.BlockSpec((lanes, long), lambda g, b: (g, 0)),
                long_spec,
                short_spec,
                short_spec,
                pl.BlockSpec((2 * BACK_GROUPS, local), lambda g, b: (g, 0)),
                pl.BlockSpec((8, local), lambda g, b: (0, 0)),
                pl.BlockSpec((long, 128), lambda g, b: (0, 0)),
                pl.BlockSpec((long, 128), lambda g, b: (0, 0)),
                pl.BlockSpec((long, 128), lambda g, b: (0, 0)),
            ],
            out_specs=[short_spec, long_spec, long_spec],
            scratch_shapes=[pltpu.VMEM((long, lanes), F32)] * 2,
        ),
        out_shape=[
            jax.ShapeDtypeStruct((local, width), BF),
            jax.ShapeDtypeStruct((long, width), BF),
            jax.ShapeDtypeStruct((long, width), BF),
        ],
        compiler_params=pltpu.CompilerParams(vmem_limit_bytes=48 * 2**20),
        cost_estimate=pl.CostEstimate(flops=5 * 2**30, bytes_accessed=16 * 2**20, transcendentals=4 * 2**20),
    )(bounds, queries, keys, turned, values, mixed, grad, lse, seg_q, seg_k, cosine, sine)


CB = 512
HIGH = lax.Precision.HIGHEST


def halves(values):
    high = values.astype(BF)
    return high, (values - high.astype(F32)).astype(BF)


def contrast_kernel(
    info_ref, emb_ref, segc_ref, segr_ref, counts_ref, positive_ref, temp_ref, grad_ref, loss_ref, tgrad_ref,
    unit, docs, docs_t, marks, marks_row, ratio, ratio_t, weights,
):
    own0, query_blocks, doc0 = info_ref[0], info_ref[1], info_ref[2]
    blocks = emb_ref.shape[0] // CB
    own_blocks = grad_ref.shape[0] // CB
    lane = lax.broadcasted_iota(jnp.int32, (1, 128), 1)
    widths = (EMB, EMB * 3 // 4, EMB // 2)
    loss_scale = temp_ref[0:1, 1:2]
    temp_inv = jnp.exp(-temp_ref[0:1, 0:1])
    segs = segc_ref[...]
    docs[...] = jnp.where((segs - NQ == lane) | ((segs == lane) & (lane >= NQ)), 1.0, 0.0).astype(BF)
    marks[...] = jnp.where((segs == lane) & (lane < NQ), 1.0, 0.0)
    down = lax.broadcasted_iota(jnp.int32, (128, 1), 0)
    across = segr_ref[0:1, :]
    docs_t[...] = jnp.where((across - NQ == down) | ((across == down) & (down >= NQ)), 1.0, 0.0).astype(BF)
    marks_row[...] = jnp.where(segr_ref[...] == lax.broadcasted_iota(jnp.int32, (NQ, 1), 0), 1.0, 0.0)
    for index, prefix in enumerate(widths):
        emb = jnp.where(lane < prefix, emb_ref[...].astype(F32), 0.0)
        unit[index] = (emb * lax.rsqrt(jnp.sum(emb * emb, axis=1, keepdims=True) + eps_unit)).astype(BF)

    def at(index):
        return pl.ds(pl.multiple_of(index * CB, CB), CB)

    def similar(index, rows, columns):
        return jnp.exp(10.0 * dot(unit[index, at(rows), :], unit[index, at(columns), :], 1, 1) - 10.0)

    def total_rows(row, seg_sums):
        def total_cols(column, totals):
            mask = docs[at(column), :]
            made = []
            for index in range(3):
                high, low = halves(similar(index, row, column))
                made.append(totals[index] + dot(high, mask) + dot(low, mask))
            return tuple(made)

        totals = lax.fori_loop(doc0, blocks, total_cols, (jnp.zeros((CB, 128), F32),) * 3)
        made = []
        for index in range(3):
            total = jnp.where(lane < NQ, totals[index], 1.0)
            ratio[index, at(row), :] = 1.0 / total
            smooth = jnp.log(total) / 10.0 + 1.0
            made.append(seg_sums[index] + dot(marks_row[:, at(row)], smooth, 1, 0, HIGH))
        return tuple(made)

    seg_sums = lax.fori_loop(0, query_blocks, total_rows, (jnp.zeros((NQ, 128), F32),) * 3)
    valid = lax.broadcasted_iota(jnp.int32, (NQ, 128), 1) < NQ
    inv_counts = 1.0 / counts_ref[0:NQ, :]
    positive = positive_ref[...]
    loss = jnp.zeros((1, 1), F32)
    tgrad = jnp.zeros((1, 1), F32)
    weights[...] = jnp.zeros_like(weights)
    for index in range(3):
        logits = jnp.where(valid, seg_sums[index] * inv_counts * temp_inv, 0.0)
        top = jnp.max(jnp.where(valid, logits, -1e30), axis=1, keepdims=True)
        powers = jnp.where(valid, jnp.exp(logits - top), 0.0)
        power_sum = jnp.sum(powers, axis=1, keepdims=True)
        term = jnp.log(power_sum) + top - jnp.sum(logits * positive, axis=1, keepdims=True)
        loss = loss + jnp.sum(term, axis=0, keepdims=True) * loss_scale
        dlogits = (powers / power_sum - positive) * loss_scale
        tgrad = tgrad - jnp.sum(jnp.sum(dlogits * logits, axis=1, keepdims=True), axis=0, keepdims=True)
        weights[index, 0:NQ, :] = dlogits * temp_inv * inv_counts

    def weigh(row, unused):
        for index in range(3):
            weight = dot(marks[at(row), :], weights[index], 1, 0, HIGH) * ratio[index, at(row), :]
            weight = jnp.where(lane < NQ, weight, 0.0)
            high = weight.astype(BF).astype(F32)
            both = high + pltpu.roll(weight - high, NQ, 1)
            ratio[index, at(row), :] = both
            ratio_t[index, :, at(row)] = both.T.astype(BF)
        return unused

    lax.fori_loop(0, query_blocks, weigh, 0)

    for own in range(own_blocks):
        mine = own0 + own

        def as_query(column, grads):
            mask = docs_t[:, at(column)]
            made = []
            for index in range(3):
                spread = dot(ratio[index, at(mine), :].astype(BF), mask)
                sim_grad = (similar(index, mine, column) * spread).astype(BF)
                made.append(grads[index] + dot(sim_grad, unit[index, at(column), :]))
            return tuple(made)

        def as_doc(row, grads):
            mask = docs[at(mine), :]
            made = []
            for index in range(3):
                spread = dot(mask, ratio_t[index, :, at(row)])
                sim_grad = (similar(index, mine, row) * spread).astype(BF)
                made.append(grads[index] + dot(sim_grad, unit[index, at(row), :]))
            return tuple(made)

        grads = (jnp.zeros((CB, 128), F32),) * 3
        grads = lax.fori_loop(doc0, jnp.where(mine < query_blocks, blocks, doc0), as_query, grads)
        grads = lax.fori_loop(0, jnp.where(mine >= doc0, query_blocks, 0), as_doc, grads)
        total = jnp.zeros((CB, 128), F32)
        for index, prefix in enumerate(widths):
            part = jnp.where(lane < prefix, emb_ref[at(mine), :].astype(F32), 0.0)
            scale = lax.rsqrt(jnp.sum(part * part, axis=1, keepdims=True) + eps_unit)
            full = part * scale
            back = scale * (grads[index] - full * jnp.sum(full * grads[index], axis=1, keepdims=True))
            total = total + jnp.where(lane < prefix, back, 0.0)
        grad_ref[pl.ds(own * CB, CB), :] = total.astype(BF)
    loss_ref[...] = jnp.broadcast_to(loss, loss_ref.shape)
    tgrad_ref[...] = jnp.broadcast_to(tgrad, tgrad_ref.shape)


def contrast(info, emb_all, seg_col, seg_row, counts, positive, temp_row, local):
    rows = emb_all.shape[0]
    return pl.pallas_call(
        contrast_kernel,
        in_specs=[pl.BlockSpec(memory_space=pltpu.SMEM)] + vmem_specs(6),
        out_specs=vmem_specs(3),
        out_shape=[
            jax.ShapeDtypeStruct((local, 128), BF),
            jax.ShapeDtypeStruct((8, 128), F32),
            jax.ShapeDtypeStruct((8, 128), F32),
        ],
        scratch_shapes=[
            pltpu.VMEM((3, rows, 128), BF),
            pltpu.VMEM((rows, 128), BF),
            pltpu.VMEM((128, rows), BF),
            pltpu.VMEM((rows, 128), F32),
            pltpu.VMEM((NQ, rows), F32),
            pltpu.VMEM((3, rows, 128), F32),
            pltpu.VMEM((3, 128, rows), BF),
            pltpu.VMEM((3, 128, 128), F32),
        ],
        compiler_params=pltpu.CompilerParams(vmem_limit_bytes=40 * 2**20),
        cost_estimate=pl.CostEstimate(flops=2**30, bytes_accessed=2**22, transcendentals=2**22),
    )(info, emb_all, seg_col, seg_row, counts, positive, temp_row)


CW = 512
SLOTS_G, SLOTS_S, SLOTS_R, SLOTS_T, SLOTS_K = 3, 3, 4, 6, 14
SMALL_ROWS = 112
LAGS = (4, 7, 2)


def neighbours():
    dp = lax.axis_index("dp")
    low = lax.rem(dp, 8)
    core = lax.rem(low, 2)
    x = lax.rem(low // 2, 2)
    y = low // 4
    return dp, low, core, x, y, dp + 1 - 2 * core, dp + 2 - 4 * x, dp + 4 - 8 * y


def entry_barrier(z, dp, plane, z_count):
    barrier = pltpu.get_barrier_semaphore()
    for other in plane:
        pl.semaphore_signal(barrier, inc=1, device_id={"dp": other, "tensor": z}, device_id_type=MESH)
    for step in range(1, z_count):
        peer = lax.rem(z + step, z_count)
        pl.semaphore_signal(barrier, inc=1, device_id={"dp": dp, "tensor": peer}, device_id_type=MESH)
    pl.semaphore_wait(barrier, len(plane) + z_count - 1)


def remote(src, dst, send_sem, recv_sem, dp, z):
    return pltpu.make_async_remote_copy(
        src_ref=src,
        dst_ref=dst,
        send_sem=send_sem,
        recv_sem=recv_sem,
        device_id={"dp": dp, "tensor": z},
        device_id_type=MESH,
    )


def scatter_kernel(
    window, attn_grad, normed, ffn_grad, dq, dk, dv, mixed, pre_grad, hidden, dxw, small_ref,
    out_qkv, out_attn, out_in, out_out, small_out, from_left, from_right,
    xw, xa, xn, xf, gs, gkv, sbuf, rbuf, ta, tb, xra, xrb, s2a, s2b, yra, yrb, keep, zs, zrl, zrr,
    sacc, srec, zsm,
    x_sem, g_sem, s_sem, r_sem, t_sem, xr_sem, s2_sem, yr_sem, zs_sem, zr_sem, sm_sem, smz_sem, h_sem, credit,
):
    dp, low, core, x, y, to_core, to_x, to_y = neighbours()
    z = lax.axis_index("tensor")
    nz = 4
    chunks = [("out", i) for i in range(8)] + [("in", i) for i in range(8)] + [("qa", i) for i in range(8)]
    count = len(chunks)
    local = attn_grad.shape[0]
    has_l = z > 0
    has_r = z < nz - 1

    x_loads = [
        pltpu.make_async_copy(src, dst, x_sem.at[index])
        for index, (src, dst) in enumerate(((ffn_grad, xf), (normed, xn), (window, xw), (attn_grad, xa)))
    ]
    for load in x_loads:
        load.start()

    def g_loads(index):
        kind, part = chunks[index]
        slot = index % SLOTS_G
        if kind != "qa":
            source = hidden if kind == "out" else pre_grad
            return [pltpu.make_async_copy(source.at[:, pl.ds(part * CW, CW)], gs.at[slot], g_sem.at[slot, 0])]
        columns = pl.ds((part // 2) * 256, 256)
        one, many = (dq, dk) if part % 2 == 0 else (mixed, dv)
        return [
            pltpu.make_async_copy(one.at[:, columns], gs.at[slot, :, pl.ds(0, 256)], g_sem.at[slot, 0]),
            pltpu.make_async_copy(many.at[:, columns], gkv.at[slot], g_sem.at[slot, 1]),
        ]

    for index in range(2):
        for load in g_loads(index):
            load.start()

    entry_barrier(z, dp, (to_core, to_x, to_y), nz)

    halo_l = remote(dxw.at[pl.ds(0, local)], from_right, h_sem.at[0], h_sem.at[1], dp, z - 1)
    halo_r = remote(dxw.at[pl.ds(2 * local, local)], from_left, h_sem.at[2], h_sem.at[3], dp, z + 1)

    peers = (to_core, to_x, to_y)

    def small_moves(stage):
        return [
            remote(sacc.at[stage], srec.at[stage], sm_sem.at[stage, 0], sm_sem.at[stage, 1], peers[stage], z),
        ]

    def small_z_moves(step):
        peer = lax.rem(z + step, nz)
        return [
            remote(sacc.at[3], zsm.at[step - 1], smz_sem.at[step - 1, 0], smz_sem.at[step - 1, 1], dp, peer),
        ]

    def small_stage(stage):
        if stage == 0:
            sacc[0] = small_ref[...]
        if 1 <= stage <= 3:
            for move in small_moves(stage - 1):
                move.wait_recv()
            sacc[stage] = sacc[stage - 1] + srec[stage - 1]
        if stage <= 2:
            for move in small_moves(stage):
                move.start()
        if stage == 3:
            for step in range(1, nz):
                for move in small_z_moves(step):
                    move.start()
        if stage == 4:
            for step in range(1, nz):
                for move in small_z_moves(step):
                    move.wait_recv()
            total = None
            for owner in range(nz):
                value = jnp.where(z == owner, sacc[3], 0.0)
                for step in range(1, nz):
                    value = jnp.where(lax.rem(z - step + nz, nz) == owner, zsm[step - 1], value)
                total = value if total is None else total + value
            small_out[...] = total

    def block_columns(j, core_bit):
        xj = lax.rem(j, 2)
        yj = j // 2
        block = core_bit + 2 * (x + xj - 2 * x * xj) + 4 * (y + yj - 2 * y * yj)
        return pl.ds(pl.multiple_of(block * 128, 128), 128)

    def product(index, j, core_bit):
        kind, part = chunks[index]
        slot = index % SLOTS_G
        at = block_columns(j, core_bit)
        if kind == "out":
            return dot(xf[:, at], gs[slot], 0, 0)
        if kind == "in":
            return dot(xn[:, at], gs[slot], 0, 0)
        one = xw[pl.ds(local, local), at] if part % 2 == 0 else xa[:, at]
        return jnp.concatenate(
            [dot(one, gs[slot, :, 0:256], 0, 0), dot(xw[:, at], gkv[slot], 0, 0)], axis=1
        )

    def core_move(index):
        return remote(
            sbuf.at[index % SLOTS_S], rbuf.at[index % SLOTS_R], s_sem.at[index % SLOTS_S], r_sem.at[index % SLOTS_R],
            to_core, z,
        )

    half = CW // 2

    def ta_move(index):
        slot = index % SLOTS_T
        return remote(ta.at[slot, pl.ds(2, 2)], xra.at[index], t_sem.at[slot, 0], xr_sem.at[index, 0], to_x, z)

    def tb_move(index):
        slot = index % SLOTS_T
        return remote(tb.at[slot, pl.ds(2, 2)], xrb.at[index], t_sem.at[slot, 1], xr_sem.at[index, 1], to_y, z)

    def s2a_move(index):
        return remote(s2a.at[index], yra.at[index], s2_sem.at[index, 0], yr_sem.at[index, 0], to_y, z)

    def s2b_move(index):
        return remote(s2b.at[index], yrb.at[index], s2_sem.at[index, 1], yr_sem.at[index, 1], to_x, z)

    def right_move(index):
        return remote(zs.at[index], zrl.at[index], zs_sem.at[index], zr_sem.at[index, 0], dp, z + 1)

    def left_move(index):
        return remote(zs.at[index], zrr.at[index], zs_sem.at[index], zr_sem.at[index, 1], dp, z - 1)

    def stage_one(index):
        kind, part = chunks[index]
        if index == 0:
            x_loads[0].wait()
        if kind == "in" and part == 0:
            x_loads[1].wait()
        if kind == "qa" and part == 0:
            x_loads[2].wait()
            x_loads[3].wait()
        for load in g_loads(index):
            load.wait()
        if index >= SLOTS_S:
            core_move(index - SLOTS_S).wait_send()

        def body(j, unused):
            sbuf[index % SLOTS_S, j] = product(index, j, 1 - core).astype(BF)
            return unused

        lax.fori_loop(0, 4, body, 0)
        if index >= SLOTS_R:
            pl.semaphore_wait(credit, 1)
        core_move(index).start()

    def stage_two(index):
        core_move(index).wait_recv()
        slot = index % SLOTS_T
        if index >= SLOTS_T:
            ta_move(index - SLOTS_T).wait_send()
            tb_move(index - SLOTS_T).wait_send()

        def body(j, unused):
            total = product(index, j, core) + rbuf[index % SLOTS_R, j].astype(F32)
            ta[slot, j // 2 + 2 * lax.rem(j, 2)] = total[:, :half].astype(BF)
            tb[slot, j] = total[:, half:].astype(BF)
            return unused

        lax.fori_loop(0, 4, body, 0)
        if index + SLOTS_R < count:
            pl.semaphore_signal(credit, inc=1, device_id={"dp": to_core, "tensor": z}, device_id_type=MESH)
        ta_move(index).start()
        tb_move(index).start()

    def stage_three(index):
        slot = index % SLOTS_T
        kslot = index % SLOTS_K
        ta_move(index).wait_recv()
        s2a[index] = (ta[slot, 1].astype(F32) + xra[index, 1].astype(F32)).astype(BF)
        s2a_move(index).start()
        keep[kslot, :, :half] = ta[slot, 0].astype(F32) + xra[index, 0].astype(F32)
        tb_move(index).wait_recv()
        s2b[index] = (tb[slot, 1].astype(F32) + xrb[index, 1].astype(F32)).astype(BF)
        s2b_move(index).start()
        keep[kslot, :, half:] = tb[slot, 0].astype(F32) + xrb[index, 0].astype(F32)

    def stage_four(index):
        kslot = index % SLOTS_K
        goal = chunks[index][1] // 2
        s2a_move(index).wait_recv()
        keep[kslot, :, :half] += yra[index].astype(F32)
        s2b_move(index).wait_recv()
        keep[kslot, :, half:] += yrb[index].astype(F32)
        if goal > 0:

            @pl.when(z == 0)
            def _():
                zs[index] = keep[kslot].astype(BF)
                right_move(index).start()

        if goal < nz - 1:

            @pl.when(z == nz - 1)
            def _():
                zs[index] = keep[kslot].astype(BF)
                left_move(index).start()

    def stage_five(index, hop):
        kslot = index % SLOTS_K
        kind, part = chunks[index]
        goal = part // 2
        if hop <= goal:

            @pl.when(z == hop)
            def _():
                right_move(index).wait_recv()
                keep[kslot] += zrl[index].astype(F32)
                if hop < goal:
                    zs[index] = keep[kslot].astype(BF)
                    right_move(index).start()

        if hop <= nz - 1 - goal:

            @pl.when(z == nz - 1 - hop)
            def _():
                left_move(index).wait_recv()
                keep[kslot] += zrr[index].astype(F32)
                if nz - 1 - hop > goal:
                    zs[index] = keep[kslot].astype(BF)
                    left_move(index).start()

        if hop == nz - 1:

            @pl.when(z == goal)
            def _():
                if kind == "qa":
                    if part % 2 == 0:
                        out_qkv[:, 0:512] = keep[kslot]
                    else:
                        out_attn[...] = keep[kslot, :, 0:256]
                        out_qkv[:, 512:768] = keep[kslot, :, 256:512]
                else:
                    target = out_in if kind == "in" else out_out
                    target[:, pl.ds((part % 2) * CW, CW)] = keep[kslot]

    lag_three, lag_four, spacing = LAGS
    for step in range(count + lag_four + spacing * (nz - 1) + 1):
        if step < count:
            stage_one(step)
        if step == 0:
            small_stage(0)
            pl.when(has_l)(lambda: halo_l.start())
            pl.when(has_r)(lambda: halo_r.start())
        if 0 <= step - 1 < count:
            stage_two(step - 1)
        if step + 2 < count:
            for load in g_loads(step + 2):
                load.start()
        if step in (2, 4, 6, 8):
            small_stage(step // 2)
        if 0 <= step - lag_three < count:
            stage_three(step - lag_three)
        if 0 <= step - lag_four < count:
            stage_four(step - lag_four)
        for hop in range(1, nz):
            index = step - lag_four - spacing * hop
            if 0 <= index < count:
                stage_five(index, hop)

    for index in range(count):
        goal = chunks[index][1] // 2
        if index >= count - SLOTS_S:
            core_move(index).wait_send()
        if index >= count - SLOTS_T:
            ta_move(index).wait_send()
            tb_move(index).wait_send()
        s2a_move(index).wait_send()
        s2b_move(index).wait_send()
        pl.when(z < goal)(lambda index=index: right_move(index).wait_send())
        pl.when(z > goal)(lambda index=index: left_move(index).wait_send())
    for stage in range(3):
        for move in small_moves(stage):
            move.wait_send()
    for step in range(1, nz):
        for move in small_z_moves(step):
            move.wait_send()

    @pl.when(has_l)
    def _():
        halo_l.wait_send()
        halo_r.wait_recv()

    @pl.when(has_r)
    def _():
        halo_r.wait_send()
        halo_l.wait_recv()


def scatter(window, attn_grad, normed, ffn_grad, dq, dk, dv, mixed, pre_grad, hidden, dxw, small):
    local, width = attn_grad.shape
    long = window.shape[0]
    dma = pltpu.SemaphoreType.DMA
    n = 24
    half = CW // 2
    shape = jax.ShapeDtypeStruct
    return pl.pallas_call(
        scatter_kernel,
        in_specs=hbm_specs(11) + vmem_specs(1),
        out_specs=vmem_specs(5) + hbm_specs(2),
        out_shape=[
            shape((128, 768), F32),
            shape((128, 256), F32),
            shape((128, 1024), F32),
            shape((128, 1024), F32),
            shape(small.shape, F32),
            shape((local, width), BF),
            shape((local, width), BF),
        ],
        scratch_shapes=[
            pltpu.VMEM((long, width), BF),
            pltpu.VMEM((local, width), BF),
            pltpu.VMEM((local, width), BF),
            pltpu.VMEM((local, width), BF),
            pltpu.VMEM((SLOTS_G, local, CW), BF),
            pltpu.VMEM((SLOTS_G, long, 256), BF),
            pltpu.VMEM((SLOTS_S, 4, 128, CW), BF),
            pltpu.VMEM((SLOTS_R, 4, 128, CW), BF),
            pltpu.VMEM((SLOTS_T, 4, 128, half), BF),
            pltpu.VMEM((SLOTS_T, 4, 128, half), BF),
            pltpu.VMEM((n, 2, 128, half), BF),
            pltpu.VMEM((n, 2, 128, half), BF),
            pltpu.VMEM((n, 128, half), BF),
            pltpu.VMEM((n, 128, half), BF),
            pltpu.VMEM((n, 128, half), BF),
            pltpu.VMEM((n, 128, half), BF),
            pltpu.VMEM((SLOTS_K, 128, CW), F32),
            pltpu.VMEM((n, 128, CW), BF),
            pltpu.VMEM((n, 128, CW), BF),
            pltpu.VMEM((n, 128, CW), BF),
            pltpu.VMEM((4,) + small.shape, F32),
            pltpu.VMEM((3,) + small.shape, F32),
            pltpu.VMEM((3,) + small.shape, F32),
            dma((4,)),
            dma((SLOTS_G, 2)),
            dma((SLOTS_S,)),
            dma((SLOTS_R,)),
            dma((SLOTS_T, 2)),
            dma((n, 2)),
            dma((n, 2)),
            dma((n, 2)),
            dma((n,)),
            dma((n, 2)),
            dma((3, 2)),
            dma((3, 2)),
            dma((4,)),
            pltpu.SemaphoreType.REGULAR,
        ],
        compiler_params=pltpu.CompilerParams(
            collective_id=2, has_side_effects=True, vmem_limit_bytes=VMEM_BIG
        ),
    )(window, attn_grad, normed, ffn_grad, dq, dk, dv, mixed, pre_grad, hidden, dxw, small)


def shard_rows(kind, ref):
    return ref.shape[1] if kind == "qkv" else (512 if kind in ("out0", "out1") else ref.shape[0])


def source_rows(kind, ref, start, rows):
    if kind == "qkv":
        return ref.at[:, pl.ds(start, rows), :]
    if kind == "out1":
        start = pl.multiple_of(start + 512, 16)
    return ref.at[pl.ds(start, rows), :]


def gathered_rows(kind, ref, shard, start, rows):
    if kind == "qkv":
        return ref.at[:, pl.ds(start, rows), pl.ds(pl.multiple_of(shard * 256, 256), 256)]
    if kind == "in":
        return ref.at[pl.ds(start, rows), pl.ds(pl.multiple_of(shard * 1024, 1024), 1024)]
    per = ref.shape[0] // 4
    if kind == "out1":
        start = start + 512
    return ref.at[pl.ds(pl.multiple_of(shard * per + start, 16), rows), :]


class Gather:
    def __init__(self, kinds, srcs, outs, z_send, z_recv, p_send, p_recv, lag):
        self.kinds, self.srcs, self.outs = kinds, srcs, outs
        self.z_send, self.z_recv, self.p_send, self.p_recv = z_send, z_recv, p_send, p_recv
        self.dp, low, core, x, y, self.to_core, self.to_x, self.to_y = neighbours()
        self.z = lax.axis_index("tensor")
        self.nz = 4
        self.has_l, self.has_r = self.z > 0, self.z < self.nz - 1
        low_x, low_y = low + 2 - 4 * x, low + 4 - 8 * y
        low_xy = low_x + 4 - 8 * y
        self.low = low
        self.places = {
            0: (low, None), 1: (low, None), 4: (low, None), 2: (low_x, 0), 3: (low_y, 1),
            5: (low_x, None), 6: (low_y, None), 7: (low_xy, 0), 8: (low_xy, 1),
        }
        self.events = [(m, distance, side) for m in range(len(kinds)) for distance in (1, 2, 3) for side in (0, 1)]
        self.lag = lag
        self.steps = len(self.events) + 2 * lag

    def barrier(self):
        entry_barrier(self.z, self.dp, (self.to_core, self.to_x, self.to_y), self.nz)

    def piece(self, m, shard, index, half=None):
        rows = shard_rows(self.kinds[m], self.srcs[m]) // 8
        start = index * rows
        if half is not None:
            rows = rows // 2
            start = start + half * rows
        return gathered_rows(self.kinds[m], self.outs[m], shard, pl.multiple_of(start, 16), rows)

    def shard_of(self, side, distance):
        return self.z - distance if side == 0 else self.z + distance

    def onward(self, side):
        return self.z + 1 if side == 0 else self.z - 1

    def can_send(self, side):
        return self.has_r if side == 0 else self.has_l

    def arrives(self, side, distance):
        return self.z >= distance if side == 0 else self.z + distance < self.nz

    def own_move(self, m, side):
        rows = shard_rows(self.kinds[m], self.srcs[m]) // 8
        src = source_rows(self.kinds[m], self.srcs[m], pl.multiple_of(self.low * rows, 16), rows)
        sems = self.z_send.at[m, side, 0], self.z_recv.at[m, side, 0]
        return remote(src, self.piece(m, self.z, self.low), *sems, self.dp, self.onward(side))

    def relay_move(self, m, side, distance):
        at = self.piece(m, self.shard_of(side, distance), self.low)
        sems = self.z_send.at[m, side, distance], self.z_recv.at[m, side, distance]
        return remote(at, at, *sems, self.dp, self.onward(side))

    def plane_move(self, m, side, distance, kind):
        ref = self.piece(m, self.shard_of(side, distance), *self.places[kind])
        to = {0: self.to_x, 1: self.to_y, 2: self.to_y, 3: self.to_x}.get(kind, self.to_core)
        slot = side * 3 + distance - 1
        return remote(ref, ref, self.p_send.at[m, slot, kind], self.p_recv.at[m, slot, kind], to, self.z)

    def own_start(self, m):
        for side in (0, 1):
            pl.when(self.can_send(side))(lambda side=side: self.own_move(m, side).start())

    def stage_z(self, m, distance, side):
        if side == 0 and distance == 2 and m + 1 < len(self.kinds):
            self.own_start(m + 1)

        @pl.when(self.arrives(side, distance))
        def _():
            if distance == 1:
                self.own_move(m, side).wait_recv()
            else:
                self.relay_move(m, side, distance - 1).wait_recv()
            if distance < 3:
                pl.when(self.can_send(side))(lambda: self.relay_move(m, side, distance).start())
            for kind in (0, 1, 4):
                self.plane_move(m, side, distance, kind).start()

    def stage_plane(self, m, distance, side, waits, shift):
        @pl.when(self.arrives(side, distance))
        def _():
            for kind in waits:
                self.plane_move(m, side, distance, kind).wait_recv()
                for more in shift:
                    self.plane_move(m, side, distance, kind + more).start()

    def step(self, step):
        count = len(self.events)
        if step < count:
            self.stage_z(*self.events[step])
        if 0 <= step - self.lag < count:
            self.stage_plane(*self.events[step - self.lag], (0, 1), (2, 5))
        if 0 <= step - 2 * self.lag < count:
            self.stage_plane(*self.events[step - 2 * self.lag], (2, 3), (5,))

    def arrived(self, m, distance, side):
        self.stage_plane(m, distance, side, (4, 5, 6, 7, 8), ())

    def arrived_all(self, m):
        for distance in (1, 2, 3):
            for side in (0, 1):
                self.arrived(m, distance, side)

    def drain(self):
        for m, distance, side in self.events:

            @pl.when(self.arrives(side, distance))
            def _():
                for kind in range(9):
                    self.plane_move(m, side, distance, kind).wait_send()
                if distance < 3:
                    pl.when(self.can_send(side))(lambda: self.relay_move(m, side, distance).wait_send())

        for m in range(len(self.kinds)):
            for side in (0, 1):
                pl.when(self.can_send(side))(lambda side=side: self.own_move(m, side).wait_send())


def gather_sems(n):
    dma = pltpu.SemaphoreType.DMA
    return [dma((n, 2, 3)), dma((n, 2, 3)), dma((n, 6, 9)), dma((n, 6, 9))]


def first_kernel(
    qkv_src, attn_src, in_src, tokens, bias, cos_ref, sin_ref,
    qkv_out, attn_out, in_out, window_out, bias_all, query_out, key_out, key_t_out, value_out, value_t_out,
    weight, xw, query, key, key_t, value, value_t, stage_a, stage_i,
    z_send, z_recv, p_send, p_recv, l_sem, h_sem, b_sem, o_sem,
):
    plan = Gather(
        ("qkv", "attn", "in"), (qkv_src, attn_src, in_src), (weight, attn_out, in_out), z_send, z_recv, p_send, p_recv, 4
    )
    z, dp, nz = plan.z, plan.dp, plan.nz
    local = tokens.shape[0]
    own_qkv = pltpu.make_async_copy(qkv_src, gathered_rows("qkv", weight, z, 0, qkv_src.shape[1]), l_sem.at[0])
    a_in = pltpu.make_async_copy(attn_src, stage_a, l_sem.at[1])
    i_in = pltpu.make_async_copy(in_src, stage_i, l_sem.at[2])
    a_out = pltpu.make_async_copy(stage_a, gathered_rows("attn", attn_out, z, 0, attn_src.shape[0]), l_sem.at[3])
    i_out = pltpu.make_async_copy(stage_i, gathered_rows("in", in_out, z, 0, in_src.shape[0]), l_sem.at[4])
    own_tokens = pltpu.make_async_copy(tokens, xw.at[pl.ds(local, local)], h_sem.at[4])
    fill_l = pltpu.make_async_copy(tokens, xw.at[pl.ds(0, local)], h_sem.at[5])
    fill_r = pltpu.make_async_copy(tokens, xw.at[pl.ds(2 * local, local)], h_sem.at[6])
    for copy in (own_qkv, a_in, i_in, own_tokens):
        copy.start()
    pl.when(jnp.logical_not(plan.has_l))(lambda: fill_l.start())
    pl.when(jnp.logical_not(plan.has_r))(lambda: fill_r.start())
    bias_all[pl.ds(z, 1)] = bias[...].reshape(1, *bias.shape)
    plan.barrier()
    to_left = remote(tokens, xw.at[pl.ds(2 * local, local)], h_sem.at[0], h_sem.at[1], dp, z - 1)
    to_right = remote(tokens, xw.at[pl.ds(0, local)], h_sem.at[2], h_sem.at[3], dp, z + 1)

    def bias_move(step):
        return remote(bias, bias_all.at[z], b_sem.at[0, step - 1], b_sem.at[1, step - 1], dp, lax.rem(z + step, nz))

    plan.own_start(0)
    for step in range(1, nz):
        bias_move(step).start()
    a_in.wait()
    a_out.start()
    i_in.wait()
    i_out.start()

    weight_out = pltpu.make_async_copy(weight, qkv_out, o_sem.at[0])
    window_copy = pltpu.make_async_copy(xw, window_out, o_sem.at[1])

    def outputs(shard):
        columns = pl.ds(shard * 256, 256)
        return [
            pltpu.make_async_copy(query.at[:, columns], query_out.at[:, columns], o_sem.at[2 + 5 * shard]),
            pltpu.make_async_copy(key.at[:, columns], key_out.at[:, columns], o_sem.at[3 + 5 * shard]),
            pltpu.make_async_copy(key_t.at[columns, :], key_t_out.at[columns, :], o_sem.at[4 + 5 * shard]),
            pltpu.make_async_copy(value.at[:, columns], value_out.at[:, columns], o_sem.at[5 + 5 * shard]),
            pltpu.make_async_copy(value_t.at[columns, :], value_t_out.at[columns, :], o_sem.at[6 + 5 * shard]),
        ]

    def ready():
        plan.arrived_all(0)
        own_qkv.wait()
        own_tokens.wait()
        weight_out.start()
        for step in range(1, nz):
            bias_move(step).wait_recv()

    def halo_ready():
        pl.when(plan.has_l)(lambda: to_right.wait_recv())
        pl.when(plan.has_r)(lambda: to_left.wait_recv())
        pl.when(jnp.logical_not(plan.has_l))(lambda: fill_l.wait())
        pl.when(jnp.logical_not(plan.has_r))(lambda: fill_r.wait())
        window_copy.start()

    def compute(shard, part):
        columns = slice(shard * 256, shard * 256 + 256)
        rows = slice(part * local, part * local + local)
        window = xw[rows, :]
        cosine, sine = cos_ref[rows, :], sin_ref[rows, :]

        def made(kind):
            add = [bias_all[shard, 2 * kind + i : 2 * kind + i + 1, :].astype(F32) for i in range(2)]
            return dot(window, weight[kind, :, columns]) + jnp.concatenate(add, axis=1)

        if part == 1:
            query[:, columns] = rotate_lanes(made(0), cosine, sine).astype(BF)
        keys = rotate_lanes(made(1), cosine, sine)
        key[rows, columns] = keys.astype(BF)
        key_t[columns, rows] = keys.T.astype(BF)
        values = made(2)
        value[rows, columns] = values.astype(BF)
        value_t[columns, rows] = values.T.astype(BF)

    pieces = [ready]
    pieces += [partial(compute, shard, 1) for shard in range(4)]
    pieces += [halo_ready]
    for shard in range(4):
        pieces += [partial(compute, shard, 0), partial(compute, shard, 2)]
        pieces += [lambda shard=shard: [copy.start() for copy in outputs(shard)]]
    first_piece = 6 + 2 * plan.lag
    for step in range(max(plan.steps, first_piece + len(pieces))):
        if step < plan.steps:
            plan.step(step)
        if step == 5:
            pl.when(plan.has_l)(lambda: to_left.start())
            pl.when(plan.has_r)(lambda: to_right.start())
        if step >= first_piece and pieces:
            pieces.pop(0)()
    for m in (1, 2):
        plan.arrived_all(m)
    plan.drain()
    a_out.wait()
    i_out.wait()
    for step in range(1, nz):
        bias_move(step).wait_send()
    pl.when(plan.has_l)(lambda: to_left.wait_send())
    pl.when(plan.has_r)(lambda: to_right.wait_send())
    weight_out.wait()
    window_copy.wait()
    for shard in range(4):
        for copy in outputs(shard):
            copy.wait()


def first(qkv_weight, attn_weight, in_weight, tokens, bias, cosine, sine):
    local, width = tokens.shape
    long = 3 * local
    shape = jax.ShapeDtypeStruct
    dma = pltpu.SemaphoreType.DMA
    return pl.pallas_call(
        first_kernel,
        in_specs=hbm_specs(4) + vmem_specs(3),
        out_specs=hbm_specs(4) + vmem_specs(1) + hbm_specs(5),
        out_shape=[
            shape((3, width, width), BF),
            shape((width, width), BF),
            shape((width, 4 * width), BF),
            shape((long, width), BF),
            shape((4,) + bias.shape, BF),
            shape((local, width), BF),
            shape((long, width), BF),
            shape((width, long), BF),
            shape((long, width), BF),
            shape((width, long), BF),
        ],
        scratch_shapes=[
            pltpu.VMEM((3, width, width), BF),
            pltpu.VMEM((long, width), BF),
            pltpu.VMEM((local, width), BF),
            pltpu.VMEM((long, width), BF),
            pltpu.VMEM((width, long), BF),
            pltpu.VMEM((long, width), BF),
            pltpu.VMEM((width, long), BF),
            pltpu.VMEM(attn_weight.shape, BF),
            pltpu.VMEM(in_weight.shape, BF),
        ]
        + gather_sems(3)
        + [dma((5,)), dma((7,)), dma((2, 3)), dma((22,))],
        compiler_params=pltpu.CompilerParams(collective_id=0, has_side_effects=True, vmem_limit_bytes=VMEM_BIG),
    )(qkv_weight, attn_weight, in_weight, tokens, bias, cosine, sine)


def normalise(values):
    mean_value = jnp.mean(values, axis=1, keepdims=True)
    centered = values - mean_value
    variance = jnp.mean(centered * centered, axis=1, keepdims=True)
    scale = lax.rsqrt(variance + eps_norm)
    return centered * scale, scale


FF_STEP = 512
ROOT_HALF = math.sqrt(0.5)
ROOT_TURN = 1.0 / math.sqrt(2.0 * math.pi)


def second_kernel(
    out_src, mixed, tokens, attn_all, in_all, in_bias, vectors, proj_weight,
    out_all, hidden_out, slope_out, normed_out, unit_one_out, scale_one, output_out, unit_two_out, scale_two, emb_all,
    weight, mixed_v, tokens_v, attn_v, in_v, hidden, slope, normed, normed_low, total, unit, output_low, unit_two, emb,
    z_send, z_recv, p_send, p_recv, l_sem, i_sem, o_sem, e_sem,
):
    plan = Gather(("out0", "out1"), (out_src, out_src), (weight, weight), z_send, z_recv, p_send, p_recv, 4)
    z, dp, nz = plan.z, plan.dp, plan.nz
    local = tokens.shape[0]
    per = out_src.shape[0]
    own = pltpu.make_async_copy(out_src, weight.at[pl.ds(pl.multiple_of(z * per, 16), per)], l_sem.at[0])
    loads = [
        pltpu.make_async_copy(src, dst, l_sem.at[1 + index])
        for index, (src, dst) in enumerate(((mixed, mixed_v), (attn_all, attn_v), (tokens, tokens_v)))
    ]
    ff = in_all.shape[1]
    ff_steps = ff // FF_STEP

    def in_load(index):
        return pltpu.make_async_copy(
            in_all.at[:, pl.ds(index * FF_STEP, FF_STEP)], in_v.at[index % 2], i_sem.at[index % 2]
        )

    for copy in (*loads, own, in_load(0), in_load(1)):
        copy.start()
    plan.barrier()
    plan.own_start(0)

    saves = [
        pltpu.make_async_copy(src, dst, o_sem.at[index])
        for index, (src, dst) in enumerate(
            ((hidden, hidden_out), (slope, slope_out), (normed_low, normed_out), (unit, unit_one_out),
             (output_low, output_out), (unit_two, unit_two_out), (weight, out_all))
        )
    ]

    def attn_half(half):
        if half == 0:
            for load in loads:
                load.wait()
        rows = slice(half * (local // 2), (half + 1) * (local // 2))
        attn_out = dot(mixed_v[rows, :], attn_v[...]) + vectors[0:1, :]
        made, scale = normalise(tokens_v[rows, :].astype(F32) + attn_out)
        unit[rows, :] = made
        scale_one[rows, :] = jnp.broadcast_to(scale, (local // 2, 128))
        full = made * vectors[2:3, :] + vectors[4:5, :]
        normed[rows, :] = full
        normed_low[rows, :] = full.astype(BF)
        if half == 1:
            saves[2].start()
            saves[3].start()

    def ff_one(index):
        in_load(index).wait()
        columns = slice(index * FF_STEP, (index + 1) * FF_STEP)

        def body(part, unused):
            rows = pl.ds(pl.multiple_of(part * 128, 128), 128)
            pre = dot(normed_low[rows, :], in_v[index % 2]) + in_bias[0:1, columns]
            spread = 0.5 + 0.5 * lax.erf(pre * ROOT_HALF)
            hidden[rows, columns] = (pre * spread).astype(BF)
            slope[rows, columns] = (spread + pre * (ROOT_TURN * jnp.exp(-0.5 * pre * pre))).astype(BF)
            return unused

        lax.fori_loop(0, local // 128, body, 0)
        if index + 2 < ff_steps:
            in_load(index + 2).start()
        if index == ff_steps - 1:
            saves[0].start()
            saves[1].start()

    def out_own():
        own.wait()
        at = pl.ds(pl.multiple_of(z * per, 128), per)
        total[...] = dot(hidden[:, at], weight[at, :]) + normed[...] + vectors[1:2, :]

    def out_shard(half, distance, side):
        plan.arrived(half, distance, side)

        @pl.when(plan.arrives(side, distance))
        def _():
            at = pl.ds(pl.multiple_of(plan.shard_of(side, distance) * per + half * 512, 128), 512)
            total[...] += dot(hidden[:, at], weight[at, :])

    pieces = [partial(attn_half, 0), partial(attn_half, 1)]
    pieces += [partial(ff_one, index) for index in range(ff_steps)]
    pieces += [out_own]
    pieces += [partial(out_shard, *event) for event in plan.events]
    for step in range(max(plan.steps, len(pieces))):
        if step < plan.steps:
            plan.step(step)
        if step < len(pieces):
            pieces[step]()
    saves[6].start()

    made, scale = normalise(total[...])
    unit_two[...] = made
    saves[5].start()
    scale_two[...] = jnp.broadcast_to(scale, (local, 128))
    output_low[...] = (made * vectors[3:4, :] + vectors[5:6, :]).astype(BF)
    saves[4].start()
    emb[...] = dot(output_low[...], proj_weight[...]).astype(BF)
    emb_all[pl.ds(z, 1)] = emb[...].reshape(1, local, 128)

    def emb_move(step):
        return remote(emb, emb_all.at[z], e_sem.at[0, step - 1], e_sem.at[1, step - 1], dp, lax.rem(z + step, nz))

    for step in range(1, nz):
        emb_move(step).start()
    plan.drain()
    for save in saves:
        save.wait()
    for step in range(1, nz):
        emb_move(step).wait()


def second(out_weight, mixed, tokens, attn_all, in_all, in_bias, vectors, proj_weight):
    local, width = tokens.shape
    ff = in_all.shape[1]
    shape = jax.ShapeDtypeStruct
    dma = pltpu.SemaphoreType.DMA
    return pl.pallas_call(
        second_kernel,
        in_specs=hbm_specs(5) + vmem_specs(3),
        out_specs=hbm_specs(5) + vmem_specs(1) + hbm_specs(2) + vmem_specs(2),
        out_shape=[
            shape((ff, width), BF),
            shape((local, ff), BF),
            shape((local, ff), BF),
            shape((local, width), BF),
            shape((local, width), F32),
            shape((local, 128), F32),
            shape((local, width), BF),
            shape((local, width), F32),
            shape((local, 128), F32),
            shape((4, local, 128), BF),
        ],
        scratch_shapes=[
            pltpu.VMEM((ff, width), BF),
            pltpu.VMEM((local, width), BF),
            pltpu.VMEM((local, width), BF),
            pltpu.VMEM((width, width), BF),
            pltpu.VMEM((2, width, FF_STEP), BF),
            pltpu.VMEM((local, ff), BF),
            pltpu.VMEM((local, ff), BF),
            pltpu.VMEM((local, width), F32),
            pltpu.VMEM((local, width), BF),
            pltpu.VMEM((local, width), F32),
            pltpu.VMEM((local, width), F32),
            pltpu.VMEM((local, width), BF),
            pltpu.VMEM((local, width), F32),
            pltpu.VMEM((local, 128), BF),
        ]
        + gather_sems(2)
        + [dma((4,)), dma((2,)), dma((7,)), dma((2, 3))],
        compiler_params=pltpu.CompilerParams(collective_id=1, has_side_effects=True, vmem_limit_bytes=VMEM_BIG),
    )(out_weight, mixed, tokens, attn_all, in_all, in_bias, vectors, proj_weight)


def norm_back(unit, scale, gain, grad):
    dn = grad * gain
    back = scale * (
        dn - jnp.mean(dn, axis=-1, keepdims=True) - unit * jnp.mean(dn * unit, axis=-1, keepdims=True)
    )
    return back, jnp.sum(grad * unit, axis=0), jnp.sum(grad, axis=0)


def segment_facts(lengths, doc_pairs, log_temp, local, z, dp_count):
    base = z * local
    row_lengths = lengths[0]
    seg_range = jnp.arange(SEGS, dtype=jnp.int32)
    seg_ends = jnp.sum(jnp.where(seg_range[:, None] >= seg_range[None, :], row_lengths[None, :], 0), axis=1)
    seg_starts = seg_ends - row_lengths
    positions = jnp.arange(SEQ, dtype=jnp.int32)
    seg_ids = jnp.sum((positions[:, None] >= seg_ends[None, :]).astype(jnp.int32), axis=1)
    near = jnp.arange(3 * local, dtype=jnp.int32) + base - local
    near_ids = jnp.sum((near[:, None] >= seg_ends[None, :]).astype(jnp.int32), axis=1)
    near_ids = jnp.where((near >= 0) & (near < SEQ), near_ids, -1)
    near_member = near_ids[:, None] == jnp.arange(SEGS, dtype=jnp.int32)[None, :]
    near_starts = jnp.sum(jnp.where(near_member, seg_starts[None, :], 0), axis=1)
    offsets = jnp.where(near_ids >= 0, near - near_starts, 0)
    half_dim = HDIM // 2
    inv_freq = jnp.exp(jnp.arange(half_dim, dtype=F32) * (-2.0 * math.log(10000.0) / HDIM))
    angles = offsets.astype(F32)[:, None] * inv_freq[None, :]
    cosine, sine = jnp.cos(angles), jnp.sin(angles)
    cosine = jnp.concatenate([cosine] * 4, axis=1)
    sine = jnp.concatenate([-sine, sine] * 2, axis=1)
    seg_q = jnp.broadcast_to(lax.slice_in_dim(near_ids, local, 2 * local)[None, :], (8, local))
    seg_k = jnp.broadcast_to(near_ids[:, None], (3 * local, 128))
    key_starts = jnp.where(near_ids >= 0, near_starts - base + local, 0)
    near_ends = jnp.sum(jnp.where(near_member, seg_ends[None, :], 0), axis=1)
    key_ends = jnp.where(near_ids >= 0, near_ends - base + local, 0)

    def live_blocks(rows):
        first_key = key_starts[local : 2 * local : rows]
        last_key = key_ends[local + rows - 1 : 2 * local : rows]
        return jnp.stack([first_key // BK, (last_key + BK - 1) // BK], axis=1)

    bounds = jnp.concatenate([live_blocks(FWD_ROWS), live_blocks(BACK_ROWS)])
    query_end = seg_ends[NQ - 1]
    info = jnp.stack([base // CB, (query_end + CB - 1) // CB, query_end // CB])
    seg_col = jnp.broadcast_to(seg_ids[:, None], (SEQ, 128))
    seg_row = jnp.broadcast_to(seg_ids[None, :], (8, SEQ))
    counts = jnp.broadcast_to(row_lengths.astype(F32)[:, None], (SEGS, 128))
    positive = (doc_pairs[0][:, None] == jnp.arange(128, dtype=jnp.int32)[None, :]).astype(F32)
    loss_scale = 1.0 / (NQ * dp_count)
    temp_row = jnp.concatenate([log_temp, jnp.full((127,), loss_scale, F32)]).reshape(1, 128)

    return bounds, seg_q, seg_k, cosine, sine, info, seg_col, seg_row, counts, positive, temp_row


def per_device(
    tokens, lengths, doc_pairs, qkv_weight, qkv_bias, attn_weight, attn_bias, ffn_in_weight, ffn_in_bias,
    ffn_out_weight, ffn_out_bias, norm_gains, norm_shifts, proj_weight, log_temp,
):
    local, width = tokens.shape
    dp_count = lax.axis_size("dp")
    tensor_count = lax.axis_size("tensor")
    groups = dp_count // 8
    z = lax.axis_index("tensor")
    bounds, seg_q, seg_k, cosine, sine, info, seg_col, seg_row, counts, positive, temp_row = segment_facts(
        lengths, doc_pairs, log_temp, local, z, dp_count
    )
    gains = norm_gains.astype(F32)
    shifts = norm_shifts.astype(F32)
    bias = jnp.concatenate([qkv_bias.reshape(6, 128), ffn_in_bias.reshape(8, 128), jnp.zeros((2, 128), BF)])
    qkv_all, attn_all, in_all, window, bias_all, queries, keys, keys_t, values, values_t = first(
        jnp.transpose(qkv_weight, (1, 0, 2)), attn_weight, ffn_in_weight, tokens, bias, cosine, sine
    )
    in_bias_all = bias_all[:, 6:14].reshape(1, 4 * width).astype(F32)
    vectors = jnp.concatenate(
        [attn_bias.astype(F32)[None], ffn_out_bias.astype(F32)[None], gains, shifts, jnp.zeros((2, width), F32)]
    )
    mixed, lse = attend(bounds[: local // FWD_ROWS], queries, keys, values_t, seg_q, seg_k)
    out_all, hidden, slope, normed_low, unit_one, scale_one, output_low, unit_two, scale_two, embedded_all = second(
        ffn_out_weight, mixed, tokens, attn_all, in_all, in_bias_all, vectors, proj_weight
    )
    embedded_all = embedded_all.reshape(-1, EMB)
    scale_one, scale_two = scale_one[:, :1], scale_two[:, :1]
    emb_grad, row_loss, row_temp = contrast(info, embedded_all, seg_col, seg_row, counts, positive, temp_row, local)

    proj_grad = dot(output_low, emb_grad, 0, 0)
    output_grad = dot(emb_grad, proj_weight, 1, 1)
    resid_two_grad, gain_two_grad, shift_two_grad = norm_back(unit_two, scale_two, gains[1], output_grad)
    ffn_grad = resid_two_grad.astype(BF)
    out_bias_grad = jnp.sum(ffn_grad.astype(F32), axis=0)
    hidden_grad = dot(ffn_grad, out_all, 1, 1)
    pre_grad = (hidden_grad * slope.astype(F32)).astype(BF)
    in_bias_grad = jnp.sum(pre_grad.astype(F32), axis=0)
    normed_grad = dot(pre_grad, in_all, 1, 1) + resid_two_grad
    resid_one_grad, gain_one_grad, shift_one_grad = norm_back(unit_one, scale_one, gains[0], normed_grad)
    attn_grad = resid_one_grad.astype(BF)
    attn_bias_grad = jnp.sum(attn_grad.astype(F32), axis=0)
    mixed_grad = dot(attn_grad, attn_all, 1, 1).astype(BF)
    dq, dk, dv = attend_back(bounds[local // FWD_ROWS :], queries, keys, keys_t, values, mixed, mixed_grad, lse, seg_q, seg_k, cosine, sine)
    window_grad = dot(dk, qkv_all[1], 1, 1) + dot(dv, qkv_all[2], 1, 1)
    window_low = window_grad.astype(BF)
    own_grad = window_grad[local : 2 * local] + dot(dq, qkv_all[0], 1, 1) + resid_one_grad
    qkv_bias_grad = jnp.concatenate([jnp.sum(part.astype(F32), axis=0) for part in (dq, dk, dv)])

    share = 1.0 / tensor_count
    proj_red = lax.psum(proj_grad, ("dp", "tensor"))
    small = jnp.concatenate(
        [
            attn_bias_grad, out_bias_grad, gain_one_grad, gain_two_grad, shift_one_grad, shift_two_grad,
            qkv_bias_grad, in_bias_grad, row_loss[0, :1] * share, row_temp[0, :1] * share,
            jnp.zeros((SMALL_ROWS * 128 - 13 * width - 2,), F32),
        ]
    ).reshape(SMALL_ROWS, 128)

    def arrange(array):
        if groups == 1:
            return array
        rows = array.shape[0]
        return array.reshape(rows, groups, 8, -1).transpose(0, 2, 1, 3).reshape(rows, width)

    qkv_red, attn_red, in_red, out_red, small, from_left, from_right = scatter(
        arrange(window), arrange(attn_grad), arrange(normed_low), arrange(ffn_grad),
        dq, dk, dv, mixed, pre_grad, hidden, window_low, small,
    )
    if groups > 1:
        ranks = [[high * 8 + low for high in range(groups)] for low in range(8)]
        qkv_red, attn_red, in_red, out_red = (
            lax.psum_scatter(part, "dp", scatter_dimension=0, axis_index_groups=ranks, tiled=True)
            for part in (qkv_red, attn_red, in_red, out_red)
        )
        small = lax.psum(small, "dp", axis_index_groups=ranks)
    tokens_grad = (
        own_grad
        + jnp.where(z > 0, from_left.astype(F32), 0.0)
        + jnp.where(z < tensor_count - 1, from_right.astype(F32), 0.0)
    )
    flat = small.reshape(-1)

    def cut(start, length):
        return lax.slice_in_dim(flat, start * width, (start + length) * width)

    qkv_bias_red = lax.dynamic_slice_in_dim(cut(6, 3).reshape(3, width), z * 256, 256, 1)
    in_bias_red = lax.dynamic_slice_in_dim(cut(9, 4), z * width, width, 0)
    return (
        flat[13 * width : 13 * width + 1],
        output_low,
        tokens_grad,
        qkv_red.reshape(-1, 3, 256),
        qkv_bias_red,
        attn_red.T,
        cut(0, 1),
        in_red,
        in_bias_red,
        out_red.T,
        cut(1, 1),
        cut(2, 2).reshape(2, width),
        cut(4, 2).reshape(2, width),
        proj_red,
        flat[13 * width + 1 : 13 * width + 2],
    )


def solution(mesh):
    in_specs = (
        P(("dp", "tensor"), None),
        P("dp", None),
        P("dp", None),
        P(None, None, "tensor"),
        P(None, "tensor"),
        P("tensor", None),
        P(),
        P(None, "tensor"),
        P("tensor"),
        P("tensor", None),
        P(),
        P(),
        P(),
        P(),
        P(),
    )
    out_specs = (
        P(),
        P(("dp", "tensor"), None),
        P(("dp", "tensor"), None),
        P("dp", None, "tensor"),
        P(None, "tensor"),
        P("tensor", "dp"),
        P(),
        P("dp", "tensor"),
        P("tensor"),
        P("tensor", "dp"),
        P(),
        P(),
        P(),
        P(),
        P(),
    )
    return jax.shard_map(
        per_device, mesh=mesh, in_specs=in_specs, out_specs=out_specs, check_vma=False
    )
```

time: 667 us -> 484 us (0.73)
  Pallas kernels: 499 us -> 367 us
  matrix products: 81 us -> 44.2 us
  blocking collectives: 17.1 us -> 0 us
  between operations: 7.06 us -> 20 us
    pallas_call x4 -> x3, Pallas kernels: 349 us -> 297 us  [the longest x1 146 us: scatter(): pl.pallas_call(scatter_kernel, in_specs=hbm_specs(11) + vmem_specs(1), ou...]
    pallas_call x1, Pallas kernels: 47.9 us -> 9.29 us  [attend(): pl.pallas_call(attend_kernel, grid_spec=pltpu.PrefetchScalarGridSpec(num_...]
    dot_general x12 -> x8, matrix products: 81 us -> 44.2 us  [dot(): lax.dot_general(left, right, (((left_dim,), (right_dim,)), ((), ())), pre...]
    pallas_call x1, Pallas kernels: 49.1 us -> 20.5 us  [contrast(): pl.pallas_call(contrast_kernel, in_specs=[pl.BlockSpec(memory_space=pltpu...]
    all_gather x1 -> x0, blocking collectives: 17.1 us -> none  [per_device(): embedded_all = lax.all_gather(embedded, 'tensor', axis=0, tiled=True)]
    pallas_call x1, Pallas kernels: 53.2 us -> 39.8 us  [attend_back(): pl.pallas_call(attend_back_kernel, grid_spec=pltpu.PrefetchScalarGridSpec...]
    unnamed x109 -> x86, local copies, waits for them, and re-layouts: 20.8 us -> 14.9 us
  transfers between devices with their start and end apart: 0 -> 1, of which waited for: 0 -> 0; matrix products, arithmetic and copies ran while one was open for 0% -> 14% of each run, Pallas kernels for 0% -> 39%
where the time goes in v2:
time: 484 us; the launch traced here: 478 us
  Pallas kernels  367 us (76%)
  matrix products  44.2 us (9%)
  local copies, waits for them, and re-layouts  30.3 us (6%)
  between operations  20 us (4%)
  other arithmetic  16.5 us (3%)
    pallas_call x1, Pallas kernels, scatter(): pl.pallas_call(scatter_kernel, in_specs=hbm_specs(11) + vmem_specs(1), ou...  146 us
    pallas_call x1, Pallas kernels, first(): pl.pallas_call(first_kernel, in_specs=hbm_specs(4) + vmem_specs(3), out_s...  91.3 us
    pallas_call x1, Pallas kernels, second(): pl.pallas_call(second_kernel, in_specs=hbm_specs(5) + vmem_specs(3), out_...  60 us
    dot_general x8, matrix products, dot(): lax.dot_general(left, right, (((left_dim,), (right_dim,)), ((), ())), pre...  44.2 us
    pallas_call x1, Pallas kernels, attend_back(): pl.pallas_call(attend_back_kernel, grid_spec=pltpu.PrefetchScalarGridSpec...  39.8 us
    pallas_call x1, Pallas kernels, contrast(): pl.pallas_call(contrast_kernel, in_specs=[pl.BlockSpec(memory_space=pltpu...  20.5 us
    unnamed x86, local copies, waits for them, and re-layouts  14.9 us
  transfers between devices with their start and end apart: 1, of which 0 were waited for; matrix products, arithmetic and copies ran while one was open for 14% of the time, Pallas kernels for 39%

profile of v2, /device:TPU:24, one launch (start us, length us, event | category | flops | bytes accessed | tf_op | source)
XLA Modules:
  0.0 478.0 jit_solution(4854393736975878517)
XLA Ops:
  7.3 0.8 select_reduce_fusion.2
  8.0 0.7 bitcast_convert_fusion
  8.7 0.6 slice.93
  12.6 0.7 reshape.143
  14.1 2.8 fusion.13
  16.9 0.7 maximum_maximum_fusion.bias
  17.6 2.4 pad_maximum_fusion
  20.0 91.3 %shard_map.262 = (bf16[3,1024,1024]{2,1,0:T(8,128)(2,1)}, bf16[1024,1024]{1,0:T(8,128)(2,1)}, bf16[1024,4096]{1,0:T(8,128)(2,1)}, bf16[1536,1024]{1,0:T(8,128)(2...) custom-call(bf16[3,1024,256]{2,1,0:T(8,128)(2,1)} %bitcast.74, ...), custom_call_target="tpu_custom_call" | custom-call | tf_op jit(solution)/shard_map/pallas_call | solution.py:1047
  111.3 1.3 slice_convert_fusion
  113.6 0.7 concatenate.21.vectors
  114.6 1.9 copy-done.4
  116.5 1.9 copy-done.5
  118.4 1.2 copy-done.8
  119.6 9.3 %shard_map.263 = (bf16[512,1024]{1,0:T(8,128)(2,1)S(1)}, f32[16,512]{1,0:T(8,128)S(1)}) custom-call(s32[4,2]{1,0:T(4,128)S(1)} %pad_add_fusion.bounds_ref, bf16[512,1024]{1,0:T(8,128)(2,1)S(1)} %copy-done.8, bf16[1536,1024]{1,0:T(8,128)(2,1)S(1)} %copy-done.4, bf16[1024,1536]{1,0:T(8,128)(2,1)S(1)} %copy-done.5, s32[8,512]{1,0:T(8,128)S(1)} %broadcast_in_dim.121.segq_ref, ...), custom_call_target="tpu_custom_call" | custom-call | flops 2147483648 | bytes 8388608 | tf_op jit(solution)/shard_map/pallas_call | solution.py:113
  128.9 1.0 copy-done
  129.8 60.0 %shard_map.264 = (bf16[4096,1024]{1,0:T(8,128)(2,1)}, bf16[512,4096]{1,0:T(8,128)(2,1)}, bf16[512,4096]{1,0:T(8,128)(2,1)}, bf16[512,1024]{1,0:T(8,128)(2,1)}, f...) custom-call(bf16[1024,1024]{1,0:T(8,128)(2,1)} %out_src.1, ...), custom_call_target="tpu_custom_call" | custom-call | tf_op jit(solution)/shard_map/pallas_call | solution.py:1214
  190.3 1.0 copy-done.10
  191.3 20.5 %shard_map.265 = (bf16[512,128]{1,0:T(8,128)(2,1)S(1)}, f32[8,128]{1,0:T(8,128)S(1)}, f32[8,128]{1,0:T(8,128)S(1)}) custom-call(s32[3]{0:T(128)S(1)} %pad_add_fusion.2.info_ref, bf16[2048,128]{1,0:T(8,128)(2,1)S(1)} %bitcast.70, s32[2048,128]{1,0:T(8,128)S(1)} %broadcast_in_dim.128.segc_ref, s32[8,2048]{1,0:T(8,128)S(1)} %broadcast_in_dim.129.segr_ref, ...), custom_call_target="tpu_custom_call" | custom-call | flops 1073741824 | bytes 4194304 | tf_op jit(solution)/shard_map/pallas_call | solution.py:357
  211.8 1.3 fusion.32
  213.6 0.8 multiply_reduce_fusion
  215.8 11.2 %convert_reduce_fusion = (f32[4096]{0:T(1024)S(1)}, bf16[512,4096]{1,0:T(8,128)(2,1)}) fusion(bf16[512,4096]{1,0:T(8,128)(2,1)} %get-tuple-element.64, bf16[512,1024]{1,0:T(8,128)(2,1)S(1)} %get-tuple-element.156.ffn_grad, bf16[4096,1024]{1,0:T(8,128)(2,1)} %get-tuple-element.63), kind=kOutput, calls=%fused_computation | convolution fusion | flops 4305448960 | bytes 17842176 | tf_op jit(solution)/shard_map/dot_general | solution.py:26
  227.0 9.4 %multiply_reduce_fusion.1 = (f32[1024]{0:T(1024)S(1)}, f32[512]{0:T(512)S(1)}, f32[512]{0:T(512)S(1)}, f32[1024]{0:T(1024)S(1)}, f32[512,1024]{1,0:T(8,128)}) fusion(f32[512,1024]{1,0:T(8,128)} %get-tuple-element.65, f32[1024]{0:T(1024)S(1)} %bitcast.85, f32[512,1024]{1,0:T(8,128)S(1)} %copy-done.13, f32[512]{0:T(512)S(1)} %broadcast_multiply_fusion.2, ...), kind=kOutput, calls=%fused_computation.17 | convolution fusion | flops 4301779968 | bytes 20998144 | tf_op jit(solution)/shard_map/dot_general | solution.py:26
  236.8 2.9 convert_reduce_fusion.5
  239.8 2.3 convolution_convert_fusion.grad_ref
  242.5 39.8 %shard_map.266 = (bf16[512,1024]{1,0:T(8,128)(2,1)S(1)}, bf16[1536,1024]{1,0:T(8,128)(2,1)}, bf16[1536,1024]{1,0:T(8,128)(2,1)}) custom-call(s32[2,2]{1,0:T(2,128)S(1)} %pad_add_fusion.1.bounds_ref, bf16[512,1024]{1,0:T(8,128)(2,1)S(1)} %copy-done.9, bf16[1536,1024]{1,0:T(8,128)(2,1)} %get-tuple-element.52.key_ref, ...), custom_call_target="tpu_custom_call" | custom-call | flops 5368709120 | bytes 16777216 | tf_op jit(solution)/shard_map/pallas_call | solution.py:203
  282.4 2.9 convert_reduce_fusion.2
  285.6 5.2 %fusion.6 = f32[1536,1024]{1,0:T(8,128)S(1)} fusion(bf16[1536,1024]{1,0:T(8,128)(2,1)S(1)} %copy-done.11, bf16[3,1024,1024]{2,1,0:T(8,128)(2,1)} %get-tuple-element.74), kind=kOutput, calls=%fused_computation.12 | convolution fusion | flops 3221225472 | bytes 11534336 | tf_op jit(solution)/shard_map/dot_general | solution.py:26
  290.9 0.6 convert_reduce_fusion.1
  291.5 7.4 %fusion.31 = (bf16[1536,1024]{1,0:T(8,128)(2,1)}, f32[1536,1024]{1,0:T(8,128)}) fusion(f32[1536,1024]{1,0:T(8,128)S(1)} %fusion.6, bf16[1536,1024]{1,0:T(8,128)(2,1)S(1)} %copy-done.12, bf16[3,1024,1024]{2,1,0:T(8,128)(2,1)} %get-tuple-element.74), kind=kOutput, calls=%fused_computation.99 | convolution fusion | flops 3224371200 | bytes 20971520 | tf_op jit(solution)/shard_map/dot_general | solution.py:26
  301.3 0.7 concatenate.23
  302.1 146.0 %shard_map.267 = (f32[128,768]{1,0:T(8,128)}, f32[128,256]{1,0:T(8,128)}, f32[128,1024]{1,0:T(8,128)}, f32[128,1024]{1,0:T(8,128)}, f32[112,128]{1,0:T(8,128)}, ...) custom-call(bf16[1536,1024]{1,0:T(8,128)(2,1)} %get-tuple-element.50.window, bf16[512,1024]{1,0:T(8,128)(2,1)} %copy-done.18, ...), custom_call_target="tpu_custom_call" | custom-call | tf_op jit(solution)/shard_map/pallas_call | solution.py:721
  448.1 0.7 slice.105
  448.8 1.3 slice_bitcast_fusion
  450.1 0.7 fusion.29
  450.8 1.3 fusion.28
  452.2 0.6 reshape.150
  452.8 6.7 %fusion.2 = f32[512,1024]{1,0:T(8,128)} fusion(f32[1536,1024]{1,0:T(8,128)} %get-tuple-element.179, bf16[512,1024]{1,0:T(8,128)(2,1)} %get-tuple-element.80, bf16[512,1024]{1,0:T(8,128)(2,1)} %get-tuple-element.79, bf16[512,1024]{1,0:T(8,128)(2,1)S(1)} %copy-done.3, bf16[3,1024,1024]{2,1,0:T(8,128)(2,1)} %get-tuple-element.74, pred[]{:T(512)S(6)} %lt.24, ...), kind=kOutput, calls=%fused_computation.8 | convolution fusion | flops 1080557568 | bytes 13641730 | tf_op jit(solution)/shard_map/dot_general | solution.py:26
  459.5 1.4 constant_dynamic-slice_fusion
  461.0 0.9 copy.59
  462.0 1.7 copy.60
  463.6 1.0 copy.61
  464.6 0.6 reshape.151
  465.2 0.6 reshape.152
  465.8 1.3 dynamic_slice.7
  467.1 1.3 slice_bitcast_fusion.1
  468.4 1.0 copy.66
  469.4 0.8 copy.67
  470.2 0.8 copy.68
  (128 shorter events, 6.2 us)
Async XLA Ops:
  7.2 9.7 %copy-start.34 = (bf16[1024]{0:T(1024)(128)(2,1)S(1)}, bf16[1024]{0:T(1024)(128)(2,1)}, u32[]{:S(2)}) copy-start(bf16[1024]{0:T(1024)(128)(2,1)} %param.23) | copy-start | bytes 6148
  7.2 461.2 %all-reduce.3.cloned.1.call-start = ((), (), s32[]{:S(2)}) async-start(), calls=%async_computation | async-start | bytes 1048576 | tf_op jit(solution)/shard_map/psum | solution.py:1354
  20.0 92.6 %copy-start.35 = (bf16[1024]{0:T(1024)(128)(2,1)S(1)}, bf16[1024]{0:T(1024)(128)(2,1)}, u32[]{:S(2)}) copy-start(bf16[1024]{0:T(1024)(128)(2,1)} %param.21) | copy-start | bytes 6148
  20.0 92.7 %copy-start.36 = (bf16[1024]{0:T(1024)(128)(2,1)S(1)}, bf16[1024]{0:T(1024)(128)(2,1)}, u32[]{:S(2)}) copy-start(bf16[1024]{0:T(1024)(128)(2,1)} %param.25) | copy-start | bytes 6148
  20.0 92.7 %copy-start.37 = (s32[1,8]{1,0:T(1,128)S(1)}, s32[1,8]{1,0:T(1,128)}, u32[]{:S(2)}) copy-start(s32[1,8]{1,0:T(1,128)} %param.17) | copy-start | bytes 100
  20.0 93.6 %copy-start.28 = (bf16[2,1024]{1,0:T(2,128)(2,1)S(1)}, bf16[2,1024]{1,0:T(2,128)(2,1)}, u32[]{:S(2)}) copy-start(bf16[2,1024]{1,0:T(2,128)(2,1)} %param.26) | copy-start | bytes 12292
  20.0 93.6 %copy-start.33 = (bf16[2,1024]{1,0:T(2,128)(2,1)S(1)}, bf16[2,1024]{1,0:T(2,128)(2,1)}, u32[]{:S(2)}) copy-start(bf16[2,1024]{1,0:T(2,128)(2,1)} %param.27) | copy-start | bytes 12292
  114.6 1.9 copy-start.4
  116.5 1.9 copy-start.5
  118.3 1.2 copy-start.8
  128.9 1.0 copy-start
  190.3 1.0 copy-start.10
  191.3 20.5 %copy-start.15 = (bf16[512,1024]{1,0:T(8,128)(2,1)S(1)}, bf16[512,1024]{1,0:T(8,128)(2,1)}, u32[]{:S(2)}) copy-start(bf16[512,1024]{1,0:T(8,128)(2,1)} %get-tuple-element.200) | copy-start | bytes 3145732
  191.3 22.0 %copy-start.21 = (bf16[1024,128]{1,0:T(8,128)(2,1)S(1)}, bf16[1024,128]{1,0:T(8,128)(2,1)}, u32[]{:S(2)}) copy-start(bf16[1024,128]{1,0:T(8,128)(2,1)} %proj_weight.1) | copy-start | bytes 786436
  211.8 1.8 copy-start.13
  213.1 23.6 %copy-start.29 = (f32[1,1024]{1,0:T(1,128)}, f32[1,1024]{1,0:T(1,128)S(1)}, u32[]{:S(2)}) copy-start(f32[1,1024]{1,0:T(1,128)S(1)} %get-tuple-element.170) | copy-start | bytes 12292
  213.6 0.9 copy-start.27
  214.4 1.3 copy-start.14
  214.7 12.3 %slice-start = ((s8[8388608]{0:T(1024)(128)(4,1)}), s8[4194304]{0:T(1024)(128)(4,1)S(1)}, s32[]{:S(2)}) async-start(s8[8388608]{0:T(1024)(128)(4,1)} %bitcast.71), calls=%async_computation.1 | async-start | bytes 8388608
  215.8 11.2 %copy-start.17 = (bf16[512,1024]{1,0:T(8,128)(2,1)}, bf16[512,1024]{1,0:T(8,128)(2,1)S(1)}, u32[]{:S(2)}) copy-start(bf16[512,1024]{1,0:T(8,128)(2,1)S(1)} %get-tuple-element.156.ffn_grad) | copy-start | bytes 3145732
  215.8 11.2 %slice-start.1 = ((s8[8388608]{0:T(1024)(128)(4,1)}), s8[4194304]{0:T(1024)(128)(4,1)S(1)}, s32[]{:S(2)}) async-start(s8[8388608]{0:T(1024)(128)(4,1)} %bitcast.71), calls=%async_computation.2 | async-start | bytes 8388608
  227.0 9.4 %copy-start.26 = (f32[512,128]{1,0:T(8,128)S(1)}, f32[512,128]{1,0:T(8,128)}, u32[]{:S(2)}) copy-start(f32[512,128]{1,0:T(8,128)} %get-tuple-element.58) | copy-start | bytes 786436
  236.4 3.3 copy-start.31
  236.4 3.3 copy-start.32
  236.5 3.2 copy-start.30
  236.8 3.0 copy-start.20
  239.7 2.3 copy-start.18
  239.7 2.4 copy-start.1
  239.8 2.4 copy-start.6
  239.8 2.4 copy-start.7
  239.8 2.8 copy-start.9
  282.4 16.5 %copy-start.2 = (bf16[512,1024]{1,0:T(8,128)(2,1)}, bf16[512,1024]{1,0:T(8,128)(2,1)S(1)}, u32[]{:S(2)}) copy-start(bf16[512,1024]{1,0:T(8,128)(2,1)S(1)} %get-tuple-element.70.dq) | copy-start | bytes 3145732
  282.4 3.3 copy-start.11
  285.6 5.2 %copy-start.12 = (bf16[1536,1024]{1,0:T(8,128)(2,1)S(1)}, bf16[1536,1024]{1,0:T(8,128)(2,1)}, u32[]{:S(2)}) copy-start(bf16[1536,1024]{1,0:T(8,128)(2,1)} %get-tuple-element.72.dv) | copy-start | bytes 9437188
  302.1 150.7 %copy-start.3 = (bf16[512,1024]{1,0:T(8,128)(2,1)S(1)}, bf16[512,1024]{1,0:T(8,128)(2,1)}, u32[]{:S(2)}) copy-start(bf16[512,1024]{1,0:T(8,128)(2,1)} %copy-done.2) | copy-start | bytes 3145732
  302.1 150.7 %copy-start.19 = (f32[512,1024]{1,0:T(8,128)S(1)}, f32[512,1024]{1,0:T(8,128)}, u32[]{:S(2)}) copy-start(f32[512,1024]{1,0:T(8,128)} %get-tuple-element.65) | copy-start | bytes 6291460
  452.8 8.1 %copy-start.25 = (f32[128,768]{1,0:T(8,128)S(1)}, f32[128,768]{1,0:T(8,128)}, u32[]{:S(2)}) copy-start(f32[128,768]{1,0:T(8,128)} %get-tuple-element.81) | copy-start | bytes 1179652
  459.5 4.2 copy-start.24
  459.5 8.9 %copy-start.16 = (bf16[512,1024]{1,0:T(8,128)(2,1)S(1)}, bf16[512,1024]{1,0:T(8,128)(2,1)}, u32[]{:S(2)}) copy-start(bf16[512,1024]{1,0:T(8,128)(2,1)} %get-tuple-element.200) | copy-start | bytes 3145732
  461.0 8.3 %copy-start.23 = (f32[128,1024]{1,0:T(8,128)S(1)}, f32[128,1024]{1,0:T(8,128)}, u32[]{:S(2)}) copy-start(f32[128,1024]{1,0:T(8,128)} %get-tuple-element.206) | copy-start | bytes 1572868
  468.4 1.8 copy-start.22
Sparse Core Ops, SparseCore 0:
  213.3 132.3 all-reduce.2

commit v3 on v2

--- a/solution.py
+++ b/solution.py
@@ -54,7 +54,6 @@
 BACK_ROWS = 256
 BK = 256
 FWD_GROUPS = 8
-BACK_GROUPS = 4
 SCALE = HDIM**-0.5
 
 
@@ -136,101 +135,6 @@
     )(bounds, queries, keys, turned, seg_q, seg_k)
 
 
-def attend_back_kernel(
-    bounds_ref, query_ref, key_ref, turned_ref, value_ref, mixed_ref, grad_ref, lse_ref, segq_ref, segk_ref,
-    cos_ref, sin_ref, dq_ref, dk_ref, dv_ref, dk_acc, dv_acc,
-):
-    local = query_ref.shape[0]
-    groups = range(0, query_ref.shape[1], 128)
-    dk_acc[...] = jnp.zeros_like(dk_acc)
-    dv_acc[...] = jnp.zeros_like(dv_acc)
-    head_row = lax.broadcasted_iota(jnp.int32, (8, 128), 0)
-    head_lane = lax.broadcasted_iota(jnp.int32, (8, 128), 1) // 64
-    chosen = jnp.where(head_row == head_lane, 1.0, 0.0)
-    for block in range(local // BACK_ROWS):
-        rows = pl.ds(block * BACK_ROWS, BACK_ROWS)
-        queries, grads, turned_q, turned_g, deltas, logs = [], [], [], [], [], []
-        for group, at in enumerate(groups):
-            lanes = slice(at, at + 128)
-            queries.append(split_pair(query_ref[rows, lanes] * jnp.asarray(SCALE, BF)))
-            grads.append(split_pair(grad_ref[rows, lanes]))
-            turned_q.append(split_pair(turn(query_ref[rows, lanes] * jnp.asarray(SCALE, BF)), 0))
-            turned_g.append(split_pair(turn(grad_ref[rows, lanes]), 0))
-            product = mixed_ref[rows, lanes].astype(F32) * grad_ref[rows, lanes].astype(F32)
-            delta = dot(chosen, product, 1, 1, lax.Precision.HIGHEST)
-            deltas.append((delta[0:1], delta[1:2]))
-            logs.append((lse_ref[2 * group : 2 * group + 1, rows], lse_ref[2 * group + 1 : 2 * group + 2, rows]))
-        seg_q = segq_ref[0:1, rows]
-
-        def body(index, carry):
-            keys_at = pl.ds(pl.multiple_of(index * BK, BK), BK)
-            live = segk_ref[keys_at, 0:1] == seg_q
-            made = []
-            for group, at in enumerate(groups):
-                lanes = slice(at, at + 128)
-                keys = key_ref[keys_at, lanes]
-                values = value_ref[keys_at, lanes]
-                turned = turned_ref[lanes, keys_at]
-                dk, dv = 0.0, 0.0
-                for head in range(2):
-                    scores = jnp.where(live, dot(keys, turned_q[group][head]), -1e9)
-                    probs = jnp.exp(scores - logs[group][head])
-                    score_low = (probs * (dot(values, turned_g[group][head]) - deltas[group][head])).astype(BF)
-                    made.append(carry[2 * group + head] + dot(turned, score_low))
-                    dk = dk + dot(score_low, queries[group][head])
-                    dv = dv + dot(probs.astype(BF), grads[group][head])
-                dk_acc[keys_at, lanes] += dk
-                dv_acc[keys_at, lanes] += dv
-            return tuple(made)
-
-        start = (jnp.zeros((128, BACK_ROWS), F32),) * (2 * len(groups))
-        done = lax.fori_loop(bounds_ref[block, 0], bounds_ref[block, 1], body, start)
-        at_window = pl.ds(local + block * BACK_ROWS, BACK_ROWS)
-        for group, at in enumerate(groups):
-            grad = jnp.concatenate([done[2 * group][0:64], done[2 * group + 1][64:128]], axis=0).T * SCALE
-            back = rotate_lanes(grad, cos_ref[at_window, :], -sin_ref[at_window, :])
-            dq_ref[rows, at : at + 128] = back.astype(BF)
-    dk_ref[...] = rotate_lanes(dk_acc[...], cos_ref[...], -sin_ref[...]).astype(BF)
-    dv_ref[...] = dv_acc[...].astype(BF)
-
-
-def attend_back(bounds, queries, keys, turned, values, mixed, grad, lse, seg_q, seg_k, cosine, sine):
-    local, width = queries.shape
-    long = keys.shape[0]
-    lanes = BACK_GROUPS * 128
-    short_spec = pl.BlockSpec((local, lanes), lambda g, b: (0, g))
-    long_spec = pl.BlockSpec((long, lanes), lambda g, b: (0, g))
-    return pl.pallas_call(
-        attend_back_kernel,
-        grid_spec=pltpu.PrefetchScalarGridSpec(
-            num_scalar_prefetch=1,
-            grid=(width // lanes,),
-            in_specs=[
-                short_spec,
-                long_spec,
-                pl.BlockSpec((lanes, long), lambda g, b: (g, 0)),
-                long_spec,
-                short_spec,
-                short_spec,
-                pl.BlockSpec((2 * BACK_GROUPS, local), lambda g, b: (g, 0)),
-                pl.BlockSpec((8, local), lambda g, b: (0, 0)),
-                pl.BlockSpec((long, 128), lambda g, b: (0, 0)),
-                pl.BlockSpec((long, 128), lambda g, b: (0, 0)),
-                pl.BlockSpec((long, 128), lambda g, b: (0, 0)),
-            ],
-            out_specs=[short_spec, long_spec, long_spec],
-            scratch_shapes=[pltpu.VMEM((long, lanes), F32)] * 2,
-        ),
-        out_shape=[
-            jax.ShapeDtypeStruct((local, width), BF),
-            jax.ShapeDtypeStruct((long, width), BF),
-            jax.ShapeDtypeStruct((long, width), BF),
-        ],
-        compiler_params=pltpu.CompilerParams(vmem_limit_bytes=48 * 2**20),
-        cost_estimate=pl.CostEstimate(flops=5 * 2**30, bytes_accessed=16 * 2**20, transcendentals=4 * 2**20),
-    )(bounds, queries, keys, turned, values, mixed, grad, lse, seg_q, seg_k, cosine, sine)
-
-
 CB = 512
 HIGH = lax.Precision.HIGHEST
 
@@ -379,9 +283,12 @@
 
 
 CW = 512
-SLOTS_G, SLOTS_S, SLOTS_R, SLOTS_T, SLOTS_K = 3, 3, 4, 6, 14
+HALF = CW // 2
+SLOTS_S, SLOTS_R, SLOTS_T, SLOTS_K = 3, 4, 6, 14
 SMALL_ROWS = 112
+QKV_ROW = 48
 LAGS = (4, 7, 2)
+RING = 12
 
 
 def neighbours():
@@ -414,366 +321,511 @@
     )
 
 
-def scatter_kernel(
-    window, attn_grad, normed, ffn_grad, dq, dk, dv, mixed, pre_grad, hidden, dxw, small_ref,
-    out_qkv, out_attn, out_in, out_out, small_out, from_left, from_right,
-    xw, xa, xn, xf, gs, gkv, sbuf, rbuf, ta, tb, xra, xrb, s2a, s2b, yra, yrb, keep, zs, zrl, zrr,
-    sacc, srec, zsm,
-    x_sem, g_sem, s_sem, r_sem, t_sem, xr_sem, s2_sem, yr_sem, zs_sem, zr_sem, sm_sem, smz_sem, h_sem, credit,
+class Scatter:
+    def __init__(self, goals, product, finish, refs):
+        (self.sbuf, self.rbuf, self.ta, self.tb, self.xra, self.xrb, self.s2a, self.s2b, self.yra, self.yrb, self.keep,
+         self.zs, self.zrl, self.zrr, self.s_sem, self.r_sem, self.t_sem, self.xr_sem, self.s2_sem, self.yr_sem,
+         self.zs_sem, self.zr_sem, self.credit) = refs
+        self.goals, self.product, self.finish = goals, product, finish
+        self.count = len(goals)
+        self.dp, low, self.core, self.x, self.y, self.to_core, self.to_x, self.to_y = neighbours()
+        self.z = lax.axis_index("tensor")
+        self.nz = 4
+        self.steps = self.count + LAGS[1] + LAGS[2] * (self.nz - 1) + 1
+
+    def barrier(self):
+        entry_barrier(self.z, self.dp, (self.to_core, self.to_x, self.to_y), self.nz)
+
+    def block(self, index):
+        other, xj, yj = index // 4, index % 2, index % 4 // 2
+        core, x, y = (bit + flip - 2 * bit * flip for bit, flip in ((self.core, other), (self.x, xj), (self.y, yj)))
+        return pl.ds(pl.multiple_of((core + 2 * x + 4 * y) * 128, 128), 128)
+
+    def core_move(self, i):
+        s, r = i % SLOTS_S, i % SLOTS_R
+        return remote(self.sbuf.at[s], self.rbuf.at[r], self.s_sem.at[s], self.r_sem.at[r], self.to_core, self.z)
+
+    def ta_move(self, i):
+        t, r = i % SLOTS_T, i % RING
+        src = self.ta.at[t, pl.ds(2, 2)]
+        return remote(src, self.xra.at[r], self.t_sem.at[t, 0], self.xr_sem.at[r, 0], self.to_x, self.z)
+
+    def tb_move(self, i):
+        t, r = i % SLOTS_T, i % RING
+        src = self.tb.at[t, pl.ds(2, 2)]
+        return remote(src, self.xrb.at[r], self.t_sem.at[t, 1], self.xr_sem.at[r, 1], self.to_y, self.z)
+
+    def s2a_move(self, i):
+        r = i % RING
+        return remote(self.s2a.at[r], self.yra.at[r], self.s2_sem.at[r, 0], self.yr_sem.at[r, 0], self.to_y, self.z)
+
+    def s2b_move(self, i):
+        r = i % RING
+        return remote(self.s2b.at[r], self.yrb.at[r], self.s2_sem.at[r, 1], self.yr_sem.at[r, 1], self.to_x, self.z)
+
+    def right_move(self, i):
+        return remote(self.zs.at[i], self.zrl.at[i], self.zs_sem.at[i], self.zr_sem.at[i, 0], self.dp, self.z + 1)
+
+    def left_move(self, i):
+        return remote(self.zs.at[i], self.zrr.at[i], self.zs_sem.at[i], self.zr_sem.at[i, 1], self.dp, self.z - 1)
+
+    def stage_one(self, i):
+        if i >= SLOTS_S:
+            self.core_move(i - SLOTS_S).wait_send()
+
+        self.sbuf[i % SLOTS_S] = self.product(i, 4).reshape(4, 128, CW).astype(BF)
+        if i >= SLOTS_R:
+            pl.semaphore_wait(self.credit, 1)
+        self.core_move(i).start()
+
+    def stage_two(self, i):
+        self.core_move(i).wait_recv()
+        slot = i % SLOTS_T
+        if i >= SLOTS_T:
+            self.ta_move(i - SLOTS_T).wait_send()
+            self.tb_move(i - SLOTS_T).wait_send()
+
+        total = self.product(i, 0).reshape(4, 128, CW) + self.rbuf[i % SLOTS_R].astype(F32)
+        for j in range(4):
+            self.ta[slot, j // 2 + 2 * (j % 2)] = total[j, :, :HALF].astype(BF)
+            self.tb[slot, j] = total[j, :, HALF:].astype(BF)
+        if i + SLOTS_R < self.count:
+            where = {"dp": self.to_core, "tensor": self.z}
+            pl.semaphore_signal(self.credit, inc=1, device_id=where, device_id_type=MESH)
+        self.ta_move(i).start()
+        self.tb_move(i).start()
+
+    def stage_three(self, i):
+        slot, k, r = i % SLOTS_T, i % SLOTS_K, i % RING
+        if i >= RING:
+            self.s2a_move(i - RING).wait_send()
+            self.s2b_move(i - RING).wait_send()
+        self.ta_move(i).wait_recv()
+        self.s2a[r] = (self.ta[slot, 1].astype(F32) + self.xra[r, 1].astype(F32)).astype(BF)
+        self.s2a_move(i).start()
+        self.keep[k, :, :HALF] = self.ta[slot, 0].astype(F32) + self.xra[r, 0].astype(F32)
+        self.tb_move(i).wait_recv()
+        self.s2b[r] = (self.tb[slot, 1].astype(F32) + self.xrb[r, 1].astype(F32)).astype(BF)
+        self.s2b_move(i).start()
+        self.keep[k, :, HALF:] = self.tb[slot, 0].astype(F32) + self.xrb[r, 0].astype(F32)
+
+    def pass_on(self, i, right):
+        self.zs[i] = self.keep[i % SLOTS_K].astype(BF)
+        (self.right_move(i) if right else self.left_move(i)).start()
+
+    def stage_four(self, i):
+        k = i % SLOTS_K
+        self.s2a_move(i).wait_recv()
+        self.keep[k, :, :HALF] += self.yra[i % RING].astype(F32)
+        self.s2b_move(i).wait_recv()
+        self.keep[k, :, HALF:] += self.yrb[i % RING].astype(F32)
+        if self.goals[i] > 0:
+            pl.when(self.z == 0)(lambda: self.pass_on(i, True))
+        if self.goals[i] < self.nz - 1:
+            pl.when(self.z == self.nz - 1)(lambda: self.pass_on(i, False))
+
+    def stage_five(self, i, hop):
+        k = i % SLOTS_K
+        goal, last = self.goals[i], self.nz - 1
+        if hop <= goal:
+
+            @pl.when(self.z == hop)
+            def _():
+                self.right_move(i).wait_recv()
+                self.keep[k] += self.zrl[i].astype(F32)
+                if hop < goal:
+                    self.pass_on(i, True)
+
+        if hop <= last - goal:
+
+            @pl.when(self.z == last - hop)
+            def _():
+                self.left_move(i).wait_recv()
+                self.keep[k] += self.zrr[i].astype(F32)
+                if last - hop > goal:
+                    self.pass_on(i, False)
+
+        if hop == last:
+            pl.when(self.z == goal)(lambda: self.finish(i, self.keep.at[k]))
+
+    def late_stages(self, step):
+        lag_three, lag_four, spacing = LAGS
+        if 0 <= step - lag_three < self.count:
+            self.stage_three(step - lag_three)
+        if 0 <= step - lag_four < self.count:
+            self.stage_four(step - lag_four)
+        for hop in range(1, self.nz):
+            i = step - lag_four - spacing * hop
+            if 0 <= i < self.count:
+                self.stage_five(i, hop)
+
+    def drain(self):
+        for i in range(self.count):
+            if i >= self.count - SLOTS_S:
+                self.core_move(i).wait_send()
+            if i >= self.count - SLOTS_T:
+                self.ta_move(i).wait_send()
+                self.tb_move(i).wait_send()
+            if i >= self.count - RING:
+                self.s2a_move(i).wait_send()
+                self.s2b_move(i).wait_send()
+            pl.when(self.z < self.goals[i])(lambda i=i: self.right_move(i).wait_send())
+            pl.when(self.z > self.goals[i])(lambda i=i: self.left_move(i).wait_send())
+
+
+def scatter_scratch(n):
+    dma = pltpu.SemaphoreType.DMA
+    slots_k = min(SLOTS_K, n)
+    return [
+        pltpu.VMEM((SLOTS_S, 4, 128, CW), BF),
+        pltpu.VMEM((SLOTS_R, 4, 128, CW), BF),
+        pltpu.VMEM((SLOTS_T, 4, 128, HALF), BF),
+        pltpu.VMEM((SLOTS_T, 4, 128, HALF), BF),
+        pltpu.VMEM((RING, 2, 128, HALF), BF),
+        pltpu.VMEM((RING, 2, 128, HALF), BF),
+        pltpu.VMEM((RING, 128, HALF), BF),
+        pltpu.VMEM((RING, 128, HALF), BF),
+        pltpu.VMEM((RING, 128, HALF), BF),
+        pltpu.VMEM((RING, 128, HALF), BF),
+        pltpu.VMEM((slots_k, 128, CW), F32),
+        pltpu.VMEM((n, 128, CW), BF),
+        pltpu.VMEM((n, 128, CW), BF),
+        pltpu.VMEM((n, 128, CW), BF),
+        dma((SLOTS_S,)),
+        dma((SLOTS_R,)),
+        dma((SLOTS_T, 2)),
+        dma((RING, 2)),
+        dma((RING, 2)),
+        dma((RING, 2)),
+        dma((n,)),
+        dma((n, 2)),
+        pltpu.SemaphoreType.REGULAR,
+    ]
+
+
+CHUNKS = (
+    [("out", i) for i in range(4)] + [("qk", 0), ("vm", 0)] + [("out", i) for i in range(4, 8)] + [("qk", 1), ("vm", 1)]
+    + [("in", i) for i in range(3)] + [("qk", 2), ("vm", 2)] + [("in", i) for i in range(3, 6)] + [("qk", 3), ("vm", 3)]
+    + [("in", i) for i in range(6, 8)]
+)
+ATTEND_AT = {0: (0, 0), 3: (0, 1), 6: (1, 0), 9: (1, 1), 12: (2, 0), 14: (2, 1), 17: (3, 0), 19: (3, 1)}
+TOKENS_AT = {
+    4: ((0, 1),), 7: ((0, 0),), 8: ((0, 2),), 10: ((1, 1),), 12: ((1, 0),), 13: ((1, 2),), 15: ((2, 1),),
+    17: ((2, 0),), 18: ((2, 2),), 20: ((3, 0), (3, 2)), 22: ((3, 1),),
+}
+HALO_AT = {21: 0, 23: 1, 25: 2, 27: 3}
+HEADS_AT = {2: 1, 7: 2, 13: 3}
+SMALL_AT = {20: 0, 22: 1, 24: 2, 26: 3, 30: 4}
+INPUTS_AT = {0: 0, 4: 1, 5: 2, 12: 3}
+WIDE = [i for i, (kind, part) in enumerate(CHUNKS) if kind in ("out", "in")]
+
+
+def last_kernel(
+    window, attn_grad, normed, ffn_grad, hidden, pre_grad, query, key, value, mixed, mixed_grad, qkv_all, resid_grad,
+    lse_ref, segq_ref, segk_ref, cos_ref, sin_ref, small_ref,
+    out_qkv, out_attn, out_in, out_out, small_out, token_grad,
+    xw, xa, xn, xf, gs, q_v, g_v, m_v, k_v, v_v, weight, dk_acc, dv_acc, dq_b, dk_b, dv_b, send_l, send_r, from_l, from_r,
+    sums, sacc, srec, zsm, x_sem, g_sem, h_sem, w_sem, sm_sem, smz_sem, e_sem, *refs,
 ):
-    dp, low, core, x, y, to_core, to_x, to_y = neighbours()
-    z = lax.axis_index("tensor")
-    nz = 4
-    chunks = [("out", i) for i in range(8)] + [("in", i) for i in range(8)] + [("qa", i) for i in range(8)]
-    count = len(chunks)
-    local = attn_grad.shape[0]
-    has_l = z > 0
-    has_r = z < nz - 1
-
-    x_loads = [
-        pltpu.make_async_copy(src, dst, x_sem.at[index])
-        for index, (src, dst) in enumerate(((ffn_grad, xf), (normed, xn), (window, xw), (attn_grad, xa)))
-    ]
-    for load in x_loads:
-        load.start()
-
-    def g_loads(index):
-        kind, part = chunks[index]
-        slot = index % SLOTS_G
-        if kind != "qa":
-            source = hidden if kind == "out" else pre_grad
-            return [pltpu.make_async_copy(source.at[:, pl.ds(part * CW, CW)], gs.at[slot], g_sem.at[slot, 0])]
-        columns = pl.ds((part // 2) * 256, 256)
-        one, many = (dq, dk) if part % 2 == 0 else (mixed, dv)
+    local = attn_grad.shape[1]
+    turned = ((ffn_grad, xf), (window, xw), (attn_grad, xa), (normed, xn))
+    resid_load = pltpu.make_async_copy(resid_grad, token_grad, x_sem.at[4, 0])
+
+    def x_loads(which):
+        source, target = turned[which]
         return [
-            pltpu.make_async_copy(one.at[:, columns], gs.at[slot, :, pl.ds(0, 256)], g_sem.at[slot, 0]),
-            pltpu.make_async_copy(many.at[:, columns], gkv.at[slot], g_sem.at[slot, 1]),
+            pltpu.make_async_copy(source.at[plan.block(index), :], target.at[index], x_sem.at[which, index])
+            for index in range(8)
         ]
 
-    for index in range(2):
-        for load in g_loads(index):
-            load.start()
-
-    entry_barrier(z, dp, (to_core, to_x, to_y), nz)
-
-    halo_l = remote(dxw.at[pl.ds(0, local)], from_right, h_sem.at[0], h_sem.at[1], dp, z - 1)
-    halo_r = remote(dxw.at[pl.ds(2 * local, local)], from_left, h_sem.at[2], h_sem.at[3], dp, z + 1)
-
-    peers = (to_core, to_x, to_y)
-
-    def small_moves(stage):
+    def g_load(order):
+        kind, part = CHUNKS[WIDE[order]]
+        source = hidden if kind == "out" else pre_grad
+        return pltpu.make_async_copy(source.at[:, pl.ds(part * CW, CW)], gs.at[order % 3], g_sem.at[order % 3])
+
+    def head_loads(shard):
+        columns, slot = pl.ds(shard * 256, 256), shard % 2
+        pairs = ((query, q_v), (mixed_grad, g_v), (mixed, m_v), (key, k_v), (value, v_v))
         return [
-            remote(sacc.at[stage], srec.at[stage], sm_sem.at[stage, 0], sm_sem.at[stage, 1], peers[stage], z),
+            pltpu.make_async_copy(source.at[:, columns], target.at[slot], h_sem.at[slot, index])
+            for index, (source, target) in enumerate(pairs)
         ]
 
-    def small_z_moves(step):
-        peer = lax.rem(z + step, nz)
-        return [
-            remote(sacc.at[3], zsm.at[step - 1], smz_sem.at[step - 1, 0], smz_sem.at[step - 1, 1], dp, peer),
-        ]
+    def weight_load(shard):
+        columns = pl.ds(shard * 256, 256)
+        return pltpu.make_async_copy(qkv_all.at[:, :, columns], weight.at[shard % 2], w_sem.at[shard % 2])
+
+    def product(i, start):
+        kind, part = CHUNKS[i]
+        four = slice(start, start + 4)
+        if kind in ("out", "in"):
+            left = (xf if kind == "out" else xn)[four].reshape(512, local)
+            return dot(left, gs[WIDE.index(i) % 3])
+        wide = xw[four].reshape(512, 3 * local)
+        if kind == "qk":
+            parts = dot(wide[:, local : 2 * local], dq_b[...]), dot(wide, dk_b[...])
+        else:
+            parts = dot(wide, dv_b[...]), dot(xa[four].reshape(512, local), m_v[part % 2])
+        return jnp.concatenate(parts, axis=1)
+
+    def finish(i, kept):
+        kind, part = CHUNKS[i]
+        if kind == "qk":
+            out_qkv[:, 0:512] = kept[...]
+        elif kind == "vm":
+            out_qkv[:, 512:768] = kept[:, 0:256]
+            out_attn[...] = kept[:, 256:512].T
+        elif kind == "in":
+            out_in[:, pl.ds((part % 2) * CW, CW)] = kept[...]
+        else:
+            out_out[pl.ds((part % 2) * CW, CW), :] = kept[...].T
+
+    goals = [part if kind in ("qk", "vm") else part // 2 for kind, part in CHUNKS]
+    plan = Scatter(goals, product, finish, refs)
+    z, dp, nz = plan.z, plan.dp, plan.nz
+    has_l, has_r = z > 0, z < nz - 1
+    for copy in (
+        *x_loads(0), g_load(0), *head_loads(0), g_load(1), *x_loads(1), g_load(2), *x_loads(2), *x_loads(3), resid_load
+    ):
+        copy.start()
+    weight_load(0).start()
+    plan.barrier()
+
+    def to_left(piece):
+        at = pl.ds(piece * 128, 128)
+        return remote(send_l.at[at], from_r.at[at], e_sem.at[piece, 0], e_sem.at[piece, 1], dp, z - 1)
+
+    def to_right(piece):
+        at = pl.ds(piece * 128, 128)
+        return remote(send_r.at[at], from_l.at[at], e_sem.at[piece, 2], e_sem.at[piece, 3], dp, z + 1)
+
+    peers = (plan.to_core, plan.to_x, plan.to_y)
+
+    def small_move(stage):
+        return remote(sacc.at[stage], srec.at[stage], sm_sem.at[stage, 0], sm_sem.at[stage, 1], peers[stage], z)
+
+    def small_z_move(step):
+        sems = smz_sem.at[step - 1, 0], smz_sem.at[step - 1, 1]
+        return remote(sacc.at[3], zsm.at[step - 1], *sems, dp, lax.rem(z + step, nz))
 
     def small_stage(stage):
         if stage == 0:
             sacc[0] = small_ref[...]
+            sacc[0, QKV_ROW : QKV_ROW + 24, :] = sums[...]
         if 1 <= stage <= 3:
-            for move in small_moves(stage - 1):
-                move.wait_recv()
+            small_move(stage - 1).wait_recv()
             sacc[stage] = sacc[stage - 1] + srec[stage - 1]
         if stage <= 2:
-            for move in small_moves(stage):
-                move.start()
+            small_move(stage).start()
         if stage == 3:
             for step in range(1, nz):
-                for move in small_z_moves(step):
-                    move.start()
+                small_z_move(step).start()
         if stage == 4:
             for step in range(1, nz):
-                for move in small_z_moves(step):
-                    move.wait_recv()
+                small_z_move(step).wait_recv()
             total = None
             for owner in range(nz):
-                value = jnp.where(z == owner, sacc[3], 0.0)
+                made = jnp.where(z == owner, sacc[3], 0.0)
                 for step in range(1, nz):
-                    value = jnp.where(lax.rem(z - step + nz, nz) == owner, zsm[step - 1], value)
-                total = value if total is None else total + value
+                    made = jnp.where(lax.rem(z - step + nz, nz) == owner, zsm[step - 1], made)
+                total = made if total is None else total + made
             small_out[...] = total
 
-    def block_columns(j, core_bit):
-        xj = lax.rem(j, 2)
-        yj = j // 2
-        block = core_bit + 2 * (x + xj - 2 * x * xj) + 4 * (y + yj - 2 * y * yj)
-        return pl.ds(pl.multiple_of(block * 128, 128), 128)
-
-    def product(index, j, core_bit):
-        kind, part = chunks[index]
-        slot = index % SLOTS_G
-        at = block_columns(j, core_bit)
-        if kind == "out":
-            return dot(xf[:, at], gs[slot], 0, 0)
-        if kind == "in":
-            return dot(xn[:, at], gs[slot], 0, 0)
-        one = xw[pl.ds(local, local), at] if part % 2 == 0 else xa[:, at]
-        return jnp.concatenate(
-            [dot(one, gs[slot, :, 0:256], 0, 0), dot(xw[:, at], gkv[slot], 0, 0)], axis=1
-        )
-
-    def core_move(index):
-        return remote(
-            sbuf.at[index % SLOTS_S], rbuf.at[index % SLOTS_R], s_sem.at[index % SLOTS_S], r_sem.at[index % SLOTS_R],
-            to_core, z,
-        )
-
-    half = CW // 2
-
-    def ta_move(index):
-        slot = index % SLOTS_T
-        return remote(ta.at[slot, pl.ds(2, 2)], xra.at[index], t_sem.at[slot, 0], xr_sem.at[index, 0], to_x, z)
-
-    def tb_move(index):
-        slot = index % SLOTS_T
-        return remote(tb.at[slot, pl.ds(2, 2)], xrb.at[index], t_sem.at[slot, 1], xr_sem.at[index, 1], to_y, z)
-
-    def s2a_move(index):
-        return remote(s2a.at[index], yra.at[index], s2_sem.at[index, 0], yr_sem.at[index, 0], to_y, z)
-
-    def s2b_move(index):
-        return remote(s2b.at[index], yrb.at[index], s2_sem.at[index, 1], yr_sem.at[index, 1], to_x, z)
-
-    def right_move(index):
-        return remote(zs.at[index], zrl.at[index], zs_sem.at[index], zr_sem.at[index, 0], dp, z + 1)
-
-    def left_move(index):
-        return remote(zs.at[index], zrr.at[index], zs_sem.at[index], zr_sem.at[index, 1], dp, z - 1)
-
-    def stage_one(index):
-        kind, part = chunks[index]
-        if index == 0:
-            x_loads[0].wait()
-        if kind == "in" and part == 0:
-            x_loads[1].wait()
-        if kind == "qa" and part == 0:
-            x_loads[2].wait()
-            x_loads[3].wait()
-        for load in g_loads(index):
-            load.wait()
-        if index >= SLOTS_S:
-            core_move(index - SLOTS_S).wait_send()
-
-        def body(j, unused):
-            sbuf[index % SLOTS_S, j] = product(index, j, 1 - core).astype(BF)
+    head_row = lax.broadcasted_iota(jnp.int32, (8, 128), 0)
+    head_lane = lax.broadcasted_iota(jnp.int32, (8, 128), 1) // 64
+    chosen = jnp.where(head_row == head_lane, 1.0, 0.0)
+    groups = (0, 128)
+
+    def attend_part(shard, block):
+        slot = shard % 2
+        if block == 0:
+            for load in head_loads(shard):
+                load.wait()
+            dk_acc[...] = jnp.zeros_like(dk_acc)
+            dv_acc[...] = jnp.zeros_like(dv_acc)
+        rows = slice(block * BACK_ROWS, (block + 1) * BACK_ROWS)
+        queries, grads, turned_q, turned_g, deltas, logs = [], [], [], [], [], []
+        for group, at in enumerate(groups):
+            lanes = slice(at, at + 128)
+            scaled = q_v[slot, rows, lanes] * jnp.asarray(SCALE, BF)
+            grad = g_v[slot, rows, lanes]
+            queries.append(split_pair(scaled))
+            grads.append(split_pair(grad))
+            turned_q.append(split_pair(turn(scaled), 0))
+            turned_g.append(split_pair(turn(grad), 0))
+            delta = dot(chosen, m_v[slot, rows, lanes].astype(F32) * grad.astype(F32), 1, 1, lax.Precision.HIGHEST)
+            deltas.append((delta[0:1], delta[1:2]))
+            first_head = 4 * shard + 2 * group
+            logs.append([lse_ref[first_head + head : first_head + head + 1, rows] for head in range(2)])
+        seg_q = segq_ref[0:1, rows]
+
+        def body(index, carry):
+            keys_at = pl.ds(pl.multiple_of(index * BK, BK), BK)
+            live = segk_ref[keys_at, 0:1] == seg_q
+            made = []
+            for group, at in enumerate(groups):
+                lanes = slice(at, at + 128)
+                keys = k_v[slot, keys_at, lanes]
+                values = v_v[slot, keys_at, lanes]
+                turned = turn(keys)
+                dk, dv = 0.0, 0.0
+                for head in range(2):
+                    scores = jnp.where(live, dot(keys, turned_q[group][head]), -1e9)
+                    probs = jnp.exp(scores - logs[group][head])
+                    score_low = (probs * (dot(values, turned_g[group][head]) - deltas[group][head])).astype(BF)
+                    made.append(carry[2 * group + head] + dot(turned, score_low))
+                    dk = dk + dot(score_low, queries[group][head])
+                    dv = dv + dot(probs.astype(BF), grads[group][head])
+                dk_acc[keys_at, lanes] += dk
+                dv_acc[keys_at, lanes] += dv
+            return tuple(made)
+
+        reach = local // BK * 2 + 1
+        start = (jnp.zeros((128, BACK_ROWS), F32),) * 4
+        done = lax.fori_loop(block, block + reach, body, start)
+        at_window = slice(local + block * BACK_ROWS, local + (block + 1) * BACK_ROWS)
+        for group, at in enumerate(groups):
+            grad = jnp.concatenate([done[2 * group][0:64], done[2 * group + 1][64:128]], axis=0).T * SCALE
+            back = rotate_lanes(grad, cos_ref[at_window, :], -sin_ref[at_window, :])
+            dq_b[rows, at : at + 128] = back.astype(BF)
+        if block == local // BACK_ROWS - 1:
+            dk_b[...] = rotate_lanes(dk_acc[...], cos_ref[...], -sin_ref[...]).astype(BF)
+            dv_b[...] = dv_acc[...].astype(BF)
+            for kind, ref in enumerate((dq_b, dk_b, dv_b)):
+                total = jnp.sum(ref[...].astype(F32), axis=0, keepdims=True)
+                row = 8 * kind + 2 * shard
+                sums[row : row + 1, :] = total[:, 0:128]
+                sums[row + 1 : row + 2, :] = total[:, 128:256]
+
+    def token_part(shard, part):
+        slot = shard % 2
+        if part == (0 if shard == 3 else 1):
+            weight_load(shard).wait()
+            if shard + 1 < 4:
+                weight_load(shard + 1).start()
+        if part == 1 and shard == 0:
+            resid_load.wait()
+
+        rows = slice(part * local, part * local + local)
+
+        def body(index, unused):
+            at = pl.ds(pl.multiple_of(index * 256, 256), 256)
+            grad = dot(dk_b[rows, :], weight[slot, 1, at, :], 1, 1) + dot(dv_b[rows, :], weight[slot, 2, at, :], 1, 1)
+            if part == 1:
+                token_grad[:, at] += grad + dot(dq_b[...], weight[slot, 0, at, :], 1, 1)
+            else:
+                target = send_l if part == 0 else send_r
+                target[:, at] = (grad if shard == 0 else grad + target[:, at].astype(F32)).astype(BF)
             return unused
 
-        lax.fori_loop(0, 4, body, 0)
-        if index >= SLOTS_R:
-            pl.semaphore_wait(credit, 1)
-        core_move(index).start()
-
-    def stage_two(index):
-        core_move(index).wait_recv()
-        slot = index % SLOTS_T
-        if index >= SLOTS_T:
-            ta_move(index - SLOTS_T).wait_send()
-            tb_move(index - SLOTS_T).wait_send()
-
-        def body(j, unused):
-            total = product(index, j, core) + rbuf[index % SLOTS_R, j].astype(F32)
-            ta[slot, j // 2 + 2 * lax.rem(j, 2)] = total[:, :half].astype(BF)
-            tb[slot, j] = total[:, half:].astype(BF)
-            return unused
-
-        lax.fori_loop(0, 4, body, 0)
-        if index + SLOTS_R < count:
-            pl.semaphore_signal(credit, inc=1, device_id={"dp": to_core, "tensor": z}, device_id_type=MESH)
-        ta_move(index).start()
-        tb_move(index).start()
-
-    def stage_three(index):
-        slot = index % SLOTS_T
-        kslot = index % SLOTS_K
-        ta_move(index).wait_recv()
-        s2a[index] = (ta[slot, 1].astype(F32) + xra[index, 1].astype(F32)).astype(BF)
-        s2a_move(index).start()
-        keep[kslot, :, :half] = ta[slot, 0].astype(F32) + xra[index, 0].astype(F32)
-        tb_move(index).wait_recv()
-        s2b[index] = (tb[slot, 1].astype(F32) + xrb[index, 1].astype(F32)).astype(BF)
-        s2b_move(index).start()
-        keep[kslot, :, half:] = tb[slot, 0].astype(F32) + xrb[index, 0].astype(F32)
-
-    def stage_four(index):
-        kslot = index % SLOTS_K
-        goal = chunks[index][1] // 2
-        s2a_move(index).wait_recv()
-        keep[kslot, :, :half] += yra[index].astype(F32)
-        s2b_move(index).wait_recv()
-        keep[kslot, :, half:] += yrb[index].astype(F32)
-        if goal > 0:
-
-            @pl.when(z == 0)
-            def _():
-                zs[index] = keep[kslot].astype(BF)
-                right_move(index).start()
-
-        if goal < nz - 1:
-
-            @pl.when(z == nz - 1)
-            def _():
-                zs[index] = keep[kslot].astype(BF)
-                left_move(index).start()
-
-    def stage_five(index, hop):
-        kslot = index % SLOTS_K
-        kind, part = chunks[index]
-        goal = part // 2
-        if hop <= goal:
-
-            @pl.when(z == hop)
-            def _():
-                right_move(index).wait_recv()
-                keep[kslot] += zrl[index].astype(F32)
-                if hop < goal:
-                    zs[index] = keep[kslot].astype(BF)
-                    right_move(index).start()
-
-        if hop <= nz - 1 - goal:
-
-            @pl.when(z == nz - 1 - hop)
-            def _():
-                left_move(index).wait_recv()
-                keep[kslot] += zrr[index].astype(F32)
-                if nz - 1 - hop > goal:
-                    zs[index] = keep[kslot].astype(BF)
-                    left_move(index).start()
-
-        if hop == nz - 1:
-
-            @pl.when(z == goal)
-            def _():
-                if kind == "qa":
-                    if part % 2 == 0:
-                        out_qkv[:, 0:512] = keep[kslot]
-                    else:
-                        out_attn[...] = keep[kslot, :, 0:256]
-                        out_qkv[:, 512:768] = keep[kslot, :, 256:512]
-                else:
-                    target = out_in if kind == "in" else out_out
-                    target[:, pl.ds((part % 2) * CW, CW)] = keep[kslot]
-
-    lag_three, lag_four, spacing = LAGS
-    for step in range(count + lag_four + spacing * (nz - 1) + 1):
-        if step < count:
-            stage_one(step)
-        if step == 0:
-            small_stage(0)
-            pl.when(has_l)(lambda: halo_l.start())
-            pl.when(has_r)(lambda: halo_r.start())
-        if 0 <= step - 1 < count:
-            stage_two(step - 1)
-        if step + 2 < count:
-            for load in g_loads(step + 2):
+        lax.fori_loop(0, weight.shape[2] // 256, body, 0)
+
+    def add_halo(copy, there, source):
+        @pl.when(there)
+        def _():
+            for piece in range(local // 128):
+                copy(piece).wait_recv()
+                rows = slice(piece * 128, piece * 128 + 128)
+                token_grad[rows, :] += source[rows, :].astype(F32)
+
+    for step in range(plan.steps):
+        if step in INPUTS_AT:
+            for load in x_loads(INPUTS_AT[step]):
+                load.wait()
+        if step < plan.count:
+            if step in WIDE:
+                g_load(WIDE.index(step)).wait()
+            plan.stage_one(step)
+        if 0 <= step - 1 < plan.count:
+            plan.stage_two(step - 1)
+            if step - 1 in WIDE and WIDE.index(step - 1) + 3 < len(WIDE):
+                g_load(WIDE.index(step - 1) + 3).start()
+        if step in HEADS_AT:
+            for load in head_loads(HEADS_AT[step]):
                 load.start()
-        if step in (2, 4, 6, 8):
-            small_stage(step // 2)
-        if 0 <= step - lag_three < count:
-            stage_three(step - lag_three)
-        if 0 <= step - lag_four < count:
-            stage_four(step - lag_four)
-        for hop in range(1, nz):
-            index = step - lag_four - spacing * hop
-            if 0 <= index < count:
-                stage_five(index, hop)
-
-    for index in range(count):
-        goal = chunks[index][1] // 2
-        if index >= count - SLOTS_S:
-            core_move(index).wait_send()
-        if index >= count - SLOTS_T:
-            ta_move(index).wait_send()
-            tb_move(index).wait_send()
-        s2a_move(index).wait_send()
-        s2b_move(index).wait_send()
-        pl.when(z < goal)(lambda index=index: right_move(index).wait_send())
-        pl.when(z > goal)(lambda index=index: left_move(index).wait_send())
+        plan.late_stages(step)
+        if step in ATTEND_AT:
+            attend_part(*ATTEND_AT[step])
+        for piece in TOKENS_AT.get(step, ()):
+            token_part(*piece)
+        if step in HALO_AT:
+            pl.when(has_l)(lambda step=step: to_left(HALO_AT[step]).start())
+            pl.when(has_r)(lambda step=step: to_right(HALO_AT[step]).start())
+        if step in SMALL_AT:
+            small_stage(SMALL_AT[step])
+    add_halo(to_right, has_l, from_l)
+    add_halo(to_left, has_r, from_r)
+    plan.drain()
     for stage in range(3):
-        for move in small_moves(stage):
-            move.wait_send()
+        small_move(stage).wait_send()
     for step in range(1, nz):
-        for move in small_z_moves(step):
-            move.wait_send()
-
-    @pl.when(has_l)
-    def _():
-        halo_l.wait_send()
-        halo_r.wait_recv()
-
-    @pl.when(has_r)
-    def _():
-        halo_r.wait_send()
-        halo_l.wait_recv()
-
-
-def scatter(window, attn_grad, normed, ffn_grad, dq, dk, dv, mixed, pre_grad, hidden, dxw, small):
-    local, width = attn_grad.shape
-    long = window.shape[0]
+        small_z_move(step).wait_send()
+    for piece in range(local // 128):
+        pl.when(has_l)(lambda piece=piece: to_left(piece).wait_send())
+        pl.when(has_r)(lambda piece=piece: to_right(piece).wait_send())
+
+
+def last(
+    window, attn_grad, normed, ffn_grad, hidden, pre_grad, query, key, value, mixed, mixed_grad, qkv_all, resid_grad,
+    lse, seg_q, seg_k, cosine, sine, small,
+):
+    width, local = attn_grad.shape
+    long = window.shape[1]
+    shape = jax.ShapeDtypeStruct
     dma = pltpu.SemaphoreType.DMA
-    n = 24
-    half = CW // 2
-    shape = jax.ShapeDtypeStruct
     return pl.pallas_call(
-        scatter_kernel,
-        in_specs=hbm_specs(11) + vmem_specs(1),
-        out_specs=vmem_specs(5) + hbm_specs(2),
+        last_kernel,
+        in_specs=hbm_specs(13) + vmem_specs(6),
+        out_specs=vmem_specs(6),
         out_shape=[
             shape((128, 768), F32),
-            shape((128, 256), F32),
+            shape((256, 128), F32),
             shape((128, 1024), F32),
-            shape((128, 1024), F32),
+            shape((1024, 128), F32),
             shape(small.shape, F32),
-            shape((local, width), BF),
-            shape((local, width), BF),
+            shape((local, width), F32),
         ],
         scratch_shapes=[
-            pltpu.VMEM((long, width), BF),
+            pltpu.VMEM((8, 128, long), BF),
+            pltpu.VMEM((8, 128, local), BF),
+            pltpu.VMEM((8, 128, local), BF),
+            pltpu.VMEM((8, 128, local), BF),
+            pltpu.VMEM((3, local, CW), BF),
+            pltpu.VMEM((2, local, 256), BF),
+            pltpu.VMEM((2, local, 256), BF),
+            pltpu.VMEM((2, local, 256), BF),
+            pltpu.VMEM((2, long, 256), BF),
+            pltpu.VMEM((2, long, 256), BF),
+            pltpu.VMEM((2, 3, width, 256), BF),
+            pltpu.VMEM((long, 256), F32),
+            pltpu.VMEM((long, 256), F32),
+            pltpu.VMEM((local, 256), BF),
+            pltpu.VMEM((long, 256), BF),
+            pltpu.VMEM((long, 256), BF),
             pltpu.VMEM((local, width), BF),
             pltpu.VMEM((local, width), BF),
             pltpu.VMEM((local, width), BF),
-            pltpu.VMEM((SLOTS_G, local, CW), BF),
-            pltpu.VMEM((SLOTS_G, long, 256), BF),
-            pltpu.VMEM((SLOTS_S, 4, 128, CW), BF),
-            pltpu.VMEM((SLOTS_R, 4, 128, CW), BF),
-            pltpu.VMEM((SLOTS_T, 4, 128, half), BF),
-            pltpu.VMEM((SLOTS_T, 4, 128, half), BF),
-            pltpu.VMEM((n, 2, 128, half), BF),
-            pltpu.VMEM((n, 2, 128, half), BF),
-            pltpu.VMEM((n, 128, half), BF),
-            pltpu.VMEM((n, 128, half), BF),
-            pltpu.VMEM((n, 128, half), BF),
-            pltpu.VMEM((n, 128, half), BF),
-            pltpu.VMEM((SLOTS_K, 128, CW), F32),
-            pltpu.VMEM((n, 128, CW), BF),
-            pltpu.VMEM((n, 128, CW), BF),
-            pltpu.VMEM((n, 128, CW), BF),
+            pltpu.VMEM((local, width), BF),
+            pltpu.VMEM((24, 128), F32),
             pltpu.VMEM((4,) + small.shape, F32),
             pltpu.VMEM((3,) + small.shape, F32),
             pltpu.VMEM((3,) + small.shape, F32),
-            dma((4,)),
-            dma((SLOTS_G, 2)),
-            dma((SLOTS_S,)),
-            dma((SLOTS_R,)),
-            dma((SLOTS_T, 2)),
-            dma((n, 2)),
-            dma((n, 2)),
-            dma((n, 2)),
-            dma((n,)),
-            dma((n, 2)),
+            dma((5, 8)),
+            dma((3,)),
+            dma((2, 5)),
+            dma((2,)),
             dma((3, 2)),
             dma((3, 2)),
-            dma((4,)),
-            pltpu.SemaphoreType.REGULAR,
-        ],
+            dma((4, 4)),
+        ]
+        + scatter_scratch(len(CHUNKS)),
         compiler_params=pltpu.CompilerParams(
-            collective_id=2, has_side_effects=True, vmem_limit_bytes=VMEM_BIG
+            collective_id=2, has_side_effects=True, vmem_limit_bytes=62 * 2**20
         ),
-    )(window, attn_grad, normed, ffn_grad, dq, dk, dv, mixed, pre_grad, hidden, dxw, small)
+    )(
+        window, attn_grad, normed, ffn_grad, hidden, pre_grad, query, key, value, mixed, mixed_grad, qkv_all, resid_grad,
+        lse, seg_q, seg_k, cosine, sine, small,
+    )
 
 
 def shard_rows(kind, ref):
@@ -924,8 +976,8 @@
 
 def first_kernel(
     qkv_src, attn_src, in_src, tokens, bias, cos_ref, sin_ref,
-    qkv_out, attn_out, in_out, window_out, bias_all, query_out, key_out, key_t_out, value_out, value_t_out,
-    weight, xw, query, key, key_t, value, value_t, stage_a, stage_i,
+    qkv_out, attn_out, in_out, window_out, bias_all, query_out, key_out, value_out, value_t_out,
+    weight, xw, turned, query, key, value, value_t, stage_a, stage_i,
     z_send, z_recv, p_send, p_recv, l_sem, h_sem, b_sem, o_sem,
 ):
     plan = Gather(
@@ -962,16 +1014,15 @@
     i_out.start()
 
     weight_out = pltpu.make_async_copy(weight, qkv_out, o_sem.at[0])
-    window_copy = pltpu.make_async_copy(xw, window_out, o_sem.at[1])
 
     def outputs(shard):
         columns = pl.ds(shard * 256, 256)
         return [
+            pltpu.make_async_copy(turned.at[columns, :], window_out.at[columns, :], o_sem.at[1 + 5 * shard]),
             pltpu.make_async_copy(query.at[:, columns], query_out.at[:, columns], o_sem.at[2 + 5 * shard]),
             pltpu.make_async_copy(key.at[:, columns], key_out.at[:, columns], o_sem.at[3 + 5 * shard]),
-            pltpu.make_async_copy(key_t.at[columns, :], key_t_out.at[columns, :], o_sem.at[4 + 5 * shard]),
-            pltpu.make_async_copy(value.at[:, columns], value_out.at[:, columns], o_sem.at[5 + 5 * shard]),
-            pltpu.make_async_copy(value_t.at[columns, :], value_t_out.at[columns, :], o_sem.at[6 + 5 * shard]),
+            pltpu.make_async_copy(value.at[:, columns], value_out.at[:, columns], o_sem.at[4 + 5 * shard]),
+            pltpu.make_async_copy(value_t.at[columns, :], value_t_out.at[columns, :], o_sem.at[5 + 5 * shard]),
         ]
 
     def ready():
@@ -987,7 +1038,6 @@
         pl.when(plan.has_r)(lambda: to_left.wait_recv())
         pl.when(jnp.logical_not(plan.has_l))(lambda: fill_l.wait())
         pl.when(jnp.logical_not(plan.has_r))(lambda: fill_r.wait())
-        window_copy.start()
 
     def compute(shard, part):
         columns = slice(shard * 256, shard * 256 + 256)
@@ -999,11 +1049,11 @@
             add = [bias_all[shard, 2 * kind + i : 2 * kind + i + 1, :].astype(F32) for i in range(2)]
             return dot(window, weight[kind, :, columns]) + jnp.concatenate(add, axis=1)
 
+        turned[columns, rows] = turn(window[:, columns])
         if part == 1:
             query[:, columns] = rotate_lanes(made(0), cosine, sine).astype(BF)
         keys = rotate_lanes(made(1), cosine, sine)
         key[rows, columns] = keys.astype(BF)
-        key_t[columns, rows] = keys.T.astype(BF)
         values = made(2)
         value[rows, columns] = values.astype(BF)
         value_t[columns, rows] = values.T.astype(BF)
@@ -1033,7 +1083,6 @@
     pl.when(plan.has_l)(lambda: to_left.wait_send())
     pl.when(plan.has_r)(lambda: to_right.wait_send())
     weight_out.wait()
-    window_copy.wait()
     for shard in range(4):
         for copy in outputs(shard):
             copy.wait()
@@ -1047,32 +1096,31 @@
     return pl.pallas_call(
         first_kernel,
         in_specs=hbm_specs(4) + vmem_specs(3),
-        out_specs=hbm_specs(4) + vmem_specs(1) + hbm_specs(5),
+        out_specs=hbm_specs(4) + vmem_specs(1) + hbm_specs(4),
         out_shape=[
             shape((3, width, width), BF),
             shape((width, width), BF),
             shape((width, 4 * width), BF),
-            shape((long, width), BF),
+            shape((width, long), BF),
             shape((4,) + bias.shape, BF),
             shape((local, width), BF),
             shape((long, width), BF),
-            shape((width, long), BF),
             shape((long, width), BF),
             shape((width, long), BF),
         ],
         scratch_shapes=[
             pltpu.VMEM((3, width, width), BF),
             pltpu.VMEM((long, width), BF),
+            pltpu.VMEM((width, long), BF),
             pltpu.VMEM((local, width), BF),
             pltpu.VMEM((long, width), BF),
-            pltpu.VMEM((width, long), BF),
             pltpu.VMEM((long, width), BF),
             pltpu.VMEM((width, long), BF),
             pltpu.VMEM(attn_weight.shape, BF),
             pltpu.VMEM(in_weight.shape, BF),
         ]
         + gather_sems(3)
-        + [dma((5,)), dma((7,)), dma((2, 3)), dma((22,))],
+        + [dma((5,)), dma((7,)), dma((2, 3)), dma((21,))],
         compiler_params=pltpu.CompilerParams(collective_id=0, has_side_effects=True, vmem_limit_bytes=VMEM_BIG),
     )(qkv_weight, attn_weight, in_weight, tokens, bias, cosine, sine)
 
@@ -1093,7 +1141,7 @@
 def second_kernel(
     out_src, mixed, tokens, attn_all, in_all, in_bias, vectors, proj_weight,
     out_all, hidden_out, slope_out, normed_out, unit_one_out, scale_one, output_out, unit_two_out, scale_two, emb_all,
-    weight, mixed_v, tokens_v, attn_v, in_v, hidden, slope, normed, normed_low, total, unit, output_low, unit_two, emb,
+    weight, mixed_v, tokens_v, attn_v, in_v, hidden, slope, normed, normed_low, normed_t, total, unit, output_low, unit_two, emb,
     z_send, z_recv, p_send, p_recv, l_sem, i_sem, o_sem, e_sem,
 ):
     plan = Gather(("out0", "out1"), (out_src, out_src), (weight, weight), z_send, z_recv, p_send, p_recv, 4)
@@ -1121,7 +1169,7 @@
     saves = [
         pltpu.make_async_copy(src, dst, o_sem.at[index])
         for index, (src, dst) in enumerate(
-            ((hidden, hidden_out), (slope, slope_out), (normed_low, normed_out), (unit, unit_one_out),
+            ((hidden, hidden_out), (slope, slope_out), (normed_t, normed_out), (unit, unit_one_out),
              (output_low, output_out), (unit_two, unit_two_out), (weight, out_all))
         )
     ]
@@ -1138,6 +1186,7 @@
         full = made * vectors[2:3, :] + vectors[4:5, :]
         normed[rows, :] = full
         normed_low[rows, :] = full.astype(BF)
+        normed_t[:, rows] = full.T.astype(BF)
         if half == 1:
             saves[2].start()
             saves[3].start()
@@ -1219,7 +1268,7 @@
             shape((ff, width), BF),
             shape((local, ff), BF),
             shape((local, ff), BF),
-            shape((local, width), BF),
+            shape((width, local), BF),
             shape((local, width), F32),
             shape((local, 128), F32),
             shape((local, width), BF),
@@ -1237,6 +1286,7 @@
             pltpu.VMEM((local, ff), BF),
             pltpu.VMEM((local, width), F32),
             pltpu.VMEM((local, width), BF),
+            pltpu.VMEM((width, local), BF),
             pltpu.VMEM((local, width), F32),
             pltpu.VMEM((local, width), F32),
             pltpu.VMEM((local, width), BF),
@@ -1288,7 +1338,7 @@
         last_key = key_ends[local + rows - 1 : 2 * local : rows]
         return jnp.stack([first_key // BK, (last_key + BK - 1) // BK], axis=1)
 
-    bounds = jnp.concatenate([live_blocks(FWD_ROWS), live_blocks(BACK_ROWS)])
+    bounds = live_blocks(FWD_ROWS)
     query_end = seg_ends[NQ - 1]
     info = jnp.stack([base // CB, (query_end + CB - 1) // CB, query_end // CB])
     seg_col = jnp.broadcast_to(seg_ids[:, None], (SEQ, 128))
@@ -1316,15 +1366,15 @@
     gains = norm_gains.astype(F32)
     shifts = norm_shifts.astype(F32)
     bias = jnp.concatenate([qkv_bias.reshape(6, 128), ffn_in_bias.reshape(8, 128), jnp.zeros((2, 128), BF)])
-    qkv_all, attn_all, in_all, window, bias_all, queries, keys, keys_t, values, values_t = first(
+    qkv_all, attn_all, in_all, window_t, bias_all, queries, keys, values, values_t = first(
         jnp.transpose(qkv_weight, (1, 0, 2)), attn_weight, ffn_in_weight, tokens, bias, cosine, sine
     )
     in_bias_all = bias_all[:, 6:14].reshape(1, 4 * width).astype(F32)
     vectors = jnp.concatenate(
         [attn_bias.astype(F32)[None], ffn_out_bias.astype(F32)[None], gains, shifts, jnp.zeros((2, width), F32)]
     )
-    mixed, lse = attend(bounds[: local // FWD_ROWS], queries, keys, values_t, seg_q, seg_k)
-    out_all, hidden, slope, normed_low, unit_one, scale_one, output_low, unit_two, scale_two, embedded_all = second(
+    mixed, lse = attend(bounds, queries, keys, values_t, seg_q, seg_k)
+    out_all, hidden, slope, normed_t, unit_one, scale_one, output_low, unit_two, scale_two, embedded_all = second(
         ffn_out_weight, mixed, tokens, attn_all, in_all, in_bias_all, vectors, proj_weight
     )
     embedded_all = embedded_all.reshape(-1, EMB)
@@ -1344,18 +1394,12 @@
     attn_grad = resid_one_grad.astype(BF)
     attn_bias_grad = jnp.sum(attn_grad.astype(F32), axis=0)
     mixed_grad = dot(attn_grad, attn_all, 1, 1).astype(BF)
-    dq, dk, dv = attend_back(bounds[local // FWD_ROWS :], queries, keys, keys_t, values, mixed, mixed_grad, lse, seg_q, seg_k, cosine, sine)
-    window_grad = dot(dk, qkv_all[1], 1, 1) + dot(dv, qkv_all[2], 1, 1)
-    window_low = window_grad.astype(BF)
-    own_grad = window_grad[local : 2 * local] + dot(dq, qkv_all[0], 1, 1) + resid_one_grad
-    qkv_bias_grad = jnp.concatenate([jnp.sum(part.astype(F32), axis=0) for part in (dq, dk, dv)])
-
     share = 1.0 / tensor_count
     proj_red = lax.psum(proj_grad, ("dp", "tensor"))
     small = jnp.concatenate(
         [
             attn_bias_grad, out_bias_grad, gain_one_grad, gain_two_grad, shift_one_grad, shift_two_grad,
-            qkv_bias_grad, in_bias_grad, row_loss[0, :1] * share, row_temp[0, :1] * share,
+            jnp.zeros((3 * width,), F32), in_bias_grad, row_loss[0, :1] * share, row_temp[0, :1] * share,
             jnp.zeros((SMALL_ROWS * 128 - 13 * width - 2,), F32),
         ]
     ).reshape(SMALL_ROWS, 128)
@@ -1363,25 +1407,20 @@
     def arrange(array):
         if groups == 1:
             return array
-        rows = array.shape[0]
-        return array.reshape(rows, groups, 8, -1).transpose(0, 2, 1, 3).reshape(rows, width)
-
-    qkv_red, attn_red, in_red, out_red, small, from_left, from_right = scatter(
-        arrange(window), arrange(attn_grad), arrange(normed_low), arrange(ffn_grad),
-        dq, dk, dv, mixed, pre_grad, hidden, window_low, small,
+        columns = array.shape[1]
+        return array.reshape(groups, 8, -1, columns).transpose(1, 0, 2, 3).reshape(width, columns)
+
+    qkv_red, attn_red, in_red, out_red, small, tokens_grad = last(
+        arrange(window_t), arrange(attn_grad.T), arrange(normed_t), arrange(ffn_grad.T), hidden, pre_grad,
+        queries, keys, values, mixed, mixed_grad, qkv_all, resid_one_grad, lse, seg_q, seg_k, cosine, sine, small,
     )
     if groups > 1:
         ranks = [[high * 8 + low for high in range(groups)] for low in range(8)]
         qkv_red, attn_red, in_red, out_red = (
-            lax.psum_scatter(part, "dp", scatter_dimension=0, axis_index_groups=ranks, tiled=True)
-            for part in (qkv_red, attn_red, in_red, out_red)
+            lax.psum_scatter(part, "dp", scatter_dimension=dim, axis_index_groups=ranks, tiled=True)
+            for part, dim in ((qkv_red, 0), (attn_red, 1), (in_red, 0), (out_red, 1))
         )
         small = lax.psum(small, "dp", axis_index_groups=ranks)
-    tokens_grad = (
-        own_grad
-        + jnp.where(z > 0, from_left.astype(F32), 0.0)
-        + jnp.where(z < tensor_count - 1, from_right.astype(F32), 0.0)
-    )
     flat = small.reshape(-1)
 
     def cut(start, length):
@@ -1395,11 +1434,11 @@
         tokens_grad,
         qkv_red.reshape(-1, 3, 256),
         qkv_bias_red,
-        attn_red.T,
+        attn_red,
         cut(0, 1),
         in_red,
         in_bias_red,
-        out_red.T,
+        out_red,
         cut(1, 1),
         cut(2, 2).reshape(2, width),
         cut(4, 2).reshape(2, width),

time: 484 us -> 476 us (0.983); the launches traced: 478 us -> 476 us
  matrix products: 44.2 us -> 25.4 us
  Pallas kernels: 367 us -> 385 us
  other arithmetic: 16.5 us -> 10.6 us
    dot_general x8 -> x5, matrix products: 44.2 us -> 25.4 us  [dot(): lax.dot_general(left, right, (((left_dim,), (right_dim,)), ((), ())), pre...]
    pallas_call x1, Pallas kernels: 91.3 us -> 103 us  [first(): pl.pallas_call(first_kernel, in_specs=hbm_specs(4) + vmem_specs(3), out_s...]
    pallas_call x2 -> x1, Pallas kernels: 186 us -> 190 us  [last(): pl.pallas_call(last_kernel, in_specs=hbm_specs(13) + vmem_specs(6), out_s...]
    unnamed x86 -> x61, local copies, waits for them, and re-layouts: 14.9 us -> 17.6 us
  transfers between devices with their start and end apart: 1 -> 1, of which waited for: 0 -> 0; matrix products, arithmetic and copies ran while one was open for 14% -> 9% of each run, Pallas kernels for 39% -> 40%
where the time goes in v3:
time: 476 us
  Pallas kernels  385 us (81%)
  local copies, waits for them, and re-layouts  34.5 us (7%)
  matrix products  25.4 us (5%)
  between operations  20 us (4%)
  other arithmetic  10.6 us (2%)
    pallas_call x1, Pallas kernels, last(): pl.pallas_call(last_kernel, in_specs=hbm_specs(13) + vmem_specs(6), out_s...  190 us
    pallas_call x1, Pallas kernels, first(): pl.pallas_call(first_kernel, in_specs=hbm_specs(4) + vmem_specs(3), out_s...  103 us
    pallas_call x1, Pallas kernels, second(): pl.pallas_call(second_kernel, in_specs=hbm_specs(5) + vmem_specs(3), out_...  56.9 us
    dot_general x5, matrix products, dot(): lax.dot_general(left, right, (((left_dim,), (right_dim,)), ((), ())), pre...  25.4 us
    pallas_call x1, Pallas kernels, contrast(): pl.pallas_call(contrast_kernel, in_specs=[pl.BlockSpec(memory_space=pltpu...  23.6 us
    unnamed x61, local copies, waits for them, and re-layouts  17.6 us
    pallas_call x1, Pallas kernels, attend(): pl.pallas_call(attend_kernel, grid_spec=pltpu.PrefetchScalarGridSpec(num_...  12.5 us
  transfers between devices with their start and end apart: 1, of which 0 were waited for; matrix products, arithmetic and copies ran while one was open for 9% of the time, Pallas kernels for 40%

profile of v3, /device:TPU:24, one launch (start us, length us, event | category | flops | bytes accessed | tf_op | source)
XLA Modules:
  0.0 475.6 jit_solution(14661485269289560496)
XLA Ops:
  7.3 0.8 select_reduce_fusion.2
  8.0 0.7 bitcast_convert_fusion
  8.7 0.6 slice.75
  12.6 0.7 reshape.143
  14.1 2.8 fusion
  16.9 0.7 maximum_maximum_fusion.bias
  17.6 2.4 pad_maximum_fusion
  20.0 102.5 %shard_map.262 = (bf16[3,1024,1024]{2,1,0:T(8,128)(2,1)}, bf16[1024,1024]{1,0:T(8,128)(2,1)}, bf16[1024,4096]{1,0:T(8,128)(2,1)}, bf16[1024,1536]{1,0:T(8,128)(2...) custom-call(bf16[3,1024,256]{2,1,0:T(8,128)(2,1)} %bitcast.52, ...), custom_call_target="tpu_custom_call" | custom-call | tf_op jit(solution)/shard_map/pallas_call | solution.py:1096
  122.5 1.3 slice_convert_fusion
  124.8 0.7 concatenate.21.vectors
  125.8 1.9 copy-done
  127.7 1.2 copy-done.2
  128.9 1.9 copy-done.4
  130.8 12.5 %shard_map.263 = (bf16[512,1024]{1,0:T(8,128)(2,1)S(1)}, f32[16,512]{1,0:T(8,128)S(1)}) custom-call(s32[4,2]{1,0:T(4,128)S(1)} %pad_add_fusion.bounds_ref, bf16[512,1024]{1,0:T(8,128)(2,1)S(1)} %copy-done.2, bf16[1536,1024]{1,0:T(8,128)(2,1)S(1)} %copy-done, bf16[1024,1536]{1,0:T(8,128)(2,1)S(1)} %copy-done.4, s32[8,512]{1,0:T(8,128)S(1)} %broadcast_in_dim.119.segq_ref, ...), custom_call_target="tpu_custom_call" | custom-call | flops 2147483648 | bytes 8388608 | tf_op jit(solution)/shard_map/pallas_call | solution.py:112
  143.3 1.0 copy-done.3
  144.3 0.6 copy-done.6
  144.9 56.9 %shard_map.264 = (bf16[4096,1024]{1,0:T(8,128)(2,1)}, bf16[512,4096]{1,0:T(8,128)(2,1)}, bf16[512,4096]{1,0:T(8,128)(2,1)}, bf16[1024,512]{1,0:T(8,128)(2,1)}, f...) custom-call(bf16[1024,1024]{1,0:T(8,128)(2,1)} %out_src.1, ...), custom_call_target="tpu_custom_call" | custom-call | tf_op jit(solution)/shard_map/pallas_call | solution.py:1263
  202.2 1.0 copy-done.7
  203.3 23.6 %shard_map.265 = (bf16[512,128]{1,0:T(8,128)(2,1)S(1)}, f32[8,128]{1,0:T(8,128)S(1)}, f32[8,128]{1,0:T(8,128)S(1)}) custom-call(s32[3]{0:T(128)S(1)} %pad_add_fusion.1.info_ref, bf16[2048,128]{1,0:T(8,128)(2,1)S(1)} %bitcast.50, s32[2048,128]{1,0:T(8,128)S(1)} %broadcast_in_dim.126.segc_ref, s32[8,2048]{1,0:T(8,128)S(1)} %broadcast_in_dim.127.segr_ref, ...), custom_call_target="tpu_custom_call" | custom-call | flops 1073741824 | bytes 4194304 | tf_op jit(solution)/shard_map/pallas_call | solution.py:261
  226.9 1.3 fusion.14
  228.7 1.8 multiply_reduce_fusion
  230.7 0.5 convert_reduce_fusion.1
  231.4 9.1 %convert_reduce_fusion = (f32[4096]{0:T(1024)S(1)}, bf16[512,4096]{1,0:T(8,128)(2,1)S(1)}) fusion(bf16[512,4096]{1,0:T(8,128)(2,1)} %get-tuple-element.59, bf16[4096,1024]{1,0:T(8,128)(2,1)} %get-tuple-element.58, f32[512,1024]{1,0:T(8,128)S(1)} %get-tuple-element.146), kind=kOutput, calls=%fused_computation | convolution fusion | flops 4305973248 | bytes 18890752 | tf_op jit(solution)/shard_map/dot_general | solution.py:26
  240.6 10.8 %multiply_reduce_fusion.1 = (f32[1024]{0:T(1024)S(1)}, f32[512]{0:T(512)S(1)}, f32[512]{0:T(512)S(1)}, f32[1024]{0:T(1024)S(1)}, f32[512,1024]{1,0:T(8,128)S(1)}) fusion(f32[512,1024]{1,0:T(8,128)} %get-tuple-element.60, f32[1024]{0:T(1024)S(1)} %bitcast.58, f32[512,1024]{1,0:T(8,128)S(1)} %get-tuple-element.146, ...), kind=kOutput, calls=%fused_computation.3 | convolution fusion | flops 4299158528 | bytes 18890752 | tf_op jit(solution)/shard_map/dot_general | solution.py:26
  252.3 1.1 copy-done.8
  253.4 1.0 copy-done.14
  254.5 2.3 convolution_convert_fusion.mixed_grad
  256.8 1.3 copy.50.attn_grad
  258.1 1.3 copy.51.ffn_grad
  261.8 0.7 concatenate.23
  262.5 189.6 %shard_map.266 = (f32[128,768]{1,0:T(8,128)}, f32[256,128]{1,0:T(8,128)}, f32[128,1024]{1,0:T(8,128)}, f32[1024,128]{1,0:T(8,128)}, f32[112,128]{1,0:T(8,128)}, /*index=5*/f32[512,1024]{1,0:T(8,128)}) custom-call(bf16[1024,1536]{1,0:T(8,128)(2,1)} %get-tuple-element.45.window, bf16[1024,512]{1,0:T(8,128)(2,1)} %copy.50.attn_grad, ...), custom_call_target="tpu_custom_call" | custom-call | tf_op jit(solution)/shard_map/pallas_call | solution.py:776
  452.1 0.9 slice.81
  452.9 0.7 slice_bitcast_fusion
  453.6 0.7 fusion.12
  454.4 1.3 fusion.11
  455.7 0.6 constant_dynamic-slice_fusion
  456.3 1.9 copy.52
  458.2 1.9 copy.53
  460.1 0.6 reshape.151
  460.7 0.6 reshape.152
  461.3 0.6 dynamic_slice.7
  461.9 1.3 slice_bitcast_fusion.1
  463.2 1.0 copy.61
  464.2 1.3 copy.62
  465.5 0.7 copy.63
  466.2 0.8 copy.64
  467.0 0.8 copy.65
  467.8 0.8 copy.66
  (93 shorter events, 4.5 us)
Async XLA Ops:
  7.2 9.7 %copy-start.23 = (bf16[1024]{0:T(1024)(128)(2,1)S(1)}, bf16[1024]{0:T(1024)(128)(2,1)}, u32[]{:S(2)}) copy-start(bf16[1024]{0:T(1024)(128)(2,1)} %param.23) | copy-start | bytes 6148
  7.2 456.0 %all-reduce.3.cloned.1.call-start = ((), (), s32[]{:S(2)}) async-start(), calls=%async_computation | async-start | bytes 1048576 | tf_op jit(solution)/shard_map/psum | solution.py:1398
  20.0 103.9 %copy-start.24 = (bf16[1024]{0:T(1024)(128)(2,1)S(1)}, bf16[1024]{0:T(1024)(128)(2,1)}, u32[]{:S(2)}) copy-start(bf16[1024]{0:T(1024)(128)(2,1)} %param.21) | copy-start | bytes 6148
  20.0 103.9 %copy-start.25 = (bf16[1024]{0:T(1024)(128)(2,1)S(1)}, bf16[1024]{0:T(1024)(128)(2,1)}, u32[]{:S(2)}) copy-start(bf16[1024]{0:T(1024)(128)(2,1)} %param.25) | copy-start | bytes 6148
  20.0 103.9 %copy-start.26 = (s32[1,8]{1,0:T(1,128)S(1)}, s32[1,8]{1,0:T(1,128)}, u32[]{:S(2)}) copy-start(s32[1,8]{1,0:T(1,128)} %param.17) | copy-start | bytes 100
  20.0 104.8 %copy-start.21 = (bf16[2,1024]{1,0:T(2,128)(2,1)S(1)}, bf16[2,1024]{1,0:T(2,128)(2,1)}, u32[]{:S(2)}) copy-start(bf16[2,1024]{1,0:T(2,128)(2,1)} %param.26) | copy-start | bytes 12292
  20.0 104.8 %copy-start.22 = (bf16[2,1024]{1,0:T(2,128)(2,1)S(1)}, bf16[2,1024]{1,0:T(2,128)(2,1)}, u32[]{:S(2)}) copy-start(bf16[2,1024]{1,0:T(2,128)(2,1)} %param.27) | copy-start | bytes 12292
  125.5 17.8 %copy-start.5 = (s32[8,512]{1,0:T(8,128)}, s32[8,512]{1,0:T(8,128)S(1)}, u32[]{:S(2)}) copy-start(s32[8,512]{1,0:T(8,128)S(1)} %broadcast_in_dim.119.segq_ref) | copy-start | bytes 49156
  125.8 1.9 copy-start
  127.7 1.2 copy-start.2
  128.9 1.9 copy-start.4
  130.8 12.5 %copy-start.1 = (s32[1536,128]{1,0:T(8,128)}, s32[1536,128]{1,0:T(8,128)S(1)}, u32[]{:S(2)}) copy-start(s32[1536,128]{1,0:T(8,128)S(1)} %broadcast_in_dim.120.segk_ref) | copy-start | bytes 2359300
  143.3 1.0 copy-start.3
  144.3 0.6 copy-start.6
  202.2 1.0 copy-start.7
  203.3 23.6 %copy-start.10 = (bf16[512,1024]{1,0:T(8,128)(2,1)S(1)}, bf16[512,1024]{1,0:T(8,128)(2,1)}, u32[]{:S(2)}) copy-start(bf16[512,1024]{1,0:T(8,128)(2,1)} %get-tuple-element.188) | copy-start | bytes 3145732
  226.9 1.8 copy-start.9
  228.7 1.9 copy-start.19
  240.5 10.9 %copy-start.11 = (bf16[512,4096]{1,0:T(8,128)(2,1)}, bf16[512,4096]{1,0:T(8,128)(2,1)S(1)}, u32[]{:S(2)}) copy-start(bf16[512,4096]{1,0:T(8,128)(2,1)S(1)} %get-tuple-element.169.pre_grad) | copy-start | bytes 12582916
  240.6 10.9 %copy-start.18 = (f32[512,128]{1,0:T(8,128)S(1)}, f32[512,128]{1,0:T(8,128)}, u32[]{:S(2)}) copy-start(f32[512,128]{1,0:T(8,128)} %get-tuple-element.53) | copy-start | bytes 786436
  240.6 11.0 %copy-start.12 = (f32[512,1024]{1,0:T(8,128)S(1)}, f32[512,1024]{1,0:T(8,128)}, u32[]{:S(2)}) copy-start(f32[512,1024]{1,0:T(8,128)} %get-tuple-element.60) | copy-start | bytes 6291460
  252.1 1.3 copy-start.8
  252.1 2.4 copy-start.14
  452.0 12.1 %copy-start.13 = (f32[512,1024]{1,0:T(8,128)S(1)}, f32[512,1024]{1,0:T(8,128)}, u32[]{:S(2)}) copy-start(f32[512,1024]{1,0:T(8,128)} %get-tuple-element.189) | copy-start | bytes 6291460
  464.2 1.3 copy-start.20
  464.2 2.0 copy-start.17
  464.2 2.8 copy-start.16
  465.5 2.3 copy-start.15
Sparse Core Ops, SparseCore 0:
  228.3 127.6 all-reduce.2

commit v4 on v3

--- a/solution.py
+++ b/solution.py
@@ -65,7 +65,7 @@
 
 
 def turn(values):
-    return values.astype(F32).T.astype(BF)
+    return values.T
 
 
 def attend_kernel(bounds_ref, query_ref, key_ref, turned_ref, segq_ref, segk_ref, mixed_ref, lse_ref):
@@ -523,7 +523,7 @@
 def last_kernel(
     window, attn_grad, normed, ffn_grad, hidden, pre_grad, query, key, value, mixed, mixed_grad, qkv_all, resid_grad,
     lse_ref, segq_ref, segk_ref, cos_ref, sin_ref, small_ref,
-    out_qkv, out_attn, out_in, out_out, small_out, token_grad,
+    out_qkv, out_attn, out_in, out_out, head_sums, qkv_sums, in_sums, last_row, token_grad,
     xw, xa, xn, xf, gs, q_v, g_v, m_v, k_v, v_v, weight, dk_acc, dv_acc, dq_b, dk_b, dv_b, send_l, send_r, from_l, from_r,
     sums, sacc, srec, zsm, x_sem, g_sem, h_sem, w_sem, sm_sem, smz_sem, e_sem, *refs,
 ):
@@ -629,7 +629,13 @@
                 for step in range(1, nz):
                     made = jnp.where(lax.rem(z - step + nz, nz) == owner, zsm[step - 1], made)
                 total = made if total is None else total + made
-            small_out[...] = total
+            zsm[0] = total
+            head_sums[...] = total[:QKV_ROW]
+            for kind in range(3):
+                at = QKV_ROW + 8 * kind
+                qkv_sums[2 * kind : 2 * kind + 2, :] = zsm[0, pl.ds(at + 2 * z, 2), :]
+            in_sums[...] = zsm[0, pl.ds(pl.multiple_of(QKV_ROW + 24 + 8 * z, 8), 8), :]
+            last_row[...] = total[QKV_ROW + 56 : QKV_ROW + 64]
 
     head_row = lax.broadcasted_iota(jnp.int32, (8, 128), 0)
     head_lane = lax.broadcasted_iota(jnp.int32, (8, 128), 1) // 64
@@ -776,13 +782,16 @@
     return pl.pallas_call(
         last_kernel,
         in_specs=hbm_specs(13) + vmem_specs(6),
-        out_specs=vmem_specs(6),
+        out_specs=vmem_specs(9),
         out_shape=[
             shape((128, 768), F32),
             shape((256, 128), F32),
             shape((128, 1024), F32),
             shape((1024, 128), F32),
-            shape(small.shape, F32),
+            shape((QKV_ROW, 128), F32),
+            shape((6, 128), F32),
+            shape((8, 128), F32),
+            shape((8, 128), F32),
             shape((local, width), F32),
         ],
         scratch_shapes=[
@@ -1323,10 +1332,9 @@
     offsets = jnp.where(near_ids >= 0, near - near_starts, 0)
     half_dim = HDIM // 2
     inv_freq = jnp.exp(jnp.arange(half_dim, dtype=F32) * (-2.0 * math.log(10000.0) / HDIM))
-    angles = offsets.astype(F32)[:, None] * inv_freq[None, :]
-    cosine, sine = jnp.cos(angles), jnp.sin(angles)
-    cosine = jnp.concatenate([cosine] * 4, axis=1)
-    sine = jnp.concatenate([-sine, sine] * 2, axis=1)
+    angles = offsets.astype(F32)[:, None] * jnp.tile(inv_freq, 4)[None, :]
+    side = jnp.where(jnp.arange(128) % HDIM < half_dim, -1.0, 1.0).astype(F32)
+    cosine, sine = jnp.cos(angles), jnp.sin(angles) * side[None, :]
     seg_q = jnp.broadcast_to(lax.slice_in_dim(near_ids, local, 2 * local)[None, :], (8, local))
     seg_k = jnp.broadcast_to(near_ids[:, None], (3 * local, 128))
     key_starts = jnp.where(near_ids >= 0, near_starts - base + local, 0)
@@ -1410,7 +1418,7 @@
         columns = array.shape[1]
         return array.reshape(groups, 8, -1, columns).transpose(1, 0, 2, 3).reshape(width, columns)
 
-    qkv_red, attn_red, in_red, out_red, small, tokens_grad = last(
+    qkv_red, attn_red, in_red, out_red, *sums, tokens_grad = last(
         arrange(window_t), arrange(attn_grad.T), arrange(normed_t), arrange(ffn_grad.T), hidden, pre_grad,
         queries, keys, values, mixed, mixed_grad, qkv_all, resid_one_grad, lse, seg_q, seg_k, cosine, sine, small,
     )
@@ -1420,30 +1428,24 @@
             lax.psum_scatter(part, "dp", scatter_dimension=dim, axis_index_groups=ranks, tiled=True)
             for part, dim in ((qkv_red, 0), (attn_red, 1), (in_red, 0), (out_red, 1))
         )
-        small = lax.psum(small, "dp", axis_index_groups=ranks)
-    flat = small.reshape(-1)
-
-    def cut(start, length):
-        return lax.slice_in_dim(flat, start * width, (start + length) * width)
-
-    qkv_bias_red = lax.dynamic_slice_in_dim(cut(6, 3).reshape(3, width), z * 256, 256, 1)
-    in_bias_red = lax.dynamic_slice_in_dim(cut(9, 4), z * width, width, 0)
+        sums = lax.psum(sums, "dp", axis_index_groups=ranks)
+    head_sums, qkv_bias_red, in_bias_red, last_row = sums
     return (
-        flat[13 * width : 13 * width + 1],
+        last_row[0, :1],
         output_low,
         tokens_grad,
         qkv_red.reshape(-1, 3, 256),
-        qkv_bias_red,
+        qkv_bias_red.reshape(3, -1),
         attn_red,
-        cut(0, 1),
+        head_sums[0:8].reshape(-1),
         in_red,
-        in_bias_red,
+        in_bias_red.reshape(-1),
         out_red,
-        cut(1, 1),
-        cut(2, 2).reshape(2, width),
-        cut(4, 2).reshape(2, width),
+        head_sums[8:16].reshape(-1),
+        head_sums[16:32].reshape(2, width),
+        head_sums[32:48].reshape(2, width),
         proj_red,
-        flat[13 * width + 1 : 13 * width + 2],
+        last_row[0, 1:2],
     )
 
 

time: 476 us -> 468 us (0.983)
  Pallas kernels: 385 us -> 374 us
    pallas_call x1, Pallas kernels: 103 us -> 91.1 us  [first(): pl.pallas_call(first_kernel, in_specs=hbm_specs(4) + vmem_specs(3), out_s...]
    unnamed x61 -> x62, local copies, waits for them, and re-layouts: 17.6 us -> 18.2 us
  transfers between devices with their start and end apart: 1 -> 1, of which waited for: 0 -> 0; matrix products, arithmetic and copies ran while one was open for 9% -> 9% of each run, Pallas kernels for 40% -> 41%
where the time goes in v4:
time: 468 us; the launch traced here: 464 us
  Pallas kernels  374 us (80%)
  local copies, waits for them, and re-layouts  33.8 us (7%)
  matrix products  25.4 us (5%)
  between operations  20.2 us (4%)
  other arithmetic  10.4 us (2%)
    pallas_call x1, Pallas kernels, last(): pl.pallas_call(last_kernel, in_specs=hbm_specs(13) + vmem_specs(6), out_s...  189 us
    pallas_call x1, Pallas kernels, first(): pl.pallas_call(first_kernel, in_specs=hbm_specs(4) + vmem_specs(3), out_s...  91.1 us
    pallas_call x1, Pallas kernels, second(): pl.pallas_call(second_kernel, in_specs=hbm_specs(5) + vmem_specs(3), out_...  60.1 us
    dot_general x5, matrix products, dot(): lax.dot_general(left, right, (((left_dim,), (right_dim,)), ((), ())), pre...  25.4 us
    pallas_call x1, Pallas kernels, contrast(): pl.pallas_call(contrast_kernel, in_specs=[pl.BlockSpec(memory_space=pltpu...  23.8 us
    unnamed x62, local copies, waits for them, and re-layouts  18.2 us
    pallas_call x1, Pallas kernels, attend(): pl.pallas_call(attend_kernel, grid_spec=pltpu.PrefetchScalarGridSpec(num_...  10.4 us
  transfers between devices with their start and end apart: 1, of which 0 were waited for; matrix products, arithmetic and copies ran while one was open for 9% of the time, Pallas kernels for 41%

profile of v4, /device:TPU:24, one launch (start us, length us, event | category | flops | bytes accessed | tf_op | source)
XLA Modules:
  0.0 463.9 jit_solution(3351764897846533721)
XLA Ops:
  7.3 0.8 select_reduce_fusion.2
  8.0 0.7 bitcast_convert_fusion
  8.7 0.6 slice.57
  12.6 0.7 reshape.152
  14.2 1.4 maximum_maximum_fusion.bias
  15.5 4.3 fusion
  19.9 91.1 %shard_map.262 = (bf16[3,1024,1024]{2,1,0:T(8,128)(2,1)}, bf16[1024,1024]{1,0:T(8,128)(2,1)}, bf16[1024,4096]{1,0:T(8,128)(2,1)}, bf16[1024,1536]{1,0:T(8,128)(2...) custom-call(bf16[3,1024,256]{2,1,0:T(8,128)(2,1)} %bitcast.52, ...), custom_call_target="tpu_custom_call" | custom-call | tf_op jit(solution)/shard_map/pallas_call | solution.py:1105
  110.9 1.3 slice_convert_fusion
  113.2 0.7 concatenate.13.vectors
  114.2 1.9 copy-done
  116.1 1.2 copy-done.2
  117.3 1.9 copy-done.4
  119.2 10.4 %shard_map.263 = (bf16[512,1024]{1,0:T(8,128)(2,1)S(1)}, f32[16,512]{1,0:T(8,128)S(1)}) custom-call(s32[4,2]{1,0:T(4,128)S(1)} %pad_add_fusion.bounds_ref, bf16[512,1024]{1,0:T(8,128)(2,1)S(1)} %copy-done.2, bf16[1536,1024]{1,0:T(8,128)(2,1)S(1)} %copy-done, bf16[1024,1536]{1,0:T(8,128)(2,1)S(1)} %copy-done.4, s32[8,512]{1,0:T(8,128)S(1)} %broadcast_in_dim.129.segq_ref, ...), custom_call_target="tpu_custom_call" | custom-call | flops 2147483648 | bytes 8388608 | tf_op jit(solution)/shard_map/pallas_call | solution.py:112
  129.6 1.0 copy-done.3
  130.6 0.6 copy-done.6
  131.2 60.1 %shard_map.264 = (bf16[4096,1024]{1,0:T(8,128)(2,1)}, bf16[512,4096]{1,0:T(8,128)(2,1)}, bf16[512,4096]{1,0:T(8,128)(2,1)}, bf16[1024,512]{1,0:T(8,128)(2,1)}, f...) custom-call(bf16[1024,1024]{1,0:T(8,128)(2,1)} %out_src.1, ...), custom_call_target="tpu_custom_call" | custom-call | tf_op jit(solution)/shard_map/pallas_call | solution.py:1272
  191.7 1.0 copy-done.7
  192.7 23.8 %shard_map.265 = (bf16[512,128]{1,0:T(8,128)(2,1)S(1)}, f32[8,128]{1,0:T(8,128)S(1)}, f32[8,128]{1,0:T(8,128)S(1)}) custom-call(s32[3]{0:T(128)S(1)} %pad_add_fusion.1.info_ref, bf16[2048,128]{1,0:T(8,128)(2,1)S(1)} %bitcast.50, s32[2048,128]{1,0:T(8,128)S(1)} %broadcast_in_dim.136.segc_ref, s32[8,2048]{1,0:T(8,128)S(1)} %broadcast_in_dim.137.segr_ref, ...), custom_call_target="tpu_custom_call" | custom-call | flops 1073741824 | bytes 4194304 | tf_op jit(solution)/shard_map/pallas_call | solution.py:261
  216.5 1.3 fusion.14
  218.3 1.9 multiply_reduce_fusion
  220.4 0.5 convert_reduce_fusion.1
  221.1 9.2 %convert_reduce_fusion = (f32[4096]{0:T(1024)S(1)}, bf16[512,4096]{1,0:T(8,128)(2,1)S(1)}) fusion(bf16[512,4096]{1,0:T(8,128)(2,1)} %get-tuple-element.62, bf16[4096,1024]{1,0:T(8,128)(2,1)} %get-tuple-element.61, f32[512,1024]{1,0:T(8,128)S(1)} %get-tuple-element.137), kind=kOutput, calls=%fused_computation | convolution fusion | flops 4305973248 | bytes 18890752 | tf_op jit(solution)/shard_map/dot_general | solution.py:26
  230.3 10.8 %multiply_reduce_fusion.1 = (f32[1024]{0:T(1024)S(1)}, f32[512]{0:T(512)S(1)}, f32[512]{0:T(512)S(1)}, f32[1024]{0:T(1024)S(1)}, f32[512,1024]{1,0:T(8,128)S(1)}) fusion(f32[512,1024]{1,0:T(8,128)} %get-tuple-element.63, f32[1024]{0:T(1024)S(1)} %bitcast.57, f32[512,1024]{1,0:T(8,128)S(1)} %get-tuple-element.137, ...), kind=kOutput, calls=%fused_computation.3 | convolution fusion | flops 4299158528 | bytes 18890752 | tf_op jit(solution)/shard_map/dot_general | solution.py:26
  241.2 0.5 convert_reduce_fusion.2
  241.9 1.1 copy-done.8
  243.0 1.0 copy-done.14
  244.1 2.3 convolution_convert_fusion.mixed_grad
  246.3 1.3 copy.43.attn_grad
  247.7 1.3 copy.44.ffn_grad
  249.0 0.5 slice.60
  249.5 0.5 slice.61
  251.3 0.7 concatenate.15
  252.0 188.8 %shard_map.266 = (f32[128,768]{1,0:T(8,128)}, f32[256,128]{1,0:T(8,128)}, f32[128,1024]{1,0:T(8,128)}, f32[1024,128]{1,0:T(8,128)}, f32[48,128]{1,0:T(8,128)}, /...) custom-call(bf16[1024,1536]{1,0:T(8,128)(2,1)} %get-tuple-element.48.window, ...), custom_call_target="tpu_custom_call" | custom-call | tf_op jit(solution)/shard_map/pallas_call | solution.py:782
  440.8 0.9 fusion.11
  441.7 1.3 fusion.12
  443.0 1.9 copy.45
  444.9 1.9 copy.46
  446.8 1.3 reshape.158
  448.1 0.6 reshape.162
  448.7 0.6 reshape.163
  449.3 1.3 slice_bitcast_fusion
  450.6 1.0 copy.55
  451.6 1.3 copy.56
  452.9 0.7 copy.57
  453.6 0.8 copy.58
  454.4 0.6 copy.59
  455.0 0.8 copy.60
  455.8 0.8 copy.61
  (90 shorter events, 3.0 us)
Async XLA Ops:
  7.2 443.4 %all-reduce.3.cloned.1.call-start = ((), (), s32[]{:S(2)}) async-start(), calls=%async_computation | async-start | bytes 1048576 | tf_op jit(solution)/shard_map/psum | solution.py:1406
  19.8 92.4 %copy-start.24 = (bf16[1024]{0:T(1024)(128)(2,1)S(1)}, bf16[1024]{0:T(1024)(128)(2,1)}, u32[]{:S(2)}) copy-start(bf16[1024]{0:T(1024)(128)(2,1)} %param.21) | copy-start | bytes 6148
  19.8 92.4 %copy-start.25 = (bf16[1024]{0:T(1024)(128)(2,1)S(1)}, bf16[1024]{0:T(1024)(128)(2,1)}, u32[]{:S(2)}) copy-start(bf16[1024]{0:T(1024)(128)(2,1)} %param.25) | copy-start | bytes 6148
  19.8 92.5 %copy-start.26 = (s32[1,8]{1,0:T(1,128)S(1)}, s32[1,8]{1,0:T(1,128)}, u32[]{:S(2)}) copy-start(s32[1,8]{1,0:T(1,128)} %param.17) | copy-start | bytes 100
  19.8 93.4 %copy-start.21 = (bf16[2,1024]{1,0:T(2,128)(2,1)S(1)}, bf16[2,1024]{1,0:T(2,128)(2,1)}, u32[]{:S(2)}) copy-start(bf16[2,1024]{1,0:T(2,128)(2,1)} %param.26) | copy-start | bytes 12292
  19.9 93.4 %copy-start.22 = (bf16[2,1024]{1,0:T(2,128)(2,1)S(1)}, bf16[2,1024]{1,0:T(2,128)(2,1)}, u32[]{:S(2)}) copy-start(bf16[2,1024]{1,0:T(2,128)(2,1)} %param.27) | copy-start | bytes 12292
  113.9 15.7 %copy-start.5 = (s32[8,512]{1,0:T(8,128)}, s32[8,512]{1,0:T(8,128)S(1)}, u32[]{:S(2)}) copy-start(s32[8,512]{1,0:T(8,128)S(1)} %broadcast_in_dim.129.segq_ref) | copy-start | bytes 49156
  114.2 1.9 copy-start
  116.1 1.2 copy-start.2
  117.3 1.9 copy-start.4
  119.2 10.4 %copy-start.1 = (s32[1536,128]{1,0:T(8,128)}, s32[1536,128]{1,0:T(8,128)S(1)}, u32[]{:S(2)}) copy-start(s32[1536,128]{1,0:T(8,128)S(1)} %broadcast_in_dim.130.segk_ref) | copy-start | bytes 2359300
  129.6 1.0 copy-start.3
  130.6 0.6 copy-start.6
  191.7 1.0 copy-start.7
  192.7 23.8 %copy-start.10 = (bf16[512,1024]{1,0:T(8,128)(2,1)S(1)}, bf16[512,1024]{1,0:T(8,128)(2,1)}, u32[]{:S(2)}) copy-start(bf16[512,1024]{1,0:T(8,128)(2,1)} %get-tuple-element.180) | copy-start | bytes 3145732
  216.5 1.8 copy-start.9
  218.3 1.9 copy-start.18
  218.3 1.9 copy-start.19
  230.3 10.9 %copy-start.11 = (bf16[512,4096]{1,0:T(8,128)(2,1)}, bf16[512,4096]{1,0:T(8,128)(2,1)S(1)}, u32[]{:S(2)}) copy-start(bf16[512,4096]{1,0:T(8,128)(2,1)S(1)} %get-tuple-element.159.pre_grad) | copy-start | bytes 12582916
  230.3 10.9 %copy-start.12 = (f32[512,1024]{1,0:T(8,128)S(1)}, f32[512,1024]{1,0:T(8,128)}, u32[]{:S(2)}) copy-start(f32[512,1024]{1,0:T(8,128)} %get-tuple-element.63) | copy-start | bytes 6291460
  241.7 1.3 copy-start.8
  241.7 2.4 copy-start.14
  440.8 10.8 %copy-start.13 = (f32[512,1024]{1,0:T(8,128)S(1)}, f32[512,1024]{1,0:T(8,128)}, u32[]{:S(2)}) copy-start(f32[512,1024]{1,0:T(8,128)} %get-tuple-element.181) | copy-start | bytes 6291460
  451.6 1.3 copy-start.20
  451.6 2.0 copy-start.17
  451.6 2.8 copy-start.23
  451.6 3.4 copy-start.16
  452.9 2.8 copy-start.15
Sparse Core Ops, SparseCore 0:
  217.9 127.1 all-reduce.2
